TPU v7x, 32 devices: a whole 2x2x4 slice. The times are simulated.
32 devices in a mesh: dp: 8 (over z, y), mp: 4 (over x, core).
Axes of the slice: x: 2, y: 2, z: 4, core: 2. Of those that a mesh axis runs over, the one named last changes fastest.
Arguments:
- mel: bfloat16 [8, 4096, 80], P('dp', 'mp'), may hold values from -6 to 6
- lengths: int32 [8], P('dp'), may hold values from 1 to 4096, 24576 in all
- alignment: int32 [8, 512], P('dp', 'mp'), may hold values from 0 to 1024
- loss_mask: int32 [8, 512], P('dp', 'mp'), may hold values 0 or 1
- ff_in: float32 [3, 2, 512, 2048], P(None, None, 'dp', 'mp')
- ff_out: float32 [3, 2, 2048, 512], P(None, None, 'mp', 'dp')
- mix_in: float32 [3, 512, 6, 512], P(None, 'dp', None, 'mp')
- mix_out: float32 [3, 2, 512, 512], P(None, None, 'mp', 'dp')
- small: float32 [3, 1985280], P(None, ('dp', 'mp'))
Outputs:
- ff_in_new: float32 [2, 512, 2048], P(None, 'dp', 'mp')
- ff_in_first: float32 [2, 512, 2048], P(None, 'dp', 'mp')
- ff_in_second: float32 [2, 512, 2048], P(None, 'dp', 'mp')
- ff_out_new: float32 [2, 2048, 512], P(None, 'mp', 'dp')
- ff_out_first: float32 [2, 2048, 512], P(None, 'mp', 'dp')
- ff_out_second: float32 [2, 2048, 512], P(None, 'mp', 'dp')
- mix_in_new: float32 [512, 6, 512], P('dp', None, 'mp')
- mix_in_first: float32 [512, 6, 512], P('dp', None, 'mp')
- mix_in_second: float32 [512, 6, 512], P('dp', None, 'mp')
- mix_out_new: float32 [2, 512, 512], P(None, 'mp', 'dp')
- mix_out_first: float32 [2, 512, 512], P(None, 'mp', 'dp')
- mix_out_second: float32 [2, 512, 512], P(None, 'mp', 'dp')
- small_new: float32 [1985280], P(('dp', 'mp'))
- small_first: float32 [1985280], P(('dp', 'mp'))
- small_second: float32 [1985280], P(('dp', 'mp'))
- vec_grad: float32 [23, 512], replicated
- loss: float32 [], replicated
- grad_norm: float32 [], replicated
Inputs may be any that keep to these rules, and one draw needn't show every extreme that they name: `lengths`: each utterance's mel frame count; the longest has 4096 frames.
All inputs are finite; a program needn't handle non-finite values. No bound on the sum of `lengths` or of `loss_mask` on one device may be relied on, other than what follows from the above.
Results may differ from a plain program's by a relative error of at most 0.014.
The roundings to bfloat16 on the way count: a program that leaves them out, or rounds other values in their place, can miss the bound.
Values may be sent and summed in bfloat16 or wider, within the bound.
No kernel may reach another device: no remote copies, remote signals or barrier semaphores. Data moves between devices by JAX's collectives and lax.ppermute only.
A program may use at most 512 MiB of HBM per device.

v0:
```python
import math

import jax
import jax.numpy as jnp
from jax import lax
from jax.sharding import PartitionSpec as P

D = 512
HEAD_DIM = 64
CHANNELS = 256
MEL = 80
KERNEL = 9
CLASSES = 1025
STEP = 7


norm_eps = 1e-05
clip_norm = 0.005
beta_one = 0.9
beta_two = 0.98
adam_eps = 1e-08
decay_rate = 0.01
small_rates = (0.8, 0.15, 0.05, 0.1, 0.3)
highest = lax.Precision.HIGHEST


def passed_along(x, axis, by):
    peers = lax.axis_size(axis)
    pairs = [(i, i + by) for i in range(peers) if 0 <= i + by < peers]
    return lax.ppermute(x, axis, pairs)


def product(left, right):
    return jnp.dot(left, right, preferred_element_type=jnp.float32)


def layer_norm(values, gain, shift):
    centre = jnp.mean(values, -1, keepdims=True)
    centered = values - centre
    variance = jnp.mean(centered * centered, -1, keepdims=True)
    return centered * lax.rsqrt(variance + norm_eps) * gain + shift


def silu_grad(pre_act):
    sigma = jax.nn.sigmoid(pre_act)
    return sigma * (1.0 + pre_act * (1.0 - sigma))


def strided_taps(field):
    out_count = (field.shape[0] - 1) // 2
    freq_width = field.shape[1]
    padding = [(0, 0), (1, 1)] + [(0, 0)] * (field.ndim - 2)
    padded = jnp.pad(field, padding)
    return [
        padded[row_tap : row_tap + 2 * out_count - 1 : 2, col_tap : col_tap + freq_width - 1 : 2]
        for row_tap in range(3)
        for col_tap in range(3)
    ]


def first_conv(field, weight):
    windows = jnp.stack(strided_taps(field), -1)
    return jnp.einsum(
        "tfk,kc->tfc", windows, weight, precision=highest, preferred_element_type=jnp.float32
    )


def depth_conv(field, weight):
    windows = strided_taps(field)
    return sum((window * weight[tap_index] for tap_index, window in enumerate(windows)))


def stem_front(field, weight_one, weight_two):
    return depth_conv(jax.nn.relu(first_conv(field, weight_one)), weight_two)


def stem_middle(field, weight_three):
    return depth_conv(jax.nn.relu(field), weight_three)


def depth_time(field, kernel):
    half_kernel = KERNEL // 2
    length = field.shape[0]
    padded = jnp.pad(field, ((half_kernel, half_kernel), (0, 0)))
    return sum(
        (padded[tap_index : tap_index + length] * kernel[tap_index] for tap_index in range(KERNEL))
    )


def glu_depth(gates, kernel, valid_full):
    half_width = gates.shape[1] // 2
    gated = gates[:, :half_width] * jax.nn.sigmoid(gates[:, half_width:]) * valid_full[:, None]
    return depth_time(gated, kernel)


def position_table(length):
    distance = (length - 1 - jnp.arange(2 * length - 1)).astype(jnp.float32)[:, None]
    inverse_freq = jnp.exp(jnp.arange(D // 2).astype(jnp.float32) * (-2.0 * math.log(10000.0) / D))
    angles = distance * inverse_freq[None, :]
    return jnp.concatenate([jnp.sin(angles), jnp.cos(angles)], 1)


def skew(field, block_rows, length):
    heads_here = field.shape[0]
    flattened = field.reshape(heads_here, -1)[
        :, block_rows - 1 : block_rows - 1 + block_rows * (block_rows + length - 2)
    ]
    return flattened.reshape(heads_here, block_rows, block_rows + length - 2)[:, :, :length]


def small_sizes():
    return [27 * CHANNELS, 2 * CHANNELS * CHANNELS, CHANNELS * (MEL // 8) * D, D * CLASSES, 23 * D]


def unpack_small(flattened):
    shapes = [
        (27, CHANNELS),
        (2, CHANNELS, CHANNELS),
        (CHANNELS * (MEL // 8), D),
        (D, CLASSES),
        (23, D),
    ]
    pieces = []
    offset = 0
    for piece_size, piece_shape in zip(small_sizes(), shapes):
        pieces.append(flattened[offset : offset + piece_size].reshape(piece_shape))
        offset += piece_size
    return pieces


def small_rate(positions):
    bounds = []
    offset = 0
    for piece_size in small_sizes():
        offset += piece_size
        bounds.append(offset)
    rate = jnp.full(positions.shape, small_rates[-1], jnp.float32)
    for piece_index in range(len(bounds) - 2, -1, -1):
        rate = jnp.where(positions < bounds[piece_index], small_rates[piece_index], rate)
    return rate


def adam(state, grad, rate):
    first_new = beta_one * state[1] + (1.0 - beta_one) * grad
    second_new = beta_two * state[2] + (1.0 - beta_two) * grad * grad
    direction = (
        first_new
        / (1.0 - beta_one**STEP)
        / (jnp.sqrt(second_new / (1.0 - beta_two**STEP)) + adam_eps)
    )
    weight_new = state[0] - rate * (direction + decay_rate * state[0])
    return (weight_new, first_new, second_new)


def gather_rows(values):
    return lax.all_gather(values, "mp", axis=0, tiled=True)


def scatter_rows(values):
    return lax.psum_scatter(
        values.astype(jnp.bfloat16), "mp", scatter_dimension=0, tiled=True
    ).astype(jnp.float32)


def norm_backward(x_rows, gain, shift, grad_normed):
    _, norm_back = jax.vjp(layer_norm, x_rows, gain, shift)
    return norm_back(grad_normed)


def stem_forward(field, stem_taps, pointwise, linear, tok_rows):
    front = stem_front(field, stem_taps[0:9], stem_taps[9:18]).astype(jnp.bfloat16)
    middle_pre = product(front, pointwise[0])
    middle = stem_middle(middle_pre, stem_taps[18:27]).astype(jnp.bfloat16)
    last_pre = product(middle, pointwise[1])
    last = jax.nn.relu(last_pre).astype(jnp.bfloat16).reshape(tok_rows, -1)
    return (product(last, linear), (field, front, middle_pre, middle, last_pre, last))


def stem_backward(grad_start, stem_kept, stem_taps, pointwise, linear, tok_rows):
    field, front, middle_pre, middle, last_pre, last = stem_kept
    grad_rows = grad_start.astype(jnp.bfloat16)
    grad_linear = product(last.T, grad_rows)
    grad_last = product(grad_rows, linear.T).reshape(tok_rows, MEL // 8, CHANNELS)
    grad_last = jnp.where(last_pre > 0, grad_last, 0.0).astype(jnp.bfloat16)
    grad_point_two = jnp.einsum(
        "nfc,nfe->ce", middle, grad_last, preferred_element_type=jnp.float32
    )
    grad_middle = product(grad_last, pointwise[1].T)
    _, middle_back = jax.vjp(stem_middle, middle_pre, stem_taps[18:27])
    grad_middle_pre, grad_three = middle_back(grad_middle)
    grad_middle_pre = grad_middle_pre.astype(jnp.bfloat16)
    grad_point_one = jnp.einsum(
        "nfc,nfe->ce", front, grad_middle_pre, preferred_element_type=jnp.float32
    )
    grad_front = product(grad_middle_pre, pointwise[0].T)
    _, front_back = jax.vjp(
        lambda w_one, w_two: stem_front(field, w_one, w_two), stem_taps[0:9], stem_taps[9:18]
    )
    grad_one, grad_two = front_back(grad_front)
    grad_taps = jnp.concatenate([grad_one, grad_two, grad_three], 0)
    return (grad_taps, jnp.stack([grad_point_one, grad_point_two]), grad_linear)


def ffn_forward(x_rows, gain, shift, weight_in, weight_out):
    normed = layer_norm(x_rows, gain, shift).astype(jnp.bfloat16)
    gathered = gather_rows(normed)
    pre_act = product(gathered, weight_in)
    hidden = jax.nn.silu(pre_act).astype(jnp.bfloat16)
    summed = scatter_rows(product(hidden, weight_out))
    return (x_rows + 0.5 * summed, (x_rows, gathered, pre_act, hidden))


def ffn_backward(grad_out, kept, gain, shift, weight_in, weight_out):
    x_rows, gathered, pre_act, hidden = kept
    grad_full = gather_rows((0.5 * grad_out).astype(jnp.bfloat16))
    grad_w_out = product(hidden.T, grad_full)
    grad_hidden = product(grad_full, weight_out.T)
    grad_pre = (grad_hidden * silu_grad(pre_act)).astype(jnp.bfloat16)
    grad_w_in = product(gathered.T, grad_pre)
    grad_normed = scatter_rows(product(grad_pre, weight_in.T))
    grad_x, grad_gain, grad_shift = norm_backward(x_rows, gain, shift, grad_normed)
    return (grad_out + grad_x, grad_w_in, grad_w_out, grad_gain, grad_shift)


def attention_scores(block_rows, length, query_u, query_v, keys_h, posit, valid_full):
    raw = jnp.einsum("rhd,khd->hrk", query_u, keys_h, preferred_element_type=jnp.float32)
    raw = raw + skew(
        jnp.einsum("rhd,nhd->hrn", query_v, posit, preferred_element_type=jnp.float32),
        block_rows,
        length,
    )
    scores = jnp.where(valid_full[None, None, :] > 0, raw * 0.125, -1e30)
    return (scores, query_u, query_v, posit)


def attention_forward(x_rows, vec_full, vec_local, weight_in, weight_out, valid_full):
    length = valid_full.shape[0]
    heads_here = weight_in.shape[2] // HEAD_DIM
    block_rows = min(512, length)
    shape_heads = (length, heads_here, HEAD_DIM)
    normed = layer_norm(x_rows, vec_full[1], vec_full[6]).astype(jnp.bfloat16)
    gathered = gather_rows(normed)
    query = product(gathered, weight_in[:, 0])
    query_u = (query + vec_local[12]).astype(jnp.bfloat16).reshape(shape_heads)
    query_v = (query + vec_local[13]).astype(jnp.bfloat16).reshape(shape_heads)
    keys_h = product(gathered, weight_in[:, 1]).astype(jnp.bfloat16).reshape(shape_heads)
    values_h = product(gathered, weight_in[:, 2]).astype(jnp.bfloat16).reshape(shape_heads)
    table = position_table(length).astype(jnp.bfloat16)
    posit = (
        product(table, weight_in[:, 3])
        .astype(jnp.bfloat16)
        .reshape(2 * length - 1, heads_here, HEAD_DIM)
    )

    def forward_block(start):
        scores = attention_scores(block_rows, length, query_u, query_v, keys_h, posit, valid_full)[
            0
        ]
        top = jnp.max(scores, -1, keepdims=True)
        expo = jnp.exp(scores - top)
        total = jnp.sum(expo, -1, keepdims=True)
        probs = expo / total
        block_out = jnp.einsum(
            "hrk,khd->rhd", probs.astype(jnp.bfloat16), values_h, preferred_element_type=jnp.float32
        )
        return (block_out, (top + jnp.log(total))[..., 0])

    starts = jnp.arange(length // block_rows, dtype=jnp.int32) * block_rows
    block_outs, lse_blocks = lax.map(forward_block, starts)
    attended = block_outs.reshape(length, -1).astype(jnp.bfloat16)
    summed = scatter_rows(product(attended, weight_out))
    kept = (
        x_rows,
        gathered,
        query_u,
        query_v,
        keys_h,
        values_h,
        table,
        posit,
        attended,
        lse_blocks,
    )
    return (x_rows + summed, kept)


def attention_backward(grad_out, kept, vec_full, weight_in, weight_out, valid_full):
    x_rows, gathered, query_u, query_v, keys_h, values_h, table, posit, attended, lse_blocks = kept
    length, heads_here = (query_u.shape[0], query_u.shape[1])
    block_rows = min(512, length)
    local_width = heads_here * HEAD_DIM
    grad_full = gather_rows(grad_out.astype(jnp.bfloat16))
    grad_w_out = product(attended.T, grad_full)
    grad_att = (
        product(grad_full, weight_out.T).astype(jnp.bfloat16).reshape(length, heads_here, HEAD_DIM)
    )
    skew_shape = (heads_here, block_rows, block_rows + length - 1)
    _, skew_back = jax.vjp(
        lambda field: skew(field, block_rows, length), jnp.zeros(skew_shape, jnp.float32)
    )

    def back_block(carry, inputs):
        grad_k, grad_v, grad_p = carry
        start, lse_block = inputs
        scores, q_u, q_v, frame = attention_scores(
            block_rows, length, query_u, query_v, keys_h, posit, valid_full
        )
        probs = jnp.exp(scores - lse_block[..., None])
        grad_prob = jnp.einsum(
            "rhd,khd->hrk", grad_att, values_h, preferred_element_type=jnp.float32
        )
        grad_scores = probs * (grad_prob - jnp.sum(probs * grad_prob, -1, keepdims=True))
        grad_raw = (grad_scores * 0.125).astype(jnp.bfloat16)
        grad_q_u = jnp.einsum("hrk,khd->rhd", grad_raw, keys_h, preferred_element_type=jnp.float32)
        grad_k = grad_k + jnp.einsum(
            "hrk,rhd->khd", grad_raw, q_u, preferred_element_type=jnp.float32
        )
        grad_v = grad_v + jnp.einsum(
            "hrk,rhd->khd", probs.astype(jnp.bfloat16), grad_att, preferred_element_type=jnp.float32
        )
        grad_skewed = skew_back(grad_raw.astype(jnp.float32))[0].astype(jnp.bfloat16)
        grad_q_v = jnp.einsum(
            "hrn,nhd->rhd", grad_skewed, frame, preferred_element_type=jnp.float32
        )
        grad_frame = jnp.einsum(
            "hrn,rhd->nhd", grad_skewed, q_v, preferred_element_type=jnp.float32
        )
        old_frame = grad_p
        grad_p = old_frame + grad_frame
        return ((grad_k, grad_v, grad_p), (grad_q_u, grad_q_v))

    starts = jnp.arange(length // block_rows, dtype=jnp.int32) * block_rows
    zero_keys = jnp.zeros((length, heads_here, HEAD_DIM), jnp.float32)
    zero_posit = jnp.zeros((2 * length - 1, heads_here, HEAD_DIM), jnp.float32)
    carried, per_block = lax.scan(
        back_block, (zero_keys, zero_keys, zero_posit), (starts, lse_blocks)
    )
    grad_k, grad_v, grad_p = carried
    grad_q_u = per_block[0].reshape(length, local_width)
    grad_q_v = per_block[1].reshape(length, local_width)
    grad_bias = jnp.stack([jnp.sum(grad_q_u, 0), jnp.sum(grad_q_v, 0)])
    grad_query = (grad_q_u + grad_q_v).astype(jnp.bfloat16)
    grad_keys = grad_k.reshape(length, local_width).astype(jnp.bfloat16)
    grad_vals = grad_v.reshape(length, local_width).astype(jnp.bfloat16)
    grad_posit = grad_p.reshape(2 * length - 1, local_width).astype(jnp.bfloat16)
    grad_w_in = jnp.stack(
        [
            product(gathered.T, grad_query),
            product(gathered.T, grad_keys),
            product(gathered.T, grad_vals),
            product(table.T, grad_posit),
        ],
        1,
    )
    grad_gathered = product(grad_query, weight_in[:, 0].T) + product(grad_keys, weight_in[:, 1].T)
    grad_gathered = grad_gathered + product(grad_vals, weight_in[:, 2].T)
    grad_normed = scatter_rows(grad_gathered)
    grad_x, grad_gain, grad_shift = norm_backward(x_rows, vec_full[1], vec_full[6], grad_normed)
    return (grad_out + grad_x, grad_w_in, grad_w_out, grad_gain, grad_shift, grad_bias)


def conv_forward(x_rows, vec_full, vec_local, weight_in, weight_out, valid_full, frame_count):
    normed = layer_norm(x_rows, vec_full[2], vec_full[7]).astype(jnp.bfloat16)
    gathered = gather_rows(normed)
    gates = product(gathered, weight_in[:, 4:6].reshape(D, -1))
    hidden = glu_depth(gates, vec_local[14:23], valid_full)
    mask_col = valid_full[:, None]
    part_one = jnp.sum(mask_col * hidden, 0)
    part_two = jnp.sum(mask_col * hidden * hidden, 0)
    sum_one, sum_two = lax.psum((part_one, part_two), "dp")
    mean_vals = sum_one / frame_count
    inverse = lax.rsqrt(sum_two / frame_count - mean_vals * mean_vals + norm_eps)
    normal_h = (hidden - mean_vals) * inverse
    batch_out = normal_h * vec_local[10] + vec_local[11]
    activated = jax.nn.silu(batch_out).astype(jnp.bfloat16)
    summed = scatter_rows(product(activated, weight_out))
    kept = (x_rows, gathered, gates, normal_h, inverse, batch_out, activated)
    return (x_rows + summed, kept, frame_count)


def conv_backward(
    grad_out, kept, vec_full, vec_local, weight_in, weight_out, valid_full, frame_count
):
    x_rows, gathered, gates, normal_h, inverse, batch_out, activated = kept
    grad_full = gather_rows(grad_out.astype(jnp.bfloat16))
    grad_w_out = product(activated.T, grad_full)
    grad_batch = product(grad_full, weight_out.T) * silu_grad(batch_out)
    grad_bn = jnp.stack([jnp.sum(grad_batch * normal_h, 0), jnp.sum(grad_batch, 0)])
    grad_normal = grad_batch * vec_local[10]
    mask_col = valid_full[:, None]
    total_one, total_two = lax.psum(
        (jnp.sum(mask_col * grad_normal, 0), jnp.sum(mask_col * grad_normal * normal_h, 0)), "dp"
    )
    grad_hidden = inverse * (
        grad_normal - mask_col * (total_one + normal_h * total_two) / frame_count
    )
    _, glu_back = jax.vjp(
        lambda gate_vals, kernel: glu_depth(gate_vals, kernel, valid_full), gates, vec_local[14:23]
    )
    grad_gates, grad_kernel = glu_back(grad_hidden)
    grad_gates = grad_gates.astype(jnp.bfloat16)
    weight_glu = weight_in[:, 4:6].reshape(D, -1)
    grad_w_glu = product(gathered.T, grad_gates).reshape(D, 2, -1)
    grad_normed = scatter_rows(product(grad_gates, weight_glu.T))
    grad_x, grad_gain, grad_shift = norm_backward(x_rows, vec_full[2], vec_full[7], grad_normed)
    return (grad_out + grad_x, grad_w_glu, grad_w_out, grad_gain, grad_shift, grad_bn, grad_kernel)


def layer_forward(start_x, weights, valid_full, frame_count):
    ff_in_w, ff_out_w, mix_in_w, mix_out_w, vec_full, vec_local = weights
    after_one, kept_one = ffn_forward(start_x, vec_full[0], vec_full[5], ff_in_w[0], ff_out_w[0])
    after_att, kept_att = attention_forward(
        after_one, vec_full, vec_local, mix_in_w, mix_out_w[0], valid_full
    )
    after_conv, kept_conv, frame_count = conv_forward(
        after_att, vec_full, vec_local, mix_in_w, mix_out_w[1], valid_full, frame_count
    )
    after_two, kept_two = ffn_forward(after_conv, vec_full[3], vec_full[8], ff_in_w[1], ff_out_w[1])
    return (after_two, (kept_one, kept_att, kept_conv, kept_two), frame_count)


def layer_backward(grad_end, layer_kept, weights, valid_full, frame_count):
    ff_in_w, ff_out_w, mix_in_w, mix_out_w, vec_full, vec_local = weights
    kept_one, kept_att, kept_conv, kept_two = layer_kept
    grad_x, in_two, out_two, gain_two, shift_two = ffn_backward(
        grad_end, kept_two, vec_full[3], vec_full[8], ff_in_w[1], ff_out_w[1]
    )
    grad_x, glu_in, conv_out, gain_conv, shift_conv, grad_bn, grad_kernel = conv_backward(
        grad_x, kept_conv, vec_full, vec_local, mix_in_w, mix_out_w[1], valid_full, frame_count
    )
    grad_x, att_in, att_out, gain_att, shift_att, grad_bias = attention_backward(
        grad_x, kept_att, vec_full, mix_in_w, mix_out_w[0], valid_full
    )
    grad_x, in_one, out_one, gain_one, shift_one = ffn_backward(
        grad_x, kept_one, vec_full[0], vec_full[5], ff_in_w[0], ff_out_w[0]
    )
    grads = (
        jnp.stack([in_one, in_two]),
        jnp.stack([out_one, out_two]),
        jnp.concatenate([att_in, glu_in], 1),
        jnp.stack([att_out, conv_out]),
        (gain_one, gain_att, gain_conv, gain_two),
        (shift_one, shift_att, shift_conv, shift_two),
        jnp.concatenate([grad_bn, grad_bias, grad_kernel], 0),
    )
    return (grad_x, grads)


def head_loss(end_x, vec_full, head_w, labels, loss_weight, frame_count):
    normed = layer_norm(end_x, vec_full[4], vec_full[9]).astype(jnp.bfloat16)
    logits = product(normed, head_w)
    top = jnp.max(logits, -1, keepdims=True)
    log_total = top[:, 0] + jnp.log(jnp.sum(jnp.exp(logits - top), -1))
    onehot = (jnp.arange(CLASSES, dtype=jnp.int32)[None, :] == labels[:, None]).astype(jnp.float32)
    picked = jnp.sum(onehot * logits, -1)
    loss_part = jnp.sum(loss_weight * (log_total - picked))
    grad_logits = (
        (jnp.exp(logits - log_total[:, None]) - onehot) * (loss_weight / frame_count)[:, None]
    ).astype(jnp.bfloat16)
    grad_head = product(normed.T, grad_logits)
    grad_normed = product(grad_logits, head_w.T)
    grad_x, grad_gain, grad_shift = norm_backward(end_x, vec_full[4], vec_full[9], grad_normed)
    return (loss_part, grad_x, grad_head, grad_gain, grad_shift)


def body(mel, lengths, alignment, loss_mask, ff_in, ff_out, mix_in, mix_out, small):
    mp_count = lax.axis_size("mp")
    mp_rank = lax.axis_index("mp")
    tok_rows = alignment.shape[1]
    seq_length = tok_rows * mp_count
    local_width = D // mp_count
    utter_len = lengths[0]
    valid_full = (8 * jnp.arange(seq_length, dtype=jnp.int32) < utter_len).astype(jnp.float32)
    valid_local = lax.dynamic_slice_in_dim(valid_full, mp_rank * tok_rows, tok_rows, 0)
    loss_weight = valid_local * loss_mask[0].astype(jnp.float32)
    frame_count = lax.psum(jnp.sum(valid_full), "dp")
    ff_in_w, ff_out_w, mix_in_w, mix_out_w = (
        lax.all_gather(ff_in[0].astype(jnp.bfloat16), "dp", axis=1, tiled=True),
        lax.all_gather(ff_out[0].astype(jnp.bfloat16), "dp", axis=2, tiled=True),
        lax.all_gather(mix_in[0].astype(jnp.bfloat16), "dp", axis=0, tiled=True),
        lax.all_gather(mix_out[0].astype(jnp.bfloat16), "dp", axis=2, tiled=True),
    )
    small_w = lax.all_gather(small[0].astype(jnp.bfloat16), ("dp", "mp"), axis=0, tiled=True)
    stem_taps, pointwise, linear, head_w, vec_low = unpack_small(small_w)
    stem_taps = stem_taps.astype(jnp.float32)
    vec_full = vec_low.astype(jnp.float32)
    vec_local = lax.dynamic_slice_in_dim(vec_full, mp_rank * local_width, local_width, 1)
    weights = (ff_in_w, ff_out_w, mix_in_w, mix_out_w, vec_full, vec_local)
    frame_index = mp_rank * (8 * tok_rows) + jnp.arange(8 * tok_rows, dtype=jnp.int32)
    mel_local = jnp.where((frame_index < utter_len)[:, None], mel[0], jnp.zeros((), jnp.bfloat16))
    prior_rows = passed_along(mel_local[-8:], "mp", 1)
    extended = jnp.concatenate([prior_rows[1:], mel_local], 0)
    start_x, stem_kept = stem_forward(
        extended.astype(jnp.float32), stem_taps, pointwise, linear, tok_rows
    )
    end_x, layer_kept, frame_count = layer_forward(start_x, weights, valid_full, frame_count)
    loss_part, grad_end, grad_head, final_gain, final_shift = head_loss(
        end_x, vec_full, head_w, alignment[0], loss_weight, frame_count
    )
    again_x = lax.optimization_barrier((start_x, grad_end))[0]
    layer_kept = layer_forward(again_x, weights, valid_full, frame_count)[1]
    grad_start, layer_grads = layer_backward(grad_end, layer_kept, weights, valid_full, frame_count)
    grad_taps, grad_point, grad_linear = stem_backward(
        grad_start, stem_kept, stem_taps, pointwise, linear, tok_rows
    )
    grad_ff_in, grad_ff_out, grad_mix_in, grad_mix_out, gain_grads, shift_grads, local_rows = (
        layer_grads
    )
    gain_rows = jnp.stack(list(gain_grads) + [final_gain] + list(shift_grads) + [final_shift])
    placed = lax.dynamic_update_slice_in_dim(
        jnp.zeros((13, D), jnp.float32), local_rows, mp_rank * local_width, 1
    )
    grad_vec = jnp.concatenate([gain_rows, placed], 0)
    small_grad = jnp.concatenate(
        [
            grad_taps.reshape(-1),
            grad_point.reshape(-1),
            grad_linear.reshape(-1),
            grad_head.reshape(-1),
            jnp.zeros((23 * D,), jnp.float32),
        ]
    )
    own_big = (
        lax.psum_scatter(grad_ff_in, "dp", scatter_dimension=1, tiled=True),
        lax.psum_scatter(grad_ff_out, "dp", scatter_dimension=2, tiled=True),
        lax.psum_scatter(grad_mix_in, "dp", scatter_dimension=0, tiled=True),
        lax.psum_scatter(grad_mix_out, "dp", scatter_dimension=2, tiled=True),
    )
    own_small = lax.psum_scatter(small_grad, ("dp", "mp"), scatter_dimension=0, tiled=True)
    local_sq = sum((jnp.sum(grad_arr * grad_arr) for grad_arr in own_big)) + jnp.sum(
        own_small * own_small
    )
    total_sq, loss_sum, vec_total = lax.psum((local_sq, loss_part, grad_vec), ("dp", "mp"))
    grad_norm = jnp.sqrt(total_sq + jnp.sum(vec_total * vec_total))
    factor = clip_norm / jnp.maximum(grad_norm, clip_norm)
    shard_size = own_small.shape[0]
    vec_start = sum(small_sizes()[:4])
    vec_flat = vec_total.reshape(-1)
    padded_vec = jnp.concatenate(
        [jnp.zeros((shard_size,), jnp.float32), vec_flat, jnp.zeros((shard_size,), jnp.float32)]
    )
    shard_start = lax.axis_index(("dp", "mp")) * shard_size
    vec_offset = jnp.clip(shard_start - vec_start + shard_size, 0, shard_size + vec_flat.shape[0])
    own_small = own_small + lax.dynamic_slice_in_dim(padded_vec, vec_offset, shard_size, 0)
    positions = shard_start + jnp.arange(shard_size, dtype=jnp.int32)
    rates = (0.1, 0.05, 0.1, jnp.array([1.0, 0.1], jnp.float32)[:, None, None])
    states = (ff_in, ff_out, mix_in, mix_out)
    new_big = [
        adam(state, grad_arr * factor, rate)
        for state, grad_arr, rate in zip(states, own_big, rates)
    ]
    new_small = adam(small, own_small * factor, small_rate(positions))
    return (
        new_big[0][0],
        new_big[0][1],
        new_big[0][2],
        new_big[1][0],
        new_big[1][1],
        new_big[1][2],
        new_big[2][0],
        new_big[2][1],
        new_big[2][2],
        new_big[3][0],
        new_big[3][1],
        new_big[3][2],
        new_small[0],
        new_small[1],
        new_small[2],
        vec_total * factor,
        loss_sum / frame_count,
        grad_norm,
    )


def solution(mesh):
    in_specs = (
        P("dp", "mp", None),
        P("dp"),
        P("dp", "mp"),
        P("dp", "mp"),
        P(None, None, "dp", "mp"),
        P(None, None, "mp", "dp"),
        P(None, "dp", None, "mp"),
        P(None, None, "mp", "dp"),
        P(None, ("dp", "mp")),
    )
    out_specs = (
        P(None, "dp", "mp"),
        P(None, "dp", "mp"),
        P(None, "dp", "mp"),
        P(None, "mp", "dp"),
        P(None, "mp", "dp"),
        P(None, "mp", "dp"),
        P("dp", None, "mp"),
        P("dp", None, "mp"),
        P("dp", None, "mp"),
        P(None, "mp", "dp"),
        P(None, "mp", "dp"),
        P(None, "mp", "dp"),
        P(("dp", "mp")),
        P(("dp", "mp")),
        P(("dp", "mp")),
        P(),
        P(),
        P(),
    )
    return jax.shard_map(body, mesh=mesh, in_specs=in_specs, out_specs=out_specs, check_vma=False)
```

profile of v0, /device:TPU:0, one launch (start us, length us, event | category | flops | bytes accessed | tf_op | source)
XLA Modules:
  0.0 2064.8 jit_solution(4998721976991620332)
XLA Ops:
  29.3 33.3 %all_gather.57 = bf16[2,128,512]{1,0,2:T(2,128)(2,1)S(1)} all-gather(bf16[2,128,64]{1,0,2:T(2,128)(2,1)S(1)} %bitcast.438), channel_id=1, replica_groups=mesh['dp'=8,'mp'=4] {'dp'}, dimensions={2}, use_global_device_ids=true | all-gather | bytes 294912 | tf_op jit(solution)/shard_map/all_gather | solution.py:481
  96.5 77.5 %all-reduce.76.cloned.1.call-done = bf16[1985280]{0:T(1024)(128)(2,1)} async-done(((bf16[1985280]{0:T(1024)(128)(2,1)}), bf16[1985280]{0:T(1024)(128)(2,1)}) %all-reduce.76.cloned.1.call-update) | async-done | bytes 3970576
  174.8 18.0 broadcast_maximum_fusion
  192.8 16.0 pad.224
  208.8 35.0 %slice.644 = f32[257,20,256]{2,0,1:T(8,128)} slice(f32[515,42,256]{2,0,1:T(8,128)} %pad.224), slice={[0:513:2], [0:39:2], [0:256:1]} | slice | bytes 10526720 | tf_op jit(solution)/shard_map/slice | solution.py:55
  243.8 34.9 %slice.647 = f32[257,20,256]{2,0,1:T(8,128)} slice(f32[515,42,256]{2,0,1:T(8,128)} %pad.224), slice={[0:513:2], [1:40:2], [0:256:1]} | slice | bytes 10526720 | tf_op jit(solution)/shard_map/slice | solution.py:55
  278.7 35.0 %slice.649 = f32[257,20,256]{2,0,1:T(8,128)} slice(f32[515,42,256]{2,0,1:T(8,128)} %pad.224), slice={[0:513:2], [2:41:2], [0:256:1]} | slice | bytes 10526720 | tf_op jit(solution)/shard_map/slice | solution.py:55
  313.7 35.0 %slice.651 = f32[257,20,256]{2,0,1:T(8,128)} slice(f32[515,42,256]{2,0,1:T(8,128)} %pad.224), slice={[1:514:2], [0:39:2], [0:256:1]} | slice | bytes 10526720 | tf_op jit(solution)/shard_map/slice | solution.py:55
  348.7 35.0 %slice.653 = f32[257,20,256]{2,0,1:T(8,128)} slice(f32[515,42,256]{2,0,1:T(8,128)} %pad.224), slice={[1:514:2], [1:40:2], [0:256:1]} | slice | bytes 10526720 | tf_op jit(solution)/shard_map/slice | solution.py:55
  383.8 34.9 %slice.655 = f32[257,20,256]{2,0,1:T(8,128)} slice(f32[515,42,256]{2,0,1:T(8,128)} %pad.224), slice={[1:514:2], [2:41:2], [0:256:1]} | slice | bytes 10526720 | tf_op jit(solution)/shard_map/slice | solution.py:55
  418.7 35.4 %slice.657 = f32[257,20,256]{2,0,1:T(8,128)} slice(f32[515,42,256]{2,0,1:T(8,128)} %pad.224), slice={[2:515:2], [0:39:2], [0:256:1]} | slice | bytes 10526720 | tf_op jit(solution)/shard_map/slice | solution.py:55
  454.1 35.3 %slice.659 = f32[257,20,256]{2,0,1:T(8,128)} slice(f32[515,42,256]{2,0,1:T(8,128)} %pad.224), slice={[2:515:2], [1:40:2], [0:256:1]} | slice | bytes 10526720 | tf_op jit(solution)/shard_map/slice | solution.py:55
  489.4 35.4 %slice.661 = f32[257,20,256]{2,0,1:T(8,128)} slice(f32[515,42,256]{2,0,1:T(8,128)} %pad.224), slice={[2:515:2], [2:41:2], [0:256:1]} | slice | bytes 10526720 | tf_op jit(solution)/shard_map/slice | solution.py:55
  526.8 16.9 add_convert_fusion
  570.6 11.9 slice.669
  617.3 11.7 slice.677
  629.1 11.7 slice.679
  640.8 11.9 slice.681
  687.5 32.4 %all_gather.56 = bf16[512,6,128]{2,0,1:T(8,128)(2,1)S(1)} all-gather(bf16[64,6,128]{2,0,1:T(8,128)(2,1)} %bitcast_convert_fusion.1), channel_id=1, replica_groups=mesh['dp'=8,'mp'=4] {'dp'}, dimensions={0}, use_global_device_ids=true | all-gather | bytes 884736 | tf_op jit(solution)/shard_map/all_gather | solution.py:480
  782.9 17.9 reduce-scatter.16.cloned.1.call-done
  813.3 22.0 %all-reduce.70 = (f32[128]{0:T(128)S(1)}, f32[]{:T(128)}, f32[128]{0:T(128)S(1)}) all-reduce(f32[128]{0:T(128)} %get-tuple-element.395, f32[]{:T(128)} %fusion.135, f32[128]{0:T(128)} %get-tuple-element.394), channel_id=1, replica_groups=mesh['dp'=8,'mp'=4] {'dp'}, use_global_device_ids=true, to_apply=%region_11.12 | all-reduce | flops 257 | bytes 2056 | tf_op jit(solution)/shard_map/psum | solution.py:370
  841.7 15.0 reduce-scatter.18.cloned.1.call-done
  875.7 15.3 reduce-scatter.20.cloned.1.call-done
  910.4 22.1 %reduce-scatter.22.cloned.1.call-done = bf16[128,512]{1,0:T(8,128)(2,1)} async-done(((bf16[512,512]{1,0:T(8,128)(2,1)}), bf16[128,512]{1,0:T(8,128)(2,1)}) %reduce-scatter.22.cloned.1.call-update) | async-done | bytes 131088 | tf_op jit(solution)/shard_map/reduce_scatter | solution.py:160
  987.3 22.1 %reduce-scatter.24.cloned.1.call-done = bf16[128,512]{1,0:T(8,128)(2,1)} async-done(((bf16[512,512]{1,0:T(8,128)(2,1)}), bf16[128,512]{1,0:T(8,128)(2,1)}) %reduce-scatter.24.cloned.1.call-update) | async-done | bytes 131088 | tf_op jit(solution)/shard_map/reduce_scatter | solution.py:160
  1023.8 22.0 %all-reduce.69 = (f32[128]{0:T(128)}, f32[128]{0:T(128)}) all-reduce(f32[128]{0:T(128)} %get-tuple-element.393, f32[128]{0:T(128)} %get-tuple-element.392), channel_id=1, replica_groups=mesh['dp'=8,'mp'=4] {'dp'}, use_global_device_ids=true, to_apply=%region_37.38 | all-reduce | flops 256 | bytes 2048 | tf_op jit(solution)/shard_map/psum | solution.py:370
  1082.6 21.7 %reduce-scatter.28.cloned.1.call-done = bf16[128,512]{1,0:T(8,128)(2,1)} async-done(((bf16[512,512]{1,0:T(8,128)(2,1)}), bf16[128,512]{1,0:T(8,128)(2,1)}) %reduce-scatter.28.cloned.1.call-update) | async-done | bytes 131088 | tf_op jit(solution)/shard_map/reduce_scatter | solution.py:160
  1118.8 22.1 %all-reduce.68 = (f32[128]{0:T(128)}, f32[128]{0:T(128)}) all-reduce(f32[128]{0:T(128)} %get-tuple-element.371, f32[128]{0:T(128)} %get-tuple-element.391), channel_id=1, replica_groups=mesh['dp'=8,'mp'=4] {'dp'}, use_global_device_ids=true, to_apply=%region_49.50 | all-reduce | flops 256 | bytes 2048 | tf_op jit(solution)/shard_map/psum | solution.py:391
  1149.4 17.1 reduce-scatter.30.cloned.1.call-done
  1240.3 17.7 reduce-scatter.32.cloned.1.call-done
  1404.4 14.6 fusion.18
  1419.1 30.4 %multiply_reduce_fusion.8 = (f32[256]{0:T(256)}, f32[256]{0:T(256)}, f32[256]{0:T(256)}, f32[256]{0:T(256)}, f32[256]{0:T(256)}, /*index=5*/f32[256]{0:T(256)}, ...) fusion(f32[257,20,256]{2,0,1:T(8,128)} %slice.661, ...), kind=kOutput, calls=%fused_computation.33 | convolution fusion | flops 709235456 | bytes 97521664 | tf_op jit(solution)/shard_map/dot_general | solution.py:34
  1449.5 21.2 %pad.252 = f32[515,42,256]{2,0,1:T(8,128)} pad(f32[257,20,256]{2,0,1:T(8,128)} %get-tuple-element.465, f32[]{:T(128)} %constant.91.clone.1), padding=2_0_1x2_1_1x0_0_0 | pad | bytes 27412484 | tf_op jit(solution)/shard_map/transpose(jvp())/pad | solution.py:55
  1470.7 21.2 %pad.253 = f32[515,42,256]{2,0,1:T(8,128)} pad(f32[257,20,256]{2,0,1:T(8,128)} %get-tuple-element.464, f32[]{:T(128)} %constant.91.clone.1), padding=2_0_1x1_2_1x0_0_0 | pad | bytes 27412484 | tf_op jit(solution)/shard_map/transpose(jvp())/pad | solution.py:55
  1491.9 21.2 %pad.254 = f32[515,42,256]{2,0,1:T(8,128)} pad(f32[257,20,256]{2,0,1:T(8,128)} %get-tuple-element.466, f32[]{:T(128)} %constant.91.clone.1), padding=2_0_1x0_3_1x0_0_0 | pad | bytes 27412484 | tf_op jit(solution)/shard_map/transpose(jvp())/pad | solution.py:55
  1513.1 20.8 %pad.492 = f32[515,41,256]{2,0,1:T(8,128)} pad(f32[257,20,256]{2,0,1:T(8,128)} %get-tuple-element.472, f32[]{:T(128)} %constant.91.clone.1), padding=0_2_1x0_2_1x0_0_0 | pad | bytes 26885124
  1533.9 21.0 %pad.493 = f32[515,41,256]{2,0,1:T(8,128)} pad(f32[257,20,256]{2,0,1:T(8,128)} %get-tuple-element.469, f32[]{:T(128)} %constant.91.clone.1), padding=1_1_1x0_2_1x0_0_0 | pad | bytes 26885124
  1555.0 20.7 %pad.321 = f32[515,40,256]{2,0,1:T(8,128)} pad(f32[257,20,256]{2,0,1:T(8,128)} %get-tuple-element.467, f32[]{:T(128)} %constant.91.clone.1), padding=1_1_1x1_0_1x0_0_0 | pad | bytes 26357764 | tf_op jit(solution)/shard_map/transpose(jvp(jit(_pad)))/pad | solution.py:53
  1575.7 20.7 %pad.322 = f32[515,40,256]{2,0,1:T(8,128)} pad(f32[257,20,256]{2,0,1:T(8,128)} %get-tuple-element.468, f32[]{:T(128)} %constant.91.clone.1), padding=1_1_1x0_1_1x0_0_0 | pad | bytes 26357764 | tf_op jit(solution)/shard_map/transpose(jvp(jit(_pad)))/pad | solution.py:53
  1596.4 20.7 %pad.324 = f32[515,40,256]{2,0,1:T(8,128)} pad(f32[257,20,256]{2,0,1:T(8,128)} %get-tuple-element.470, f32[]{:T(128)} %constant.91.clone.1), padding=0_2_1x1_0_1x0_0_0 | pad | bytes 26357764 | tf_op jit(solution)/shard_map/transpose(jvp(jit(_pad)))/pad | solution.py:53
  1617.1 20.8 %pad.325 = f32[515,40,256]{2,0,1:T(8,128)} pad(f32[257,20,256]{2,0,1:T(8,128)} %get-tuple-element.471, f32[]{:T(128)} %constant.91.clone.1), padding=0_2_1x0_1_1x0_0_0 | pad | bytes 26357764 | tf_op jit(solution)/shard_map/transpose(jvp(jit(_pad)))/pad | solution.py:53
  1637.9 29.5 %add_add_fusion = f32[515,42,256]{2,0,1:T(8,128)} fusion(f32[515,42,256]{2,0,1:T(8,128)} %pad.254, f32[515,42,256]{2,0,1:T(8,128)} %pad.252, f32[515,42,256]{2,0,1:T(8,128)} %pad.253), kind=kLoop, calls=%fused_computation.2 | loop fusion | flops 11074560 | bytes 88596480 | tf_op jit(solution)/shard_map/transpose(jvp())/add_any | solution.py:55
  1667.4 59.6 %fusion.291 = f32[515,40,256]{2,0,1:T(8,128)} fusion(f32[515,40,256]{2,0,1:T(8,128)} %pad.325, f32[515,40,256]{2,0,1:T(8,128)} %pad.324, f32[515,40,256]{2,0,1:T(8,128)} %pad.322, f32[515,40,256]{2,0,1:T(8,128)} %pad.321, f32[515,42,256]{2,0,1:T(8,128)} %add_add_fusion, f32[515,40,256]{2,0,1:T(8,128)} %get-tuple-element.555, ...), kind=kLoop, calls=%fused_computation.9.clone.clone.clone.clone.1 | loop fusion | flops 42188800 | bytes 189849600 | tf_op jit(solution)/shard_map/transpose(jvp(tfk,kc->tfc))/dot_general | solution.py:63
  1729.7 15.2 fusion.31
  1752.7 45.5 %dynamic-update-slice.3 = f32[1985280]{0:T(1024)} dynamic-update-slice(f32[1985280]{0:T(1024)} %constant_dynamic-update-slice_fusion.1, f32[1310720]{0:T(1024)} %bitcast.397, s32[]{} %constant.396) | dynamic-update-slice | bytes 10485764
  1798.2 18.1 dynamic-update-slice.4
  1829.6 164.2 %all-reduce.78.cloned.1.call-done = f32[1985280]{0:T(1024)} async-done(((f32[1985280]{0:T(1024)}), f32[1985280]{0:T(1024)}) %all-reduce.78.cloned.1.call-update) | async-done | bytes 7941136
  1996.1 40.7 %all-reduce.67 = (f32[]{:T(128)}, f32[23,512]{1,0:T(8,128)S(1)}, f32[]{:T(128)}) all-reduce(f32[]{:T(128)S(6)} %add.839, f32[23,512]{1,0:T(8,128)S(1)} %concatenate.32, f32[]{:T(128)} %get-tuple-element.431), channel_id=1, replica_groups=mesh['dp'=8,'mp'=4] {'dp','mp'}, use_global_device_ids=true, to_apply=%region_88.89 | all-reduce | flops 11778 | bytes 94224 | tf_op jit(solution)/shard_map/psum | solution.py:533
  (876 shorter events, 657.7 us)
Async XLA Ops:
  8.0 81.6 %all-gather.5.cloned.1.call-start = ((), (), s32[]{:S(2)}) async-start(), calls=%async_computation.14 | async-start | bytes 1179648 | tf_op jit(solution)/shard_map/all_gather | solution.py:479
  11.7 162.4 %all-reduce.76.cloned.1.call-start = ((), (), s32[]{:S(2)}) async-start(), calls=%async_computation.28 | async-start | bytes 7942144
  20.4 658.7 %all-gather.3.cloned.1.call-start = ((), (), s32[]{:S(2)}) async-start(), calls=%async_computation.13 | async-start | bytes 1179648 | tf_op jit(solution)/shard_map/all_gather | solution.py:478
  21.2 42.7 %collective-permute-start = (bf16[8,80]{0,1:T(8,128)(2,1)S(1)}, bf16[8,80]{0,1:T(8,128)(2,1)S(1)}, u32[]{:S(2)}, u32[]{:S(2)}) collective-permute-start(bf16[8,80]{0,1:T(8,128)(2,1)S(1)} %slice.758), channel_id=1, source_target_pairs={{0,1},{1,2},{2,3},{4,5},{5,6},{6,7},{8,9},{9,10},{10,11},{12,13},{... | collective-permute-start | bytes 3848 | tf_op jit(solution)/shard_map/ppermute | solution.py:30
  25.2 696.8 %reduce-scatter.14.cloned.1.call-start = ((), (), s32[]{:S(2)}) async-start(), calls=%async_computation.15 | async-start | bytes 655360 | tf_op jit(solution)/shard_map/reduce_scatter | solution.py:160
  63.9 713.7 %copy-start.66 = (bf16[1,128,512]{2,1,0:T(8,128)(2,1)}, bf16[1,128,512]{2,1,0:T(8,128)(2,1)S(1)}, u32[]{:S(2)}) copy-start(bf16[1,128,512]{2,1,0:T(8,128)(2,1)S(1)} %copy.844) | copy-start | bytes 393220
  89.6 85.2 %copy-start.2 = (f32[515,40,9]{0,1,2:T(8,128)}, f32[515,40,9]{0,1,2:T(8,128)S(1)}, u32[]{:S(2)}) copy-start(f32[515,40,9]{0,1,2:T(8,128)S(1)} %bitcast_dynamic-update-slice_fusion) | copy-start | bytes 2224804
  525.6 127.1 %copy-start.161 = (f32[256]{0:T(256)}, f32[256]{0:T(256)S(1)}, u32[]{:S(2)}) copy-start(f32[256]{0:T(256)S(1)} %get-tuple-element.533) | copy-start | bytes 3076
  525.6 127.1 %copy-start.163 = (f32[256]{0:T(256)}, f32[256]{0:T(256)S(1)}, u32[]{:S(2)}) copy-start(f32[256]{0:T(256)S(1)} %get-tuple-element.534) | copy-start | bytes 3076
  525.6 127.1 %copy-start.165 = (f32[256]{0:T(256)}, f32[256]{0:T(256)S(1)}, u32[]{:S(2)}) copy-start(f32[256]{0:T(256)S(1)} %get-tuple-element.535) | copy-start | bytes 3076
  525.6 127.1 %copy-start.167 = (f32[256]{0:T(256)}, f32[256]{0:T(256)S(1)}, u32[]{:S(2)}) copy-start(f32[256]{0:T(256)S(1)} %get-tuple-element.536) | copy-start | bytes 3076
  525.6 127.1 %copy-start.169 = (f32[256]{0:T(256)}, f32[256]{0:T(256)S(1)}, u32[]{:S(2)}) copy-start(f32[256]{0:T(256)S(1)} %get-tuple-element.537) | copy-start | bytes 3076
  525.7 127.1 %copy-start.171 = (f32[256]{0:T(256)}, f32[256]{0:T(256)S(1)}, u32[]{:S(2)}) copy-start(f32[256]{0:T(256)S(1)} %get-tuple-element.538) | copy-start | bytes 3076
  525.7 127.1 %copy-start.173 = (f32[256]{0:T(256)}, f32[256]{0:T(256)S(1)}, u32[]{:S(2)}) copy-start(f32[256]{0:T(256)S(1)} %get-tuple-element.539) | copy-start | bytes 3076
  525.7 127.1 %copy-start.175 = (f32[256]{0:T(256)}, f32[256]{0:T(256)S(1)}, u32[]{:S(2)}) copy-start(f32[256]{0:T(256)S(1)} %get-tuple-element.540) | copy-start | bytes 3076
  525.7 127.1 %copy-start.177 = (f32[256]{0:T(256)}, f32[256]{0:T(256)S(1)}, u32[]{:S(2)}) copy-start(f32[256]{0:T(256)S(1)} %get-tuple-element.541) | copy-start | bytes 3076
  560.2 92.7 %copy-start.4 = (f32[128,10,256]{2,0,1:T(8,128)}, f32[128,10,256]{2,0,1:T(8,128)S(1)}, u32[]{:S(2)}) copy-start(f32[128,10,256]{2,0,1:T(8,128)S(1)} %slice.665) | copy-start | bytes 3932164
  570.6 82.2 %copy-start.6 = (f32[128,10,256]{2,0,1:T(8,128)}, f32[128,10,256]{2,0,1:T(8,128)S(1)}, u32[]{:S(2)}) copy-start(f32[128,10,256]{2,0,1:T(8,128)S(1)} %slice.667) | copy-start | bytes 3932164
  670.7 52.6 %copy-start.132 = (f32[512]{0:T(512)}, f32[512]{0:T(512)S(1)}, u32[]{:S(2)}) copy-start(f32[512]{0:T(512)S(1)} %get-tuple-element.516) | copy-start | bytes 6148
  682.0 39.3 %copy-start.122 = (f32[11776]{0:T(1024)S(1)}, f32[11776]{0:T(1024)}, u32[]{:S(2)}) copy-start(f32[11776]{0:T(1024)} %copy-done.121) | copy-start | bytes 141316
  682.0 118.8 %reduce-scatter.16.cloned.1.call-start = ((), (), s32[]{:S(2)}) async-start(), calls=%async_computation.16 | async-start | bytes 655360 | tf_op jit(solution)/shard_map/reduce_scatter | solution.py:160
  779.6 77.1 %reduce-scatter.18.cloned.1.call-start = ((), (), s32[]{:S(2)}) async-start(), calls=%async_computation.17 | async-start | bytes 655360 | tf_op jit(solution)/shard_map/reduce_scatter | solution.py:160
  811.1 45.5 %copy-start.65 = (bf16[128,512]{1,0:T(8,128)(2,1)S(1)}, bf16[128,512]{1,0:T(8,128)(2,1)}, u32[]{:S(2)}) copy-start(bf16[128,512]{1,0:T(8,128)(2,1)} %reduce-scatter.16.cloned.1.call-done) | copy-start | bytes 393220
  838.1 52.9 %reduce-scatter.20.cloned.1.call-start = ((), (), s32[]{:S(2)}) async-start(), calls=%async_computation.18 | async-start | bytes 655360 | tf_op jit(solution)/shard_map/reduce_scatter | solution.py:160
  868.8 63.6 %reduce-scatter.22.cloned.1.call-start = ((), (), s32[]{:S(2)}) async-start(), calls=%async_computation.19 | async-start | bytes 655360 | tf_op jit(solution)/shard_map/reduce_scatter | solution.py:160
  910.3 99.1 %reduce-scatter.24.cloned.1.call-start = ((), (), s32[]{:S(2)}) async-start(), calls=%async_computation.20 | async-start | bytes 655360 | tf_op jit(solution)/shard_map/reduce_scatter | solution.py:160
  942.7 38.9 %copy-start.113 = (bf16[512,128]{0,1:T(8,128)(2,1)}, bf16[512,128]{0,1:T(8,128)(2,1)S(1)}, u32[]{:S(2)}) copy-start(bf16[512,128]{0,1:T(8,128)(2,1)S(1)} %get-tuple-element.501) | copy-start | bytes 393220
  987.3 81.0 %reduce-scatter.26.cloned.1.call-start = ((), (), s32[]{:S(2)}) async-start(), calls=%async_computation.21 | async-start | bytes 655360 | tf_op jit(solution)/shard_map/reduce_scatter | solution.py:160
  1049.8 54.5 %reduce-scatter.28.cloned.1.call-start = ((), (), s32[]{:S(2)}) async-start(), calls=%async_computation.22 | async-start | bytes 655360 | tf_op jit(solution)/shard_map/reduce_scatter | solution.py:160
  1082.1 84.4 %reduce-scatter.30.cloned.1.call-start = ((), (), s32[]{:S(2)}) async-start(), calls=%async_computation.23 | async-start | bytes 655360 | tf_op jit(solution)/shard_map/reduce_scatter | solution.py:160
  1148.1 109.9 %reduce-scatter.32.cloned.1.call-start = ((), (), s32[]{:S(2)}) async-start(), calls=%async_computation.24 | async-start | bytes 655360 | tf_op jit(solution)/shard_map/reduce_scatter | solution.py:160
  1235.8 79.8 %reduce-scatter.38.cloned.1.call-start = ((), (), s32[]{:S(2)}) async-start(), calls=%async_computation.27 | async-start | bytes 655360 | tf_op jit(solution)/shard_map/reduce_scatter | solution.py:160
  1273.2 547.2 %reduce-scatter.36.cloned.1.call-start = ((), (), s32[]{:S(2)}) async-start(), calls=%async_computation.26 | async-start | bytes 2359296 | tf_op jit(solution)/shard_map/reduce_scatter | solution.py:526
  1286.4 535.7 %all-reduce.80.cloned.1.call-start = ((), (), s32[]{:S(2)}) async-start(), calls=%async_computation.30 | async-start | bytes 5242880
  1298.7 526.7 %reduce-scatter.34.cloned.1.call-start = ((), (), s32[]{:S(2)}) async-start(), calls=%async_computation.25 | async-start | bytes 2359296 | tf_op jit(solution)/shard_map/reduce_scatter | solution.py:524
  1315.6 678.2 %all-reduce.78.cloned.1.call-start = ((), (), s32[]{:S(2)}) async-start(), calls=%async_computation.29 | async-start | bytes 15884288
  1667.4 59.6 %copy-start.50 = (bf16[128,10,256]{2,0,1:T(8,128)(2,1)S(1)}, bf16[128,10,256]{2,0,1:T(8,128)(2,1)}, u32[]{:S(2)}) copy-start(bf16[128,10,256]{2,0,1:T(8,128)(2,1)} %copy-done.49) | copy-start | bytes 1966084
  1667.4 59.6 %copy-start.52 = (bf16[128,10,256]{2,0,1:T(8,128)(2,1)S(1)}, bf16[128,10,256]{2,0,1:T(8,128)(2,1)}, u32[]{:S(2)}) copy-start(bf16[128,10,256]{2,0,1:T(8,128)(2,1)} %copy-done.51) | copy-start | bytes 1966084
  1667.4 60.0 %copy-start.12 = (bf16[257,20,256]{2,0,1:T(8,128)(2,1)S(1)}, bf16[257,20,256]{2,0,1:T(8,128)(2,1)}, u32[]{:S(2)}) copy-start(bf16[257,20,256]{2,0,1:T(8,128)(2,1)} %fusion.18) | copy-start | bytes 7895044
  1667.4 60.0 %copy-start.14 = (bf16[257,20,256]{2,0,1:T(8,128)(2,1)S(1)}, bf16[257,20,256]{2,0,1:T(8,128)(2,1)}, u32[]{:S(2)}) copy-start(bf16[257,20,256]{2,0,1:T(8,128)(2,1)} %copy-done.13) | copy-start | bytes 7895044
  1752.7 45.5 %copy-start.17 = (f32[524800]{0:T(1024)S(1)}, f32[524800]{0:T(1024)}, u32[]{:S(2)}) copy-start(f32[524800]{0:T(1024)} %reshape.717) | copy-start | bytes 6297604
  1817.9 222.8 %copy-start.96 = (f32[1,2,128,64]{2,3,1,0:T(8,128)S(1)}, f32[1,2,128,64]{2,3,1,0:T(8,128)}, u32[]{:S(2)}) copy-start(f32[1,2,128,64]{2,3,1,0:T(8,128)} %copy-done.95) | copy-start | bytes 196612
  1818.0 222.8 %copy-start.123 = (f32[1,2,128,64]{2,3,1,0:T(8,128)S(1)}, f32[1,2,128,64]{2,3,1,0:T(8,128)}, u32[]{:S(2)}) copy-start(f32[1,2,128,64]{2,3,1,0:T(8,128)} %get-tuple-element.507) | copy-start | bytes 196612
  1818.0 222.8 %copy-start.124 = (f32[1,2,128,64]{2,3,1,0:T(8,128)S(1)}, f32[1,2,128,64]{2,3,1,0:T(8,128)}, u32[]{:S(2)}) copy-start(f32[1,2,128,64]{2,3,1,0:T(8,128)} %get-tuple-element.508) | copy-start | bytes 196612
  1818.0 222.8 %copy-start.257 = (f32[2]{0:T(128)S(1)}, f32[2]{0:T(128)}, u32[]{:S(2)}) copy-start(f32[2]{0:T(128)} %constant.244.clone) | copy-start | bytes 28
  1818.0 225.8 %copy-start.59 = (f32[1,2,512,64]{2,3,1,0:T(8,128)S(1)}, f32[1,2,512,64]{2,3,1,0:T(8,128)}, u32[]{:S(2)}) copy-start(f32[1,2,512,64]{2,3,1,0:T(8,128)} %copy-done.58) | copy-start | bytes 786436
  1818.0 225.7 %copy-start.85 = (f32[1,2,512,64]{2,3,1,0:T(8,128)S(1)}, f32[1,2,512,64]{2,3,1,0:T(8,128)}, u32[]{:S(2)}) copy-start(f32[1,2,512,64]{2,3,1,0:T(8,128)} %get-tuple-element.486) | copy-start | bytes 786436
  1818.0 225.7 %copy-start.86 = (f32[1,2,512,64]{2,3,1,0:T(8,128)S(1)}, f32[1,2,512,64]{2,3,1,0:T(8,128)}, u32[]{:S(2)}) copy-start(f32[1,2,512,64]{2,3,1,0:T(8,128)} %get-tuple-element.487) | copy-start | bytes 786436
  (233 other events, 1345.9 us)
Sparse Core Ops, SparseCore 0:
  11.8 50.4 all-gather.4
  65.1 40.8 all-gather.2
  1298.8 131.0 all-reduce.79
  1818.1 175.5 all-reduce.77
Sparse Core Ops, SparseCore 1:
  20.4 153.6 all-reduce.75
  682.0 21.0 reduce-scatter.13
  779.7 21.1 reduce-scatter.15
  838.2 18.4 reduce-scatter.17
  868.9 22.0 reduce-scatter.19
  910.4 22.0 reduce-scatter.21
  987.4 22.0 reduce-scatter.23
  1049.9 18.3 reduce-scatter.25
  1082.2 22.0 reduce-scatter.27
  1148.2 18.3 reduce-scatter.29
  1235.9 22.0 reduce-scatter.31
  1273.2 22.0 reduce-scatter.37
  1299.1 95.5 reduce-scatter.35
  1398.6 82.1 reduce-scatter.33
where the time goes:
time: 2090 us; the launch traced here: 2060 us
  local copies, waits for them, and re-layouts  970 us (46%)
  waiting for transfers between devices  402 us (19%)
  blocking collectives  255 us (12%)
  other arithmetic  228 us (11%)
  matrix products  178 us (9%)
  between operations  28.8 us (1%)
    slice x27, local copies, waits for them, and re-layouts, strided_taps(): padded[row_tap:row_tap + 2 * out_count - 1:2, col_tap:col_tap + freq_widt...  444 us
    unnamed x21, waiting for transfers between devices  242 us
    unnamed x561, local copies, waits for them, and re-layouts  184 us
    reduce_scatter x11, waiting for transfers between devices, scatter_rows(): lax.psum_scatter(values.astype(jnp.bfloat16), 'mp', scatter_dimension=0,...  160 us
    pad x10, local copies, waits for them, and re-layouts, strided_taps(): padded = jnp.pad(field, padding)  127 us
    dot_general x49, matrix products, product(): return jnp.dot(left, right, preferred_element_type=jnp.float32)  104 us
    pad x6, local copies, waits for them, and re-layouts, strided_taps(): padded[row_tap:row_tap + 2 * out_count - 1:2, col_tap:col_tap + freq_widt...  86.2 us
    all_gather x12, blocking collectives, gather_rows(): return lax.all_gather(values, 'mp', axis=0, tiled=True)  82.5 us
  transfers between devices with their start and end apart: 19, of which 11 were waited for; matrix products, arithmetic and copies ran while one was open for 54% of the time, Pallas kernels for 0%

commit v1 on v0

v1 whole, which is shorter than its diff:
```python
import functools
import math

import jax
import jax.numpy as jnp
from jax import lax
from jax.experimental import pallas as pl
from jax.experimental.pallas import tpu as pltpu
from jax.sharding import PartitionSpec as P

D = 512
HEADS = 8
HEAD_DIM = 64
CHANNELS = 256
MEL = 80
KERNEL = 9
CLASSES = 1025
STEP = 7
LANES = 128
NPIECE = 4
F1, F2, F3 = MEL // 2, MEL // 4, MEL // 8
CPAD = 1152
HALO = 8
EDGE = 16

norm_eps = 1e-05
clip_norm = 0.005
beta_one = 0.9
beta_two = 0.98
adam_eps = 1e-08
decay_rate = 0.01
small_rates = (0.8, 0.15, 0.05, 0.1, 0.3)
f32 = jnp.float32
bf16 = jnp.bfloat16

SIZES = [27 * CHANNELS, 2 * CHANNELS * CHANNELS, CHANNELS * F3 * D, D * CLASSES, 23 * D]
NSMALL = sum(SIZES)
ROWS = [size // LANES for size in SIZES]
ROW_AT = [sum(ROWS[:k]) for k in range(5)]
NROWS = NSMALL // LANES


CORES, COLS, LINES = 2, 2, 2


def planned(n_dp, n_mp):
    return (n_dp, n_mp) == (8, 4)


def sent(x, name, by=1):
    axis, stride, size = {
        "c": ("mp", 1, 2),
        "x": ("mp", 2, 2),
        "y": ("dp", 1, 2),
        "z": ("dp", 2, lax.axis_size("dp") // 2),
    }[name]
    pairs = []
    for i in range(lax.axis_size(axis)):
        k = (i // stride) % size
        pairs.append((i, i + (((k + by) % size) - k) * stride))
    return lax.ppermute(x, axis, pairs)


def total(*parts):
    return functools.reduce(lambda a, b: a + b, [part.astype(f32) for part in parts])


def low_total(*parts):
    return total(*parts).astype(bf16)


class Reduced:
    def __init__(self, *parts):
        self.parts, self.deep = parts[:2], parts[0].shape[2]
        self.out = [parts[2], parts[3]]

    def cores(self):
        got = [sent(x, "c") for x in self.out]
        self.a, self.b = ([keep, more] for keep, more in zip(self.parts, got))
        self.out = [
            low_total(*[part[1] for part in self.a]),
            low_total(*[part[:, 1] for part in self.b]),
        ]
        return self.out

    def first(self):
        got_a, got_b = sent(self.out[0], "x"), sent(self.out[1], "y")
        self.a = [part[0] for part in self.a] + [got_a]
        self.b = [part[:, 0] for part in self.b] + [got_b]
        self.out = [
            low_total(*[part[1] for part in self.a]),
            low_total(*[part[1] for part in self.b]),
        ]
        return self.out

    def second(self):
        got_a, got_b = sent(self.out[0], "y"), sent(self.out[1], "x")
        self.a = [part[0] for part in self.a] + [got_a]
        self.b = [part[0] for part in self.b] + [got_b]
        self.out = [
            jnp.stack(
                [low_total(*[part[k] for part in self.a]), low_total(*[part[k] for part in self.b])]
            )
            for k in range(1, self.deep)
        ]
        return self.out

    def lines(self):
        got = [sent(x, "z", k + 1) for k, x in enumerate(self.out)]
        return [
            total(*[part[0] for part in side], *[x[k] for x in got])
            for k, side in enumerate((self.a, self.b))
        ]


class Gathered:
    def __init__(self, low):
        self.low = low

    def after(self, *others):
        (self.a, self.b), _ = lax.optimization_barrier(((self.a, self.b), others))
        return self

    def lines(self):
        lines, rows = lax.axis_size("dp") // LINES, self.low.shape[0] // 2
        parts = [self.low] + [sent(self.low, "z", lines - k) for k in range(1, lines)]
        self.a = jnp.stack([part[:rows] for part in parts])
        self.b = jnp.stack([part[rows:] for part in parts])
        return [self.a, self.b]

    def first(self):
        self.a = jnp.stack([self.a, sent(self.a, "x")])
        self.b = jnp.stack([self.b, sent(self.b, "y")])
        return [self.a, self.b]

    def second(self):
        both = [self.a, sent(self.a, "y")], [self.b, sent(self.b, "x")]
        both = jnp.stack([jnp.stack(side) for side in both])
        self.mine = both.reshape((2, -1) + both.shape[4:])
        return [self.mine]

    def cores(self):
        return [self.mine, sent(self.mine, "c")]


def reduced_whole(parts, own_rows):
    own = []
    for keep, send in zip(parts[:2], parts[2:]):
        both = jnp.stack([keep, send], 1)[:, :, 0, 0]
        both = both.reshape((lax.axis_size("mp"), lax.axis_size("dp"), -1, keep.shape[-1]))
        both = lax.psum_scatter(both, "mp", scatter_dimension=0, tiled=True)
        both = lax.psum_scatter(both, "dp", scatter_dimension=1, tiled=True)
        own.append(both.reshape(own_rows, keep.shape[-1]).astype(f32))
    return own


def spread(x):
    return lax.all_to_all(x, ("dp", "mp"), 0, 0, tiled=True)


def passed_along(x, by):
    peers = lax.axis_size("mp")
    pairs = [(i, i + by) for i in range(peers) if 0 <= i + by < peers]
    return lax.ppermute(x, "mp", pairs)


def call(kernel, outs, args, scratch=(), us=1, after=(), out_any=(), name=None):
    whole = pl.BlockSpec(memory_space=pltpu.VMEM)
    specs, arrays = [], []
    for arg in args:
        array, space = arg if isinstance(arg, tuple) else (arg, pltpu.VMEM)
        specs.append(pl.BlockSpec(memory_space=space))
        arrays.append(array)
    used = len(arrays)
    arrays += list(after)
    specs += [pl.BlockSpec(memory_space=pl.ANY)] * len(after)

    def run(*refs):
        kernel(*refs[:used], *refs[len(arrays) :])

    return pl.pallas_call(
        run,
        out_shape=[jax.ShapeDtypeStruct(shape, dtype) for shape, dtype in outs],
        in_specs=specs,
        out_specs=[pl.BlockSpec(memory_space=pl.ANY) if k in out_any else whole for k in range(len(outs))],
        scratch_shapes=list(scratch),
        compiler_params=pltpu.CompilerParams(vmem_limit_bytes=56 * 1024 * 1024),
        cost_estimate=pl.CostEstimate(
            flops=int(us * 1.15e9), bytes_accessed=int(us * 1e6), transcendentals=0
        ),
        name=name,
    )(*arrays)


def fetched(weights, which, lo, hi, buf, sem):
    copies = [
        pltpu.make_async_copy(weights.at[:, m, which, :, lo:hi], buf.at[m], sem.at[m])
        for m in range(buf.shape[0])
    ]
    for copy in copies:
        copy.start()
    return copies


def buffers(weights, *widths):
    deep, n_mp, _, rows, _ = weights.shape
    out = []
    for width in widths:
        out.append(pltpu.VMEM((n_mp, deep, rows, width), bf16))
        out.append(pltpu.SemaphoreType.DMA((n_mp,)))
    return out


def block(buf, m, lanes=slice(None)):
    part = buf[m, :, :, lanes]
    return part.reshape(part.shape[0] * part.shape[1], part.shape[2])


def aligned(at):
    return pl.ds(pl.multiple_of(at, LANES), LANES)


def pieces(spot):
    for c in range(CORES):
        for x in range(COLS):
            if spot is None:
                yield c, x, x * CORES + c
                continue
            yield c, x, ((spot[1] + x) % COLS) * CORES + (spot[0] + c) % CORES


def write_whole(to, half, m, grad):
    rows = to.shape[3]
    for k in range(to.shape[0]):
        to[k, m, half] = grad[rows * k : rows * k + rows].astype(bf16)


def write_piece(spot, parts, half, c, x, grad):
    to = parts[half + 2 * c]
    _, deep, lines, _, _ = to.shape
    rows = D // (lines * deep)
    grad = grad.astype(bf16)
    for z in range(lines):
        for y in range(deep):
            at = (z * deep + y) * rows
            to[x, (y + deep - spot[2]) % deep, (z + lines - spot[3]) % lines] = grad[at : at + rows]


def nn(left, right):
    return jnp.dot(left, right, preferred_element_type=f32)


def nt(left, right):
    return lax.dot_general(left, right, (((1,), (1,)), ((), ())), preferred_element_type=f32)


def tn(left, right):
    return lax.dot_general(left, right, (((0,), (0,)), ((), ())), preferred_element_type=f32)


def sigmoid(v):
    return 1.0 / (1.0 + jnp.exp(-v))


def layer_norm(x, gain, shift):
    centered = x - jnp.mean(x, -1, keepdims=True)
    rstd = lax.rsqrt(jnp.mean(centered * centered, -1, keepdims=True) + norm_eps)
    return centered * rstd * gain + shift


def layer_norm_back(x, gain, grad):
    centered = x - jnp.mean(x, -1, keepdims=True)
    rstd = lax.rsqrt(jnp.mean(centered * centered, -1, keepdims=True) + norm_eps)
    xhat = centered * rstd
    g = grad * gain
    dx = rstd * (
        g - jnp.mean(g, -1, keepdims=True) - xhat * jnp.mean(g * xhat, -1, keepdims=True)
    )
    return dx, jnp.sum(grad * xhat, 0, keepdims=True), jnp.sum(grad, 0, keepdims=True)


def eight(x):
    rows = x.shape[0] // 8
    return jnp.sum(x.reshape(rows, 8, x.shape[1]), 0)


def flip_matrix(size):
    at = lax.broadcasted_iota(jnp.int32, (size, size), 0)
    to = lax.broadcasted_iota(jnp.int32, (size, size), 1)
    return (at + to == size - 1).astype(bf16)


def first_row(shard, device):
    return lax.shift_left(lax.shift_right_logical(shard * device, 11), 4)


def rows_at(at, rows):
    return pl.ds(pl.multiple_of(at, 16), rows)


def piece_place(spot, c, half, q):
    i, j, z = q // 8, (q // 4) % 2, q % 4
    y, x = (j, i) if half else (i, j)
    dp = ((spot[3] + z) % 4) * LINES + (spot[2] + y) % LINES
    return dp, ((spot[1] + x) % COLS) * CORES + (spot[0] + c) % CORES


def unpack_kernel(
    shard, spot, mine_ref, other_ref, taps_ref, one_ref, pw_ref, lin_ref, head_ref, vec_ref, flat
):
    flat[...] = jnp.zeros_like(flat)
    rows = mine_ref.shape[2]
    for c, ref in enumerate((mine_ref, other_ref)):
        for half in range(2):

            def step(q, carry, c=c, ref=ref, half=half):
                dp, mp = piece_place(spot, c, half, q)
                at = first_row(shard, dp * (COLS * CORES) + mp) + rows * half
                flat[rows_at(at, rows), :] += ref[half, q].astype(f32)
                return carry

            lax.fori_loop(0, ref.shape[1], step, 0)
    unpack_flat(flat, taps_ref, one_ref, pw_ref, lin_ref, head_ref, vec_ref)


def unpack_whole_kernel(
    shard, all_ref, taps_ref, one_ref, pw_ref, lin_ref, head_ref, vec_ref, flat
):
    flat[...] = jnp.zeros_like(flat)
    rows = all_ref.shape[1]

    def step(device, carry):
        flat[rows_at(first_row(shard, device), rows), :] += all_ref[device].astype(f32)
        return carry

    lax.fori_loop(0, all_ref.shape[0], step, 0)
    unpack_flat(flat, taps_ref, one_ref, pw_ref, lin_ref, head_ref, vec_ref)


def unpack_flat(flat, taps_ref, one_ref, pw_ref, lin_ref, head_ref, vec_ref):
    one_ref[...] = jnp.zeros_like(one_ref)
    taps_ref[...] = jnp.zeros_like(taps_ref)
    vec_ref[...] = jnp.zeros_like(vec_ref)
    for h in range(2):
        lanes = slice(LANES * h, LANES * h + LANES)
        taps = flat[pl.ds(h, 27, stride=2), :]
        taps_ref[0:27, lanes] = taps
        padded = jnp.concatenate([taps[0:9], jnp.zeros((7, LANES), f32)], 0).astype(bf16)
        for k in range(8):
            one_ref[k, 16 * k : 16 * k + 16, lanes] = padded
        for k in range(2):
            part = flat[pl.ds(ROW_AT[1] + 512 * k + h, CHANNELS, stride=2), :]
            pw_ref[k, :, lanes] = part.astype(bf16)
    for j in range(4):
        lanes = slice(LANES * j, LANES * j + LANES)
        for f in range(F3):
            part = flat[pl.ds(ROW_AT[2] + 1024 * f + j, CHANNELS, stride=4), :]
            lin_ref[f, :, lanes] = part.astype(bf16)
        vec_ref[0:23, lanes] = flat[pl.ds(ROW_AT[4] + j, 23, stride=4), :]
    flip = flip_matrix(LANES)
    column = lax.broadcasted_iota(jnp.int32, (LANES, CPAD), 1)
    for q in range(D // LANES):
        at = ROW_AT[3] + 1025 * q
        wide = jnp.concatenate(
            [flat[pl.ds(at + c, LANES, stride=8), :] for c in range(CPAD // LANES)], 1
        )
        turned = nn(flip, wide.astype(bf16))
        turned = pltpu.roll(turned, CPAD - LANES + 1, 1, stride=1, stride_axis=0)
        turned = jnp.where(column < CLASSES, turned, 0.0)
        head_ref[LANES * q : LANES * q + LANES, :] = nn(flip, turned.astype(bf16)).astype(bf16)


def pack_kernel(shard, n_dp, spot, last_ref, dx_ref, dhead_ref, *refs):
    parts, flat = refs[:4], refs[4]
    dx = dx_ref[...]
    flat[0 : ROW_AT[2], :] = jnp.zeros((ROW_AT[2], LANES), f32)
    flat[ROW_AT[4] :, :] = jnp.zeros((flat.shape[0] - ROW_AT[4], LANES), f32)
    for f in range(F3):
        grad = tn(last_ref[f], dx)
        for j in range(4):
            flat[pl.ds(ROW_AT[2] + 1024 * f + j, CHANNELS, stride=4), :] = grad[
                :, LANES * j : LANES * j + LANES
            ]
    for q in range(D // LANES):
        at = ROW_AT[3] + 1025 * q
        turned = pltpu.roll(
            dhead_ref[LANES * q : LANES * q + LANES, :], 0, 1, stride=1, stride_axis=0
        )
        flat[pl.ds(at + 8, LANES, stride=8), :] = turned[:, 8 * LANES :]
        flat[at : at + 1, :] = turned[0:1, 0:LANES]
        flat[pl.ds(at + 8, LANES - 1, stride=8), :] += turned[1:, 0:LANES]
        for c in range(1, 8):
            flat[pl.ds(at + c, LANES, stride=8), :] = turned[:, LANES * c : LANES * c + LANES]
    _, deep, lines, rows, _ = parts[0].shape
    each = n_dp // (deep * lines)
    rows = rows // each
    for c in range(CORES):

        def step(q, carry, c=c):
            k = q % each
            z, y, x = (q // each) % lines, (q // (each * lines)) % deep, q // (each * lines * deep)
            mp = ((spot[1] + x) % COLS) * CORES + (spot[0] + c) % CORES
            dp = ((spot[3] + z) % lines) * deep + (spot[2] + y) % deep + k
            row = first_row(shard, dp * (COLS * CORES) + mp)
            for half in range(2):
                part = flat[rows_at(row + rows * half, rows), :]
                parts[half + 2 * c][x, y, z, rows_at(rows * k, rows), :] = part.astype(bf16)
            return carry

        lax.fori_loop(0, COLS * deep * lines * each, step, 0)


def stem_chunks(rows):
    for lane in range(0, CHANNELS, LANES):
        for at in range(0, rows, 48):
            yield slice(lane, lane + LANES), at


def stem_scratch(rows):
    return [
        pltpu.VMEM((5, 4 * rows, CHANNELS), f32),
        pltpu.VMEM((F2, 2 * rows, CHANNELS), f32),
        pltpu.VMEM((rows + 8, CHANNELS), f32),
        pltpu.VMEM((rows - EDGE, F3 * CHANNELS), bf16),
        pltpu.VMEM((F3, CHANNELS, D), bf16),
        pltpu.VMEM((F2, 2 * rows, CHANNELS), bf16),
        pltpu.SemaphoreType.DMA((2,)),
    ]


def first_rows(win_ref, one_ref, f):
    return jax.nn.relu(nn(win_ref[f // 8], one_ref[f % 8]))


def staged(sources, targets, sem):
    copies = [pltpu.make_async_copy(s, t, sem.at[k]) for k, (s, t) in enumerate(zip(sources, targets))]
    for copy in copies:
        copy.start()
    return copies


def stem_kernel(
    win_ref,
    one_ref,
    taps_ref,
    pw_ref,
    lin_hbm,
    x0_ref,
    front_hbm,
    mid_ref,
    last_ref,
    t_ref,
    r_ref,
    lag_ref,
    flat,
    lin_ref,
    front_ref,
    sem,
):
    rows = lag_ref.shape[0] - 8
    (lin_copy,) = staged([lin_hbm], [lin_ref], sem.at[pl.ds(0, 1)])
    lag_ref[0:8, :] = jnp.zeros((8, CHANNELS), f32)
    t_ref[4] = jnp.zeros_like(t_ref[4])

    def second(slots, to):
        for lanes, at in stem_chunks(rows):

            def tap(k):
                return taps_ref[k : k + 1, lanes]

            lag, even, odd = 0.0, 0.0, 0.0
            for df, slot in enumerate(slots):
                t0, t1, t2, t3 = (
                    t_ref[slot, a * rows + at : a * rows + at + 48, lanes] for a in range(4)
                )
                lag += t3 * tap(9 + df)
                even += t0 * tap(12 + df) + t1 * tap(15 + df)
                odd += t1 * tap(9 + df) + t2 * tap(12 + df) + t3 * tap(15 + df)
            lag_ref[8 + at : 56 + at, lanes] = lag
            even += lag_ref[7 + at : 55 + at, lanes]
            front_ref[to, at : at + 48, lanes] = even.astype(bf16)
            front_ref[to, rows + at : rows + at + 48, lanes] = odd.astype(bf16)

    def step_front(f, carry):
        for k in range(4):
            t_ref[k] = first_rows(win_ref, one_ref, 4 * f + k)
        second((4, 0, 1), 2 * f)
        second((1, 2, 3), 2 * f + 1)
        t_ref[4] = t_ref[3]
        return carry

    lax.fori_loop(0, F3, step_front, 0)

    def step_point(f, carry):
        for k in range(4):
            r_ref[4 * f + k] = jax.nn.relu(nn(front_ref[4 * f + k], pw_ref[0]))
        return carry

    lax.fori_loop(0, F2 // 4, step_point, 0)

    front_copy = pltpu.make_async_copy(front_ref, front_hbm, sem.at[1])
    front_copy.start()

    def third(f, whole):
        for lanes, at in stem_chunks(rows):

            def tap(k):
                return taps_ref[k : k + 1, lanes]

            lag, out = 0.0, 0.0
            for df in range(0 if whole else 1, 3):
                slot = 2 * f - 1 + df
                even = r_ref[slot, at : at + 48, lanes]
                odd = r_ref[slot, rows + at : rows + at + 48, lanes]
                lag += odd * tap(18 + df)
                out += even * tap(21 + df) + odd * tap(24 + df)
            lag_ref[8 + at : 56 + at, lanes] = lag
            out += lag_ref[7 + at : 55 + at, lanes]
            skip = max(0, EDGE - at)
            mid_ref[f, at + skip - EDGE : at + 48 - EDGE, lanes] = out[skip:].astype(bf16)

    third(0, False)

    def step_mid(f, carry):
        third(f, True)
        return carry

    lax.fori_loop(1, F3, step_mid, 0)
    for f in range(F3):
        last = jax.nn.relu(nn(mid_ref[f], pw_ref[1])).astype(bf16)
        last_ref[f] = last
        flat[:, CHANNELS * f : CHANNELS * f + CHANNELS] = last
    lin_copy.wait()
    x0_ref[...] = nn(flat[...], lin_ref[...].reshape(F3 * CHANNELS, D))
    front_copy.wait()


def back_scratch(rows):
    return [
        pltpu.VMEM((F3, rows - EDGE, CHANNELS), bf16),
        pltpu.VMEM((F3 + 1, rows + 8, CHANNELS), f32),
        pltpu.VMEM((F2 + 1, 3 * rows, CHANNELS), f32),
        pltpu.VMEM((F2, 2 * rows, CHANNELS), f32),
        pltpu.VMEM((F2, 2 * rows, CHANNELS), bf16),
        pltpu.VMEM((2, 4 * rows, CHANNELS), f32),
        pltpu.VMEM((F2, 8 * rows, CHANNELS), bf16),
        pltpu.VMEM((F3, CHANNELS, D), bf16),
        pltpu.VMEM((F3, rows - EDGE, CHANNELS), bf16),
        pltpu.VMEM((F3, rows - EDGE, CHANNELS), bf16),
        pltpu.VMEM((F2, 2 * rows, CHANNELS), bf16),
        pltpu.VMEM((F1 // 8, 4 * rows, LANES), bf16),
        pltpu.VMEM((16, F2 * 8 * rows), bf16),
        pltpu.SemaphoreType.DMA((6,)),
    ]


def stem_back_kernel(
    dx_ref,
    win_hbm,
    turn_hbm,
    one_ref,
    taps_ref,
    pw_ref,
    lin_hbm,
    front_hbm,
    mid_hbm,
    last_hbm,
    g_pw,
    sums,
    g_one,
    g_last,
    g_mid,
    g_front,
    p_ref,
    q_ref,
    t_ref,
    s_ref,
    lin_ref,
    last_ref,
    mid_ref,
    front_ref,
    win_ref,
    turn_ref,
    sem,
):
    copies = staged(
        [lin_hbm, last_hbm, mid_hbm, front_hbm, win_hbm, turn_hbm],
        [lin_ref, last_ref, mid_ref, front_ref, win_ref, turn_ref],
        sem,
    )
    rows = g_mid.shape[1] - 8
    tokens = rows - EDGE
    sums[...] = jnp.zeros_like(sums)
    g_one[...] = jnp.zeros_like(g_one)
    g_mid[:, 0:EDGE, :] = jnp.zeros((F3 + 1, EDGE, CHANNELS), f32)
    g_mid[:, rows:, :] = jnp.zeros((F3 + 1, 8, CHANNELS), f32)
    g_mid[F3] = jnp.zeros_like(g_mid[F3])
    g_front[F2] = jnp.zeros_like(g_front[F2])
    dx = dx_ref[...]
    copies[0].wait()
    copies[1].wait()
    for f in range(F3):
        grad = nt(dx, lin_ref[f])
        grad = jnp.where(last_ref[f].astype(f32) > 0, grad, 0.0).astype(bf16)
        g_last[f] = grad
    for f in range(F3):
        g_mid[f, EDGE:rows, :] = nt(g_last[f], pw_ref[1])
    whole = (F3 * tokens, CHANNELS)
    copies[2].wait()
    g_pw[1] = tn(mid_ref[...].reshape(whole), g_last[...].reshape(whole))

    copies[3].wait()

    def step_point(f, carry):
        for k in range(4):
            p_ref[4 * f + k] = jax.nn.relu(nn(front_ref[4 * f + k], pw_ref[0]))
        return carry

    lax.fori_loop(0, F2 // 4, step_point, 0)

    def step_mid(f, carry):
        for odd in range(2):
            uses = [(f, 2), (f + 1, 0)] if odd else [(f, 1)]
            here = 2 * f + odd
            for lane in range(0, CHANNELS, LANES):
                lanes = slice(lane, lane + LANES)

                def tap(k):
                    return taps_ref[k : k + 1, lanes]

                found = {}
                for at in range(0, rows, 48):
                    p_even = p_ref[here, at : at + 48, lanes]
                    p_odd = p_ref[here, rows + at : rows + at + 48, lanes]
                    d_even, d_odd = 0.0, 0.0
                    for which, df in uses:
                        g = g_mid[which, at : at + 48, lanes]
                        g_up = g_mid[which, at + 1 : at + 49, lanes]
                        d_even += g * tap(21 + df)
                        d_odd += g * tap(24 + df) + g_up * tap(18 + df)
                        for k, x in ((df, g_up * p_odd), (3 + df, g * p_even), (6 + df, g * p_odd)):
                            found[k] = found.get(k, 0.0) + eight(x)
                    q_ref[here, at : at + 48, lanes] = jnp.where(p_even > 0, d_even, 0.0).astype(bf16)
                    q_ref[here, rows + at : rows + at + 48, lanes] = jnp.where(
                        p_odd > 0, d_odd, 0.0
                    ).astype(bf16)
                for k, x in found.items():
                    sums[9 + k, :, lanes] += x
        return carry

    lax.fori_loop(0, F3, step_mid, 0)

    def step_back(f, carry):
        for k in range(4):
            grad = nt(q_ref[4 * f + k], pw_ref[0])
            g_front[4 * f + k, 0 : 2 * rows, :] = grad
            g_front[4 * f + k, 2 * rows :, :] = pltpu.roll(grad[:rows], rows - 1, 0)
        size = (8 * rows, CHANNELS)
        grad = tn(front_ref[pl.ds(4 * f, 4)].reshape(size), q_ref[pl.ds(4 * f, 4)].reshape(size))
        g_pw[0] = jnp.where(f == 0, grad, g_pw[0] + grad)
        return carry

    lax.fori_loop(0, F2 // 4, step_back, 0)

    copies[4].wait()
    copies[5].wait()

    def step_front(f, carry):
        for odd in range(2):
            t_ref[odd] = first_rows(win_ref, one_ref, 2 * f + odd)
        for odd in range(2):
            uses = [(f, 2), (f + 1, 0)] if odd else [(f, 1)]
            for lane in range(0, CHANNELS, LANES):
                lanes = slice(lane, lane + LANES)

                def tap(k):
                    return taps_ref[k : k + 1, lanes]

                found = {}
                for at in range(0, rows, 48):
                    t0, t1, t2, t3 = (
                        t_ref[odd, a * rows + at : a * rows + at + 48, lanes] for a in range(4)
                    )
                    d = [0.0] * 4
                    for which, df in uses:
                        e = g_front[which, at : at + 48, lanes]
                        o = g_front[which, rows + at : rows + at + 48, lanes]
                        e_up = g_front[which, 2 * rows + at : 2 * rows + at + 48, lanes]
                        d[0] += e * tap(12 + df)
                        d[1] += e * tap(15 + df) + o * tap(9 + df)
                        d[2] += o * tap(12 + df)
                        d[3] += o * tap(15 + df) + e_up * tap(9 + df)
                        for k, x in (
                            (df, t1 * o + t3 * e_up),
                            (3 + df, t0 * e + t2 * o),
                            (6 + df, t1 * e + t3 * o),
                        ):
                            found[k] = found.get(k, 0.0) + eight(x)
                    for a, (t, grad) in enumerate(zip((t0, t1, t2, t3), d)):
                        to = (4 * odd + a) * rows + at
                        s_ref[f, to : to + 48, lanes] = jnp.where(t > 0, grad, 0.0).astype(bf16)
                for k, x in found.items():
                    sums[k, :, lanes] += x

        return carry

    lax.fori_loop(0, F2, step_front, 0)
    part = F2 // 4
    for k in range(4):
        at = part * 8 * rows
        g_one[...] += nn(
            turn_ref[:, k * at : (k + 1) * at],
            s_ref[part * k : part * (k + 1)].reshape(at, CHANNELS),
        )


def stem_rows_kernel(
    g_pw, sums, g_one, vg_last, vg_conv, vg_mid, vg_att, out_ref, flat
):
    taps = jnp.concatenate(
        [g_one[0:9, :]]
        + [jnp.sum(sums[k], 0, keepdims=True) for k in range(18)],
        0,
    )
    order = [
        (vg_last, 2),
        (vg_last, 0),
        (vg_conv, 0),
        (vg_mid, 2),
        (vg_mid, 0),
        (vg_last, 3),
        (vg_last, 1),
        (vg_conv, 1),
        (vg_mid, 3),
        (vg_mid, 1),
        (vg_mid, 4),
        (vg_mid, 5),
        (vg_att, 0),
        (vg_att, 1),
    ] + [(vg_conv, k) for k in range(2, 11)]
    flat[ROW_AT[2] + ROWS[4] - 8 :, :] = jnp.zeros((flat.shape[0] - ROW_AT[2] - ROWS[4] + 8, LANES), f32)
    for h in range(2):
        lanes = slice(LANES * h, LANES * h + LANES)
        flat[pl.ds(h, 27, stride=2), :] = taps[:, lanes]
        for k in range(2):
            flat[pl.ds(ROW_AT[1] + 512 * k + h, CHANNELS, stride=2), :] = g_pw[k, :, lanes]
    for k, (ref, row) in enumerate(order):
        for j in range(4):
            at = ROW_AT[2] + 4 * k + j
            flat[at : at + 1, :] = ref[row : row + 1, LANES * j : LANES * j + LANES]
    out_ref[...] = flat[...].astype(bf16)


def ffn_forward(x, vec_ref, which, win, wout, pre_ref, normed_ref):
    normed = layer_norm(x, vec_ref[which : which + 1, :], vec_ref[which + 5 : which + 6, :])
    normed = normed.astype(bf16)
    normed_ref[...] = normed
    total = jnp.zeros_like(x)
    (in_copies, in_buf), (out_copies, out_buf) = win, wout
    for m in range(NPIECE):
        in_copies[m].wait()
        pre = nn(normed, block(in_buf, m))
        pre_ref[m] = pre
        out_copies[m].wait()
        total += nt((pre * sigmoid(pre)).astype(bf16), block(out_buf, m))
    return x + 0.5 * total


def ffn_backward(spot, grad, x, vec_ref, which, in_buf, out_buf, pre_ref, normed_ref, parts):
    low = (0.5 * grad).astype(bf16)
    back = jnp.zeros_like(x)
    for c, col, m in pieces(spot):

        def write(half, piece):
            if spot is None:
                write_whole(parts, half, m, piece)
            else:
                write_piece(spot, parts, half, c, col, piece)

        pre = pre_ref[m]
        sig = sigmoid(pre)
        write(1, tn(low, (pre * sig).astype(bf16)))
        g_pre = (nn(low, block(out_buf, m)) * (sig * (1.0 + pre * (1.0 - sig)))).astype(bf16)
        write(0, tn(normed_ref[...], g_pre))
        back += nt(g_pre, block(in_buf, m))
    dx, gain, shift = layer_norm_back(x, vec_ref[which : which + 1, :], back)
    return grad + dx, gain, shift


def first_kernel(
    weights,
    x_ref,
    vec_ref,
    x1_ref,
    pre_ref,
    n1_ref,
    n2_ref,
    in_buf,
    in_sem,
    out_buf,
    out_sem,
):
    win = fetched(weights, 0, 0, D, in_buf, in_sem)
    wout = fetched(weights, 1, 0, D, out_buf, out_sem)
    x1 = ffn_forward(x_ref[...], vec_ref, 0, (win, in_buf), (wout, out_buf), pre_ref, n1_ref)
    x1_ref[...] = x1
    n2_ref[...] = layer_norm(x1, vec_ref[1:2, :], vec_ref[6:7, :]).astype(bf16)


def position_kernel(
    weights, table_ref, n2_ref, vec_ref, pe_ref, qu_ref, qv_ref, buf, sem, q_buf, q_sem
):
    q_copies = fetched(weights, 2, 0, LANES, q_buf, q_sem)
    copies = fetched(weights, 2, 3 * LANES, 4 * LANES, buf, sem)
    for m in range(NPIECE):
        lanes = slice(LANES * m, LANES * m + LANES)
        q_copies[m].wait()
        query = nn(n2_ref[...], block(q_buf, m))
        qu_ref[:, lanes] = (query + vec_ref[12:13, lanes]).astype(bf16)
        qv_ref[:, lanes] = (query + vec_ref[13:14, lanes]).astype(bf16)
        copies[m].wait()
        pe_ref[:, lanes] = nn(table_ref[...], block(buf, m)).astype(bf16)


def head_lanes(h):
    return h // 2, HEAD_DIM * (h % 2), slice(HEAD_DIM * h, HEAD_DIM * h + HEAD_DIM)


def attention_kernel(
    weights,
    all_ref,
    x1_ref,
    qu_ref,
    qv_ref,
    pe_ref,
    vec_ref,
    keep_ref,
    valid_ref,
    x2_ref,
    kv_ref,
    prob_ref,
    att_ref,
    n3_ref,
    ga_ref,
    gb_ref,
    gated_ref,
    low_ref,
    high_ref,
    kv_buf,
    kv_sem,
    abo_buf,
    abo_sem,
):
    kv_copies = fetched(weights, 2, LANES, 3 * LANES, kv_buf, kv_sem)
    abo_copies = fetched(weights, 3, 0, 3 * LANES, abo_buf, abo_sem)
    rows, length = x1_ref.shape[0], all_ref.shape[0]
    width = rows + length
    for m in range(NPIECE):
        kv_copies[m].wait()
        kv_ref[m] = nn(all_ref[...], block(kv_buf, m)).astype(bf16)
    keep = keep_ref[...] > 0
    for h in range(HEADS):
        m, at, lanes = head_lanes(h)
        raw = nt(qu_ref[:, lanes], kv_ref[m, :, at : at + HEAD_DIM])
        far = nt(qv_ref[:, lanes], pe_ref[:, lanes])
        far = pltpu.roll(far, width - rows + 1, 1, stride=1, stride_axis=0)
        scores = jnp.where(keep, (raw + far[:, :length]) * 0.125, -1e30)
        expo = jnp.exp(scores - jnp.max(scores, -1, keepdims=True))
        prob = expo / jnp.sum(expo, -1, keepdims=True)
        prob_ref[h] = prob
        value = kv_ref[m, :, LANES + at : LANES + at + HEAD_DIM]
        att_ref[:, lanes] = nn(prob.astype(bf16), value).astype(bf16)
    x2 = x1_ref[...]
    for m in range(NPIECE):
        abo_copies[m].wait()
        lanes = slice(LANES * m, LANES * m + LANES)
        x2 += nt(att_ref[:, lanes], block(abo_buf, m, slice(2 * LANES, 3 * LANES)))
    x2_ref[...] = x2
    normed = layer_norm(x2, vec_ref[2:3, :], vec_ref[7:8, :]).astype(bf16)
    n3_ref[...] = normed
    for m in range(NPIECE):
        lanes = slice(LANES * m, LANES * m + LANES)
        gates = nn(normed, block(abo_buf, m, slice(0, 2 * LANES)))
        ga, gb = gates[:, :LANES], gates[:, LANES:]
        ga_ref[:, lanes] = ga
        gb_ref[:, lanes] = gb
        gated_ref[:, lanes] = ga * sigmoid(gb) * valid_ref[...]
    low_ref[...] = gated_ref[0:HALO, :]
    high_ref[...] = gated_ref[rows - HALO :, :]


def write_stats(stat_ref, first, second, number):
    rows = [x[:, LANES * k : LANES * k + LANES] for x in (first, second) for k in range(4)]
    rows.append(jnp.broadcast_to(number, (8, LANES)))
    stat_ref[...] = jnp.broadcast_to(jnp.concatenate(rows, 0)[None], stat_ref.shape)


def read_stats(stat_ref):
    whole = jnp.sum(stat_ref[...], 0)
    first = jnp.concatenate([whole[k : k + 1] for k in range(4)], 1)
    second = jnp.concatenate([whole[k : k + 1] for k in range(4, 8)], 1)
    return first, second, whole[8:9, 0:1]


def conv_kernel(prev_ref, gated_ref, next_ref, vec_ref, valid_ref, hidden_ref, stat_ref, wide):
    rows = gated_ref.shape[0]
    wide[0:HALO, :] = prev_ref[...]
    wide[HALO : HALO + rows, :] = gated_ref[...]
    wide[HALO + rows :, :] = next_ref[...]
    at = HALO - KERNEL // 2
    hidden = sum(wide[at + k : at + k + rows, :] * vec_ref[14 + k : 15 + k, :] for k in range(KERNEL))
    hidden_ref[...] = hidden
    valid = valid_ref[...]
    kept = hidden * valid
    write_stats(
        stat_ref,
        jnp.sum(kept, 0, keepdims=True),
        jnp.sum(kept * hidden, 0, keepdims=True),
        jnp.sum(valid, 0, keepdims=True),
    )


def middle_kernel(
    weights,
    more,
    hidden_ref,
    stat_ref,
    x2_ref,
    head_ref,
    vec_ref,
    label_ref,
    weight_ref,
    valid_ref,
    grad_ref,
    g_head_ref,
    dx3_ref,
    act_ref,
    dy_ref,
    yhat_ref,
    low_ref,
    high_ref,
    part_ref,
    vgrad_ref,
    pre_ref,
    n4_ref,
    c_buf,
    c_sem,
    in_buf,
    in_sem,
    out_buf,
    out_sem,
):
    c_copies = fetched(weights, 3, 3 * LANES, 4 * LANES, c_buf, c_sem)
    win = fetched(more, 0, 0, D, in_buf, in_sem), in_buf
    wout = fetched(more, 1, 0, D, out_buf, out_sem), out_buf
    rows = x2_ref.shape[0]
    first, second, count = read_stats(stat_ref)
    mean = first / count
    inverse = lax.rsqrt(second / count - mean * mean + norm_eps)
    yhat = (hidden_ref[...] - mean) * inverse
    yhat_ref[...] = yhat
    c = yhat * vec_ref[10:11, :] + vec_ref[11:12, :]
    sig = sigmoid(c)
    act = (c * sig).astype(bf16)
    act_ref[...] = act
    x3 = x2_ref[...]
    for m in range(NPIECE):
        c_copies[m].wait()
        x3 += nt(act[:, LANES * m : LANES * m + LANES], block(c_buf, m))
    x4 = ffn_forward(x3, vec_ref, 3, win, wout, pre_ref, n4_ref)
    normed = layer_norm(x4, vec_ref[4:5, :], vec_ref[9:10, :]).astype(bf16)
    logits = nn(normed, head_ref[...])
    column = lax.broadcasted_iota(jnp.int32, logits.shape, 1)
    logits = jnp.where(column < CLASSES, logits, -1e30)
    top = jnp.max(logits, -1, keepdims=True)
    total = top + jnp.log(jnp.sum(jnp.exp(logits - top), -1, keepdims=True))
    hit = column == label_ref[...]
    picked = jnp.sum(jnp.where(hit, logits, 0.0), -1, keepdims=True)
    weight = weight_ref[...]
    loss = jnp.sum(weight * (total - picked), 0, keepdims=True)
    g_logits = (jnp.exp(logits - total) - hit.astype(f32)) * (weight / count)
    g_logits = g_logits.astype(bf16)
    g_head_ref[...] = tn(normed, g_logits)
    dx4, gain, shift = layer_norm_back(x4, vec_ref[4:5, :], nt(g_logits, head_ref[...]))
    vgrad_ref[0:1, :] = gain
    vgrad_ref[1:2, :] = shift
    dx3, gain, shift = ffn_backward(
        None, dx4, x3, vec_ref, 3, in_buf, out_buf, pre_ref, n4_ref, grad_ref
    )
    vgrad_ref[2:3, :] = gain
    vgrad_ref[3:4, :] = shift
    dx3_ref[...] = dx3
    low = dx3.astype(bf16)
    valid = valid_ref[...]
    parts = []
    for m in range(NPIECE):
        lanes = slice(LANES * m, LANES * m + LANES)
        slope = sig[:, lanes] * (1.0 + c[:, lanes] * (1.0 - sig[:, lanes]))
        dc = nn(low, block(c_buf, m)) * slope
        vgrad_ref[4:5, lanes] = jnp.sum(dc * yhat[:, lanes], 0, keepdims=True)
        vgrad_ref[5:6, lanes] = jnp.sum(dc, 0, keepdims=True)
        dy = dc * vec_ref[10:11, lanes]
        dy_ref[:, lanes] = dy
        kept = dy * valid
        parts.append(
            (
                jnp.sum(kept, 0, keepdims=True),
                jnp.sum(kept * yhat[:, lanes], 0, keepdims=True),
            )
        )
    for k, ref in enumerate((dy_ref, yhat_ref)):
        low_ref[HALO * k : HALO * k + HALO, :] = ref[0:HALO, :]
        high_ref[HALO * k : HALO * k + HALO, :] = ref[rows - HALO :, :]
    write_stats(
        part_ref,
        jnp.concatenate([a for a, _ in parts], 1),
        jnp.concatenate([b for _, b in parts], 1),
        loss,
    )


def conv_back_kernel(
    weights,
    dy_ref,
    yhat_ref,
    prev_ref,
    next_ref,
    part_ref,
    stat_ref,
    wide_valid_ref,
    gprev_ref,
    gated_ref,
    gnext_ref,
    ga_ref,
    gb_ref,
    x2_ref,
    dx3_ref,
    vec_ref,
    dgate_ref,
    dx2_ref,
    vgrad_ref,
    loss_ref,
    wide,
    wide_y,
    dh,
    buf,
    sem,
):
    copies = fetched(weights, 3, 0, 2 * LANES, buf, sem)
    rows = dy_ref.shape[0]
    first, second, count = read_stats(stat_ref)
    mean = first / count
    inverse = lax.rsqrt(second / count - mean * mean + norm_eps)
    first, second, loss = read_stats(part_ref)
    loss_ref[...] = loss / count
    wide[0:HALO, :] = prev_ref[0:HALO, :]
    wide[HALO : HALO + rows, :] = dy_ref[...]
    wide[HALO + rows :, :] = next_ref[0:HALO, :]
    wide_y[0:HALO, :] = prev_ref[HALO:, :]
    wide_y[HALO : HALO + rows, :] = yhat_ref[...]
    wide_y[HALO + rows :, :] = next_ref[HALO:, :]
    mean_part = (first + wide_y[...] * second) / count
    dh[...] = inverse * (wide[...] - wide_valid_ref[...] * mean_part)
    wide[0:HALO, :] = gprev_ref[...]
    wide[HALO : HALO + rows, :] = gated_ref[...]
    wide[HALO + rows :, :] = gnext_ref[...]
    half = KERNEL // 2
    own = dh[HALO : HALO + rows, :]
    d_gated = jnp.zeros((rows, D), f32)
    for k in range(KERNEL):
        d_gated += dh[HALO - k + half : HALO - k + half + rows, :] * vec_ref[14 + k : 15 + k, :]
        at = HALO + k - half
        vgrad_ref[2 + k : 3 + k, :] = jnp.sum(own * wide[at : at + rows, :], 0, keepdims=True)
    d_gated = d_gated * wide_valid_ref[HALO : HALO + rows, :]
    sig = sigmoid(gb_ref[...])
    dga = (d_gated * sig).astype(bf16)
    dgb = (d_gated * ga_ref[...] * sig * (1.0 - sig)).astype(bf16)
    back = jnp.zeros((rows, D), f32)
    for m in range(NPIECE):
        lanes = slice(LANES * m, LANES * m + LANES)
        both = jnp.concatenate([dga[:, lanes], dgb[:, lanes]], 1)
        dgate_ref[m] = both
        copies[m].wait()
        back += nt(both, block(buf, m))
    dx, gain, shift = layer_norm_back(x2_ref[...], vec_ref[2:3, :], back)
    vgrad_ref[0:1, :] = gain
    vgrad_ref[1:2, :] = shift
    dx2_ref[...] = dx3_ref[...] + dx


def back_kernel(
    weights,
    dx2_ref,
    prob_ref,
    kv_ref,
    qu_ref,
    qv_ref,
    pe_ref,
    dquery_ref,
    dkv_ref,
    dpe_ref,
    dall_ref,
    down_ref,
    vgrad_ref,
    dq,
    o_buf,
    o_sem,
    mix_buf,
    mix_sem,
):
    o_copies = fetched(weights, 3, 2 * LANES, 3 * LANES, o_buf, o_sem)
    mix_copies = fetched(weights, 2, 0, 3 * LANES, mix_buf, mix_sem)
    rows, length = dx2_ref.shape[0], dall_ref.shape[0]
    low = dx2_ref[...].astype(bf16)
    flip = flip_matrix(rows)
    turned_q = nn(flip, qv_ref[...]).astype(bf16)
    for h in range(HEADS):
        m, at, lanes = head_lanes(h)
        if at == 0:
            o_copies[m].wait()
            d_att = nn(low, block(o_buf, m)).astype(bf16)
        d_out = d_att[:, at : at + HEAD_DIM]
        prob = prob_ref[h]
        key = kv_ref[m, :, at : at + HEAD_DIM]
        value = kv_ref[m, :, LANES + at : LANES + at + HEAD_DIM]
        d_prob = nt(d_out, value)
        d_scores = prob * (d_prob - jnp.sum(prob * d_prob, -1, keepdims=True))
        d_raw = (d_scores * 0.125).astype(bf16)
        dkv_ref[m, :, LANES + at : LANES + at + HEAD_DIM] = tn(prob.astype(bf16), d_out).astype(bf16)
        dkv_ref[m, :, at : at + HEAD_DIM] = tn(d_raw, qu_ref[:, lanes]).astype(bf16)
        dq[0:rows, lanes] = nn(d_raw, key)
        turned = nn(flip, d_raw)
        turned = jnp.concatenate([turned, jnp.zeros((rows, rows), f32)], 1)
        turned = pltpu.roll(turned, 0, 1, stride=1, stride_axis=0).astype(bf16)
        dq[rows : 2 * rows, lanes] = nn(turned, pe_ref[:, lanes])
        dpe_ref[:, lanes] = tn(turned, turned_q[:, lanes]).astype(bf16)
    d_u, d_v = dq[0:rows, :], dq[rows : 2 * rows, :]
    vgrad_ref[0:1, :] = jnp.sum(d_u, 0, keepdims=True)
    vgrad_ref[1:2, :] = jnp.sum(d_v, 0, keepdims=True)
    straight = jnp.dot(
        flip.astype(f32), d_v, precision=lax.Precision.HIGHEST, preferred_element_type=f32
    )
    dquery = (d_u + straight).astype(bf16)
    dquery_ref[...] = dquery
    d_all = jnp.zeros((length, D), f32)
    d_own = jnp.zeros((rows, D), f32)
    for m in range(NPIECE):
        mix_copies[m].wait()
        d_own += nt(dquery[:, LANES * m : LANES * m + LANES], block(mix_buf, m, slice(0, LANES)))
        d_all += nt(dkv_ref[m], block(mix_buf, m, slice(LANES, 3 * LANES)))
    dall_ref[...] = d_all.astype(bf16)
    down_ref[...] = d_own


def mix_grad_kernel(
    spot,
    dx2_ref,
    dx3_ref,
    dgate_ref,
    n3_ref,
    act_ref,
    att_ref,
    n2_ref,
    all_ref,
    table_ref,
    dquery_ref,
    dkv_ref,
    dpe_ref,
    *parts,
):
    low = dx2_ref[...].astype(bf16)
    low_three = dx3_ref[...].astype(bf16)
    for c, x, m in pieces(spot):
        lanes = aligned(LANES * m)
        grads = [
            tn(n2_ref[...], dquery_ref[:, lanes]),
            tn(all_ref[...], dkv_ref[m]),
            tn(table_ref[...], dpe_ref[:, lanes]),
        ]
        write_piece(spot, parts, 0, c, x, jnp.concatenate(grads, 1))
        grads = [
            tn(n3_ref[...], dgate_ref[m]),
            tn(low, att_ref[:, lanes]),
            tn(low_three, act_ref[:, lanes]),
        ]
        write_piece(spot, parts, 1, c, x, jnp.concatenate(grads, 1))


def last_kernel(
    spot,
    weights,
    dx2_ref,
    d_all_ref,
    d_own_ref,
    x1_ref,
    x0_ref,
    pre_ref,
    n1_ref,
    vec_ref,
    a_ref,
    b_ref,
    a_send_ref,
    b_send_ref,
    dx0_ref,
    vgrad_ref,
    in_buf,
    in_sem,
    out_buf,
    out_sem,
):
    copies = fetched(weights, 0, 0, D, in_buf, in_sem)
    copies += fetched(weights, 1, 0, D, out_buf, out_sem)
    grad = total(*[d_all_ref[k] for k in range(d_all_ref.shape[0])]) + d_own_ref[...]
    dx, gain, shift = layer_norm_back(x1_ref[...], vec_ref[1:2, :], grad)
    vgrad_ref[0:1, :] = gain
    vgrad_ref[1:2, :] = shift
    for copy in copies:
        copy.wait()
    dx0, gain, shift = ffn_backward(
        spot,
        dx2_ref[...] + dx,
        x0_ref[...],
        vec_ref,
        0,
        in_buf,
        out_buf,
        pre_ref,
        n1_ref,
        (a_ref, b_ref, a_send_ref, b_send_ref),
    )
    vgrad_ref[2:3, :] = gain
    vgrad_ref[3:4, :] = shift
    dx0_ref[...] = dx0.astype(bf16)


def adam(state, grad, rate):
    first_new = beta_one * state[1] + (1.0 - beta_one) * grad
    second_new = beta_two * state[2] + (1.0 - beta_two) * grad * grad
    direction = (
        first_new
        / (1.0 - beta_one**STEP)
        / (jnp.sqrt(second_new / (1.0 - beta_two**STEP)) + adam_eps)
    )
    weight_new = state[0] - rate * (direction + decay_rate * state[0])
    return (weight_new, first_new, second_new)


def small_rate(positions):
    rate = jnp.full(positions.shape, small_rates[-1], f32)
    for k in range(3, -1, -1):
        rate = jnp.where(positions < sum(SIZES[: k + 1]), small_rates[k], rate)
    return rate


def mel_windows(mel, utter_len, rank, tokens):
    frame = rank * (8 * tokens) + jnp.arange(8 * tokens, dtype=jnp.int32)
    kept = jnp.where((frame < utter_len)[:, None], mel, jnp.zeros((), bf16))
    prior = passed_along(kept[-8:], 1)
    rows = tokens + EDGE
    field = jnp.concatenate([jnp.zeros((8 * (EDGE - 1), MEL), bf16), prior, kept], 0)
    field = field.reshape(rows, 8, MEL).transpose(1, 2, 0)
    lag = jnp.concatenate([jnp.zeros((1, MEL, 1), bf16), field[7:8, :, :-1]], 2)
    field = jnp.concatenate([lag, field], 0)
    field = jnp.pad(field, ((0, 0), (1, 1), (0, 0))).reshape(9, F1 + 1, 2, rows)
    bands = [field[:, :F1, 0], field[:, :F1, 1], field[:, 1:, 0]]
    taps = [bands[df][dt : dt + 7 : 2] for dt in range(3) for df in range(3)]
    taps = jnp.stack(taps + [jnp.zeros_like(taps[0])] * 7, 0)
    turned = taps.transpose(0, 2, 1, 3).reshape(16, F1 * 4 * rows)
    wide = taps.reshape(16, 4, F1 // 8, 8, rows).transpose(2, 1, 4, 3, 0)
    return wide.reshape(F1 // 8, 4 * rows, LANES), turned


def position_table(rank, rows, length):
    distance = (rows * rank + rows - 1 - jnp.arange(rows + length)).astype(f32)[:, None]
    inverse_freq = jnp.exp(jnp.arange(D // 2).astype(f32) * (-2.0 * math.log(10000.0) / D))
    angles = distance * inverse_freq[None, :]
    return jnp.concatenate([jnp.sin(angles), jnp.cos(angles)], 1).astype(bf16)


def gathered_heads(n2, planned_mesh):
    if not planned_mesh:
        return lax.all_gather(n2, "mp", axis=0, tiled=True)
    rows = n2.shape[0]
    pair = jnp.stack([n2, sent(n2, "x")])
    both = jnp.stack([pair, sent(pair, "c")])
    rank = lax.axis_index("mp")
    order = [(rank % 2, rank // 2)]
    whole = jnp.zeros((4, rows, D), bf16)
    c, x = order[0]
    for i in range(2):
        for j in range(2):
            at = ((x + j) % 2) * 2 + (c + i) % 2
            whole = lax.dynamic_update_slice(whole, both[i, j][None], (at, 0, 0))
    return whole.reshape(4 * rows, D)


def body(mel, lengths, alignment, loss_mask, ff_in, ff_out, mix_in, mix_out, small):
    n_dp, n_mp = lax.axis_size("dp"), lax.axis_size("mp")
    ndev = n_dp * n_mp
    plan = planned(n_dp, n_mp)
    rank, dp_rank = lax.axis_index("mp"), lax.axis_index("dp")
    device = lax.axis_index(("dp", "mp"))
    tokens = alignment.shape[1]
    length = tokens * n_mp
    rows = tokens + EDGE
    own_rows = ff_in.shape[2]
    shard = small.shape[1]
    half = -(-(-(-(shard + 16 * LANES - 1) // LANES)) // 32) * 16
    chunk = 2 * half
    flat_rows = max((shard * (ndev - 1)) // (16 * LANES) * 16 + chunk, NROWS)
    flat_rows = -(-flat_rows // 8) * 8
    if plan:
        spot = jnp.stack([rank % 2, rank // 2, dp_rank % 2, dp_rank // 2])
        deep, lines = LINES, n_dp // LINES
    else:
        spot = jnp.zeros((4,), jnp.int32)
        deep, lines = 1, 1
    spot = spot.astype(jnp.int32), pltpu.SMEM
    piece_rows = D // (deep * lines)
    small_rows = half * (n_dp // (deep * lines))

    row = first_row(shard, device)
    offset = shard * device - row * LANES
    small_low = lax.dynamic_update_slice_in_dim(
        jnp.zeros((chunk * LANES,), bf16), small[0].astype(bf16), offset, 0
    ).reshape(chunk, LANES)
    in_low = ff_in[0].astype(bf16)
    out_low = ff_out[0].astype(bf16).transpose(0, 2, 1)
    mix_low = mix_in[0].astype(bf16)
    mixo_low = mix_out[0].astype(bf16).transpose(0, 2, 1)
    qkvp_low = mix_low[:, 0:4].reshape(own_rows, 4 * LANES)
    abo_low = jnp.concatenate([mix_low[:, 4], mix_low[:, 5], mixo_low[0], mixo_low[1]], 1)
    def gathered(low):
        whole = lax.all_gather(jnp.stack(low), ("dp", "mp"), axis=0)
        whole = whole.reshape(n_dp, n_mp, len(low), own_rows, D)
        if not plan:
            whole = whole.transpose(1, 2, 0, 3, 4).reshape(1, n_mp, len(low), D, D)
        return whole

    big_all = gathered([in_low[0], out_low[0], qkvp_low, abo_low])
    more_all = gathered([in_low[1], out_low[1]])
    weights, more = (big_all, pl.ANY), (more_all, pl.ANY)
    utter_len = lengths[0]
    windows, windows_t = mel_windows(mel[0], utter_len, rank, tokens)
    table = position_table(rank, tokens, length)
    if plan:
        few_all = Gathered(small_low)
        few_all.lines(), few_all.after(windows, windows_t, table).first(), few_all.second()
        small_all = few_all.cores()
    else:
        small_all = [lax.all_gather(small_low, ("dp", "mp"), axis=0)]

    frames = jnp.arange(length, dtype=jnp.int32)
    keep_row = (8 * frames < utter_len).astype(f32)[None, :]
    wide_frame = rank * tokens - HALO + jnp.arange(tokens + 2 * HALO, dtype=jnp.int32)
    wide_valid = (wide_frame >= 0) & (wide_frame < length) & (8 * wide_frame < utter_len)
    wide_valid = wide_valid.astype(f32)[:, None]
    valid = wide_valid[HALO : HALO + tokens]
    weight = valid * loss_mask[0].astype(f32)[:, None]

    def split(each):
        return [((COLS, deep, lines, each, D), bf16)] * 4

    unpack = functools.partial(unpack_kernel if plan else unpack_whole_kernel, shard)
    taps, tap_one, pointwise, linear, head, vec = call(
        unpack,
        [
            ((32, CHANNELS), f32),
            ((8, LANES, CHANNELS), bf16),
            ((2, CHANNELS, CHANNELS), bf16),
            ((F3, CHANNELS, D), bf16),
            ((D, CPAD), bf16),
            ((24, D), f32),
        ],
        ([spot] if plan else []) + small_all,
        [pltpu.VMEM((flat_rows, LANES), f32)],
        us=7,
        name="unpack",
    )
    x0, front, mid, last = call(
        stem_kernel,
        [
            ((tokens, D), f32),
            ((F2, 2 * rows, CHANNELS), bf16),
            ((F3, tokens, CHANNELS), bf16),
            ((F3, tokens, CHANNELS), bf16),
        ],
        [windows, tap_one, taps, pointwise, (linear, pl.ANY)],
        stem_scratch(rows),
        us=13,
        out_any=(1,),
        name="stem",
    )
    x1, pre_one, n1, n2 = call(
        first_kernel,
        [
            ((tokens, D), f32),
            ((n_mp, tokens, D), f32),
            ((tokens, D), bf16),
            ((tokens, D), bf16),
        ],
        [weights, x0, vec],
        buffers(big_all, D, D),
        us=6,
        name="first",
    )
    n_all = gathered_heads(n2, plan)
    pe, qu, qv = call(
        position_kernel,
        [((tokens + length, D), bf16), ((tokens, D), bf16), ((tokens, D), bf16)],
        [weights, table, n2, vec],
        buffers(big_all, LANES, LANES),
        us=5,
        name="position",
    )
    x2, kv, prob, att, n3, ga, gb, gated, g_low, g_high = call(
        attention_kernel,
        [
            ((tokens, D), f32),
            ((n_mp, length, 2 * LANES), bf16),
            ((HEADS, tokens, length), f32),
            ((tokens, D), bf16),
            ((tokens, D), bf16),
            ((tokens, D), f32),
            ((tokens, D), f32),
            ((tokens, D), f32),
            ((HALO, D), f32),
            ((HALO, D), f32),
        ],
        [weights, n_all, x1, qu, qv, pe, vec, keep_row, valid],
        buffers(big_all, 2 * LANES, 3 * LANES),
        us=10,
        name="attention",
    )
    g_prev, g_next = passed_along(g_high, 1), passed_along(g_low, -1)
    stat_shape = ((ndev, 16, LANES), f32)
    wide = pltpu.VMEM((tokens + 2 * HALO, D), f32)
    hidden, stat = call(
        conv_kernel,
        [((tokens, D), f32), stat_shape],
        [g_prev, gated, g_next, vec, valid],
        [wide],
        us=2,
        name="conv",
    )
    stat = spread(stat)
    two, g_head, dx3, act, dy, yhat, b_low, b_high, part, vg_mid = call(
        middle_kernel,
        [
            ((n_dp if plan else 1, n_mp, 2, own_rows if plan else D, D), bf16),
            ((D, CPAD), f32),
            ((tokens, D), f32),
            ((tokens, D), bf16),
            ((tokens, D), f32),
            ((tokens, D), f32),
            ((2 * HALO, D), f32),
            ((2 * HALO, D), f32),
            stat_shape,
            ((6, D), f32),
        ],
        [weights, more, hidden, stat, x2, head, vec, alignment[0][:, None], weight, valid],
        [
            pltpu.VMEM((n_mp, tokens, D), f32),
            pltpu.VMEM((tokens, D), bf16),
            *buffers(big_all, LANES, D, D),
        ],
        us=13,
        name="middle",
    )
    b_prev, b_next = passed_along(b_high, 1), passed_along(b_low, -1)
    part = spread(part)
    if not plan:
        two = two.reshape(n_mp, 2, n_dp, own_rows, D).transpose(2, 0, 1, 3, 4)
    two = lax.psum_scatter(
        two.reshape(ndev, 2 * own_rows, D), ("dp", "mp"), scatter_dimension=0, tiled=True
    )
    own_in_two, own_out_two = two.reshape(2, own_rows, D).astype(f32)
    dgate, dx2, vg_conv, loss = call(
        conv_back_kernel,
        [
            ((n_mp, tokens, 2 * LANES), bf16),
            ((tokens, D), f32),
            ((11, D), f32),
            ((1, 1), f32),
        ],
        [
            weights,
            dy,
            yhat,
            b_prev,
            b_next,
            part,
            stat,
            wide_valid,
            g_prev,
            gated,
            g_next,
            ga,
            gb,
            x2,
            dx3,
            vec,
        ],
        [wide, wide, wide, *buffers(big_all, 2 * LANES)],
        us=4,
        name="conv_back",
    )
    dquery, dkv, dpe, d_all, d_own, vg_att = call(
        back_kernel,
        [
            ((tokens, D), bf16),
            ((n_mp, length, 2 * LANES), bf16),
            ((tokens + length, D), bf16),
            ((length, D), bf16),
            ((tokens, D), f32),
            ((2, D), f32),
        ],
        [weights, dx2, prob, kv, qu, qv, pe],
        [pltpu.VMEM((2 * tokens, D), f32), *buffers(big_all, LANES, 3 * LANES)],
        us=10,
        name="back",
    )
    if plan:
        pair = d_all.reshape(2, 2, tokens, D)
        core, col = rank % 2, rank // 2
        other = lax.dynamic_slice_in_dim(pair, 1 - core, 1, 1)[:, 0]
        own = lax.dynamic_slice_in_dim(pair, core, 1, 1)[:, 0]
        pair = low_total(own, sent(other, "c"))
        wait = [pair]
        other = lax.dynamic_slice_in_dim(pair, 1 - col, 1, 0)
        own = lax.dynamic_slice_in_dim(pair, col, 1, 0)
        d_mine = jnp.concatenate([own, sent(other, "x")], 0)
    else:
        d_mine = lax.psum_scatter(d_all, "mp", scatter_dimension=0, tiled=True)[None]
        wait = ()
    mix = call(
        mix_grad_kernel,
        split(piece_rows),
        [spot, dx2, dx3, dgate, n3, act, att, n2, n_all, table, dquery, dkv, dpe],
        us=7,
        after=wait,
        name="mix_grad",
    )
    mix_sum = Reduced(*mix)
    *one, dx0, vg_last = call(
        last_kernel,
        [*split(piece_rows), ((tokens, D), bf16), ((4, D), f32)],
        [spot, weights, dx2, d_mine, d_own, x1, x0, pre_one, n1, vec],
        buffers(big_all, D, D),
        us=8,
        after=mix[:1],
        name="last",
    )
    one_sum = Reduced(*one)
    few_parts = call(
        functools.partial(pack_kernel, shard, n_dp),
        [((COLS, deep, lines, small_rows, LANES), bf16)] * 4,
        [spot, last, dx0, g_head],
        [pltpu.VMEM((flat_rows, LANES), f32)],
        us=5,
        after=mix_sum.cores() if plan else (),
        name="pack",
    )
    few_sum = Reduced(*few_parts)
    g_pw, sums, g_one = call(
        stem_back_kernel,
        [
            ((2, CHANNELS, CHANNELS), f32),
            ((18, 8, CHANNELS), f32),
            ((16, CHANNELS), f32),
        ],
        [
            dx0,
            (windows, pl.ANY),
            (windows_t, pl.ANY),
            tap_one,
            taps,
            pointwise,
            (linear, pl.ANY),
            (front, pl.ANY),
            (mid, pl.ANY),
            (last, pl.ANY),
        ],
        back_scratch(rows),
        us=27,
        after=one_sum.cores() if plan else (),
        name="stem_back",
    )
    used = ROW_AT[2] + ROWS[4]
    share = -(-(-(-used // ndev)) // 16) * 16
    (few,) = call(
        stem_rows_kernel,
        [((ndev * share, LANES), bf16)],
        [g_pw, sums, g_one, vg_last, vg_conv, vg_mid, vg_att],
        [pltpu.VMEM((ndev * share, LANES), f32)],
        us=2,
        after=mix_sum.first() + one_sum.first() + few_sum.cores() if plan else (),
        name="stem_rows",
    )
    few = jnp.sum(spread(few.reshape(ndev, share, LANES)).astype(f32), 0)

    if plan:
        mix_sum.second()
        own_mix, own_abo = mix_sum.lines()
        few_sum.first()
        one_sum.second()
        own_in_one, own_out_one = one_sum.lines()
        few_sum.second()
        own_few = few_sum.lines()
    else:
        own_mix, own_abo = reduced_whole(mix, own_rows)
        own_in_one, own_out_one = reduced_whole(one, own_rows)
        own_few = reduced_whole(few_parts, half)
    own_chunk = jnp.concatenate(own_few, 0)

    start = shard * device
    positions = start + jnp.arange(shard, dtype=jnp.int32)
    own = [own_in_one, own_out_one, own_mix, own_abo, own_in_two, own_out_two]
    packed = lax.dynamic_slice_in_dim(own_chunk.reshape(-1), offset, shard, 0)
    local_sq = sum(jnp.sum(grad * grad) for grad in own) + jnp.sum(packed * packed)
    high = local_sq.astype(bf16)
    rest = local_sq - high.astype(f32)
    middle = rest.astype(bf16)
    lowest = (rest - middle.astype(f32)).astype(bf16)
    lane = jnp.arange(LANES)[None, :]
    number = jnp.where(lane == 0, high, jnp.where(lane == 1, middle, jnp.where(lane == 2, lowest, 0)))
    number = jnp.broadcast_to(number, (16, LANES)).astype(bf16)
    known = jnp.concatenate([few.astype(bf16), number], 0)
    known = spread(jnp.broadcast_to(known[None], (ndev, share + 16, LANES))).astype(f32)
    few = known[:, :share].reshape(ndev * share, LANES)
    total_sq = jnp.sum(known[:, share, 0:3]) + jnp.sum(few * few)
    grad_norm = jnp.sqrt(total_sq)
    factor = clip_norm / jnp.maximum(grad_norm, clip_norm)

    gap = jnp.zeros((chunk, LANES), f32)
    def window(part, at):
        padded = jnp.concatenate([gap, part, gap], 0)
        where = jnp.clip(row - at + chunk, 0, chunk + part.shape[0])
        return lax.dynamic_slice_in_dim(padded, where, chunk, 0)

    own_chunk = own_chunk + window(few[: ROW_AT[2]], 0) + window(few[ROW_AT[2] : used], ROW_AT[4])
    own_small = lax.dynamic_slice_in_dim(own_chunk.reshape(-1), offset, shard, 0)

    grad_in = jnp.stack([own_in_one, own_in_two])
    grad_out = jnp.stack([own_out_one, own_out_two]).transpose(0, 2, 1)
    grad_mix = jnp.concatenate([own_mix, own_abo[:, : 2 * LANES]], 1).reshape(own_rows, 6, LANES)
    grad_mixo = own_abo[:, 2 * LANES :].reshape(own_rows, 2, LANES).transpose(1, 2, 0)
    rates = (0.1, 0.05, 0.1, jnp.array([1.0, 0.1], f32)[:, None, None])
    states = (ff_in, ff_out, mix_in, mix_out)
    grads = (grad_in, grad_out, grad_mix, grad_mixo)
    outs = []
    for state, grad, rate in zip(states, grads, rates):
        outs.extend(adam(state, grad * factor, rate))
    outs.extend(adam(small, own_small * factor, small_rate(positions)))
    vec_grad = few[ROW_AT[2] : used].reshape(23, D) * factor
    return (*outs, vec_grad, loss[0, 0], grad_norm)


def solution(mesh):
    in_specs = (
        P("dp", "mp", None),
        P("dp"),
        P("dp", "mp"),
        P("dp", "mp"),
        P(None, None, "dp", "mp"),
        P(None, None, "mp", "dp"),
        P(None, "dp", None, "mp"),
        P(None, None, "mp", "dp"),
        P(None, ("dp", "mp")),
    )
    in_block, out_block = P(None, "dp", "mp"), P(None, "mp", "dp")
    mix_block, flat = P("dp", None, "mp"), P(("dp", "mp"))
    out_specs = (
        (in_block,) * 3 + (out_block,) * 3 + (mix_block,) * 3 + (out_block,) * 3 + (flat,) * 3
    )
    out_specs = out_specs + (P(), P(), P())
    return jax.shard_map(body, mesh=mesh, in_specs=in_specs, out_specs=out_specs, check_vma=False)
```

time: 2090 us -> 417 us (0.20)
  local copies, waits for them, and re-layouts: 970 us -> 25.2 us
  waiting for transfers between devices: 402 us -> 115 us
  blocking collectives: 255 us -> 0 us
  matrix products: 178 us -> 0 us
  other arithmetic: 228 us -> 50.7 us
  Pallas kernels: 0 us -> 127 us
  starting transfers between devices: 3.9 us -> 71.4 us
    slice x46 -> x10, local copies, waits for them, and re-layouts: 478 us -> 1.65 us  [the longest x1 0.74 us: body(): valid = wide_valid[HALO:HALO + tokens]]
    unnamed x21 -> x3, waiting for transfers between devices: 242 us -> 0.05 us
    pad x18 -> x1, local copies, waits for them, and re-layouts: 221 us -> 0.11 us  [mel_windows(): field = jnp.pad(field, ((0, 0), (1, 1), (0, 0))).reshape(9, F1 + 1, 2, rows)]
    unnamed x561 -> x124, local copies, waits for them, and re-layouts: 184 us -> 5.8 us
    dot_general x65 -> x0, matrix products: 173 us -> none  [the longest x49 104 us: product(): return jnp.dot(left, right, preferred_element_type=jnp.float32)]
    reduce_scatter x13 -> x1, waiting for transfers between devices: 160 us -> 5.87 us  [body(): lax.psum_scatter(two.reshape(ndev, 2 * own_rows, D), ('dp', 'mp'), scatte...]
    all_gather x14 -> x0, blocking collectives: 148 us -> none  [the longest x12 82.5 us: gather_rows(): return lax.all_gather(values, 'mp', axis=0, tiled=True)]
    pallas_call x0 -> x14, Pallas kernels: none -> 127 us  [call(): pl.pallas_call(run, out_shape=[jax.ShapeDtypeStruct(shape, dtype) for sha...]
  transfers between devices with their start and end apart: 19 -> 51, of which waited for: 11 -> 21; matrix products, arithmetic and copies ran while one was open for 54% -> 13% of each run, Pallas kernels for 0% -> 24%
where the time goes in v1:
time: 417 us; the launch traced here: 412 us
  Pallas kernels  127 us (30%)
  waiting for transfers between devices  115 us (28%)
  starting transfers between devices  71.4 us (17%)
  other arithmetic  50.7 us (12%)
  local copies, waits for them, and re-layouts  25.2 us (6%)
  between operations  23.2 us (6%)
    pallas_call x14, Pallas kernels, call(): pl.pallas_call(run, out_shape=[jax.ShapeDtypeStruct(shape, dtype) for sha...  127 us
    ppermute x39, waiting for transfers between devices, sent(): return lax.ppermute(x, axis, pairs)  49.2 us
    ppermute x39, starting transfers between devices, sent(): return lax.ppermute(x, axis, pairs)  48.5 us
    all_gather x2, waiting for transfers between devices, gathered(): whole = lax.all_gather(jnp.stack(low), ('dp', 'mp'), axis=0)  31.7 us
    all_to_all x4, waiting for transfers between devices, spread(): return lax.all_to_all(x, ('dp', 'mp'), 0, 0, tiled=True)  23.6 us
    convert_element_type x19, other arithmetic, low_total(): return total(*parts).astype(bf16)  16.8 us
    all_to_all x4, starting transfers between devices, spread(): return lax.all_to_all(x, ('dp', 'mp'), 0, 0, tiled=True)  14.3 us
    ppermute x5, starting transfers between devices, passed_along(): return lax.ppermute(x, 'mp', pairs)  8.43 us
  transfers between devices with their start and end apart: 51, of which 21 were waited for; matrix products, arithmetic and copies ran while one was open for 13% of the time, Pallas kernels for 24%

profile of v1, /device:TPU:0, one launch (start us, length us, event | category | flops | bytes accessed | tf_op | source)
XLA Modules:
  0.0 412.1 jit_solution(16219424662547926005)
XLA Ops:
  12.1 2.8 multiply_reduce_fusion.3
  16.9 5.1 %collective-permute-start.1 = (bf16[512,128]{1,0:T(8,128)(2,1)S(1)}, bf16[512,128]{1,0:T(8,128)(2,1)S(1)}, u32[]{:S(2)}, u32[]{:S(2)}) collective-permute-start(bf16[512,128]{1,0:T(8,128)(2,1)S(1)} %bitcast.664), channel_id=1, source_target_pairs={{0,24},{4,28},{8,0},{12,4},{16,8},{20,12},{24,16},{28,20},{1,25},{... | collective-permute-start | bytes 393224 | tf_op jit(solution)/shard_map/ppermute | solution.py:61
  25.6 2.7 fusion.1
  33.0 3.1 reshape.1394.refs_2_
  41.1 5.7 %collective-permute-done.4 = bf16[4,256,128]{2,1,0:T(8,128)(2,1)S(1)} collective-permute-done((bf16[4,256,128]{2,1,0:T(8,128)(2,1)S(1)}, bf16[4,256,128]{2,1,0:T(8,128)(2,1)S(1)}, u32[]{:S(2)}, u32[]{:S(2)}) %collective-permute-start.4) | collective-permute-done | bytes 262176 | tf_op jit(solution)/shard_map/ppermute | solution.py:61
  49.8 13.9 %collective-permute-done.5 = bf16[2,4,256,128]{3,2,1,0:T(8,128)(2,1)S(1)} collective-permute-done((bf16[2,4,256,128]{3,2,1,0:T(8,128)(2,1)S(1)}, bf16[2,4,256,128]{3,2,1,0:T(8,128)(2,1)S(1)}, u32[]{:S(2)}, u32[]{:S(2)}) %collective-permute-start.5) | collective-permute-done | bytes 524320 | tf_op jit(solution)/shard_map/ppermute | solution.py:61
  63.8 3.6 collective-permute-done.7
  72.1 9.8 %unpack.1 = (f32[32,256]{1,0:T(8,128)}, bf16[8,128,256]{2,1,0:T(8,128)(2,1)}, bf16[2,256,256]{2,1,0:T(8,128)(2,1)}, bf16[10,256,512]{2,1,0:T(8,128)(2,1)}, bf16[512,1152]{1,0:T(8,128)(2,1)}, /*index=5*/f32[24,512]{1,0:T(8,128)}) custom-call(s32[4]{0:T(128)} %pad_add_fusion.refs_0_, bf16[2,16,256,128]{3,2,1,0:T(8,128)(2,1)} %copy-done.2, ...), custom_call_target="tpu_custom_call" | custom-call | flops 8049999872 | bytes 7000000 | tf_op jit(solution)/shard_map/unpack/pallas_call | solution.py:181
  81.9 13.4 %stem.1 = (f32[128,512]{1,0:T(8,128)}, bf16[20,288,256]{2,1,0:T(8,128)(2,1)}, bf16[10,128,256]{2,1,0:T(8,128)(2,1)}, bf16[10,128,256]{2,1,0:T(8,128)(2,1)}) custom-call(bf16[5,576,128]{2,1,0:T(8,128)(2,1)} %copy.162.refs_0_.refs_1_, bf16[8,128,256]{2,1,0:T(8,128)(2,1)} %get-tuple-element.88.refs_1_.refs_3_, f32[32,256]{1,0:T(8,128)} %get-tuple-element.89.refs_2_.refs_4_, ...), custom_call_target="tpu_custom_call" | custom-call | flops 14949999616 | bytes 13000000 | tf_op jit(solution)/shard_map/stem/pallas_call | solution.py:181
  95.2 8.4 %all-gather.5.cloned.1.call-done = bf16[128,64,512]{2,1,0:T(8,128)(2,1)} async-done(((bf16[4,64,512]{2,1,0:T(8,128)(2,1)}), bf16[128,64,512]{2,1,0:T(8,128)(2,1)}) %all-gather.5.cloned.1.call-update) | async-done | bytes 8388624 | tf_op jit(solution)/shard_map/all_gather | solution.py:1334
  103.7 4.8 %first.1 = (f32[128,512]{1,0:T(8,128)}, f32[4,128,512]{2,1,0:T(8,128)}, bf16[128,512]{1,0:T(8,128)(2,1)}, bf16[128,512]{1,0:T(8,128)(2,1)}) custom-call(bf16[8,4,4,64,512]{4,3,2,1,0:T(8,128)(2,1)} %bitcast.677, f32[128,512]{1,0:T(8,128)} %get-tuple-element.92.refs_1_.refs_6_, f32[24,512]{1,0:T(8,128)} %get-tuple-element.93.refs_2_.refs_3_.refs_6_.refs_15_.refs_9_), custom_call_target="tpu_custom_call" | custom-call | flops 6899999744 | bytes 6000000 | tf_op jit(solution)/shard_map/first/pallas_call | solution.py:181
  110.0 5.8 %position.1 = (bf16[640,512]{1,0:T(8,128)(2,1)}, bf16[128,512]{1,0:T(8,128)(2,1)}, bf16[128,512]{1,0:T(8,128)(2,1)}) custom-call(bf16[8,4,4,64,512]{4,3,2,1,0:T(8,128)(2,1)} %bitcast.678, bf16[640,512]{1,0:T(8,128)(2,1)} %pad_maximum_fusion.3.refs_1_.refs_9_, bf16[128,512]{1,0:T(8,128)(2,1)} %get-tuple-element.94.refs_2_.refs_7_, ...), custom_call_target="tpu_custom_call" | custom-call | flops 5750000128 | bytes 5000000 | tf_op jit(solution)/shard_map/position/pallas_call | solution.py:181
  118.3 10.9 %attention.1 = (f32[128,512]{1,0:T(8,128)}, bf16[4,512,256]{2,1,0:T(8,128)(2,1)}, f32[8,128,512]{2,1,0:T(8,128)}, bf16[128,512]{1,0:T(8,128)(2,1)}, bf16[128,512...) custom-call(bf16[8,4,4,64,512]{4,3,2,1,0:T(8,128)(2,1)} %bitcast.679, ...), custom_call_target="tpu_custom_call" | custom-call | flops 11500000256 | bytes 10000000 | tf_op jit(solution)/shard_map/attention/pallas_call | solution.py:181
  129.2 2.1 collective-permute-start.11
  132.6 2.0 collective-permute-done.12.refs_2_.refs_10_
  135.3 2.3 conv.1
  137.6 6.0 %all-to-all-start = ((f32[32,16,128]{2,1,0:T(8,128)}), f32[32,16,128]{2,1,0:T(8,128)S(1)}, u32[]{:S(2)}, u32[]{:S(2)}) async-start(f32[32,16,128]{2,1,0:T(8,128)} %get-tuple-element.103), calls=%async_computation | async-start | bytes 524288 | tf_op jit(solution)/shard_map/all_to_all | solution.py:158
  145.1 23.3 %all-gather.7.cloned.1.call-done = bf16[64,64,512]{2,1,0:T(8,128)(2,1)} async-done(((bf16[2,64,512]{2,1,0:T(8,128)(2,1)}), bf16[64,64,512]{2,1,0:T(8,128)(2,1)}) %all-gather.7.cloned.1.call-update) | async-done | bytes 4194320 | tf_op jit(solution)/shard_map/all_gather | solution.py:1334
  169.1 11.4 %middle.1 = (bf16[8,4,2,64,512]{4,3,2,1,0:T(8,128)(2,1)}, f32[512,1152]{1,0:T(8,128)}, f32[128,512]{1,0:T(8,128)}, bf16[128,512]{1,0:T(8,128)(2,1)}, f32[128,512...) custom-call(bf16[8,4,4,64,512]{4,3,2,1,0:T(8,128)(2,1)} %bitcast.680, ...), custom_call_target="tpu_custom_call" | custom-call | flops 14949999616 | bytes 13000000 | tf_op jit(solution)/shard_map/middle/pallas_call | solution.py:181
  180.5 3.1 all-to-all-start.1
  183.7 2.2 collective-permute-start.13
  187.9 2.3 collective-permute-done.14.refs_4_
  190.3 3.9 all-to-all-done.1.refs_5_
  194.9 4.3 %conv_back.1 = (bf16[4,128,256]{2,1,0:T(8,128)(2,1)}, f32[128,512]{1,0:T(8,128)}, f32[11,512]{1,0:T(8,128)}, f32[1,1]{1,0:T(1,128)}) custom-call(bf16[8,4,4,64,512]{4,3,2,1,0:T(8,128)(2,1)} %bitcast.681, f32[128,512]{1,0:T(8,128)} %get-tuple-element.106.refs_1_, f32[128,512]{1,0:T(8,128)} %get-tuple-element.107.refs_2_, f32[16,512]{1,0:T(8,128)} %copy-done.44, ...), custom_call_target="tpu_custom_call" | custom-call | flops 4600000000 | bytes 4000000 | tf_op jit(solution)/shard_map/conv_back/pallas_call | solution.py:181
  199.2 13.3 %back.1 = (bf16[128,512]{1,0:T(8,128)(2,1)}, bf16[4,512,256]{2,1,0:T(8,128)(2,1)}, bf16[640,512]{1,0:T(8,128)(2,1)}, bf16[512,512]{1,0:T(8,128)(2,1)}, f32[128,512]{1,0:T(8,128)}, /*index=5*/f32[2,512]{1,0:T(2,128)}) custom-call(bf16[8,4,4,64,512]{4,3,2,1,0:T(8,128)(2,1)} %bitcast.682, f32[128,512]{1,0:T(8,128)} %get-tuple-element.114.refs_1_.refs_2_, ...), custom_call_target="tpu_custom_call" | custom-call | flops 11500000256 | bytes 10000000 | tf_op jit(solution)/shard_map/back/pallas_call | solution.py:181
  216.8 6.2 %mix_grad.1 = (bf16[2,2,4,64,512]{4,3,2,1,0:T(8,128)(2,1)}, bf16[2,2,4,64,512]{4,3,2,1,0:T(8,128)(2,1)}, bf16[2,2,4,64,512]{4,3,2,1,0:T(8,128)(2,1)}, bf16[2,2,4,64,512]{4,3,2,1,0:T(8,128)(2,1)}) custom-call(s32[4]{0:T(128)} %pad_add_fusion.refs_0_, f32[128,512]{1,0:T(8,128)} %get-tuple-element.114.refs_1_.refs_2_, ...), custom_call_target="tpu_custom_call" | custom-call | flops 8049999872 | bytes 7000000 | tf_op jit(solution)/shard_map/mix_grad/pallas_call | solution.py:181
  224.3 8.6 %last.1 = (bf16[2,2,4,64,512]{4,3,2,1,0:T(8,128)(2,1)}, bf16[2,2,4,64,512]{4,3,2,1,0:T(8,128)(2,1)}, bf16[2,2,4,64,512]{4,3,2,1,0:T(8,128)(2,1)}, bf16[2,2,4,64,...) custom-call(s32[4]{0:T(128)} %pad_add_fusion.refs_0_, bf16[8,4,4,64,512]{4,3,2,1,0:T(8,128)(2,1)} %bitcast.683, ...), custom_call_target="tpu_custom_call" | custom-call | flops 9200000000 | bytes 8000000 | tf_op jit(solution)/shard_map/last/pallas_call | solution.py:181
  238.0 6.4 %pack.1 = (bf16[2,2,4,256,128]{4,3,2,1,0:T(8,128)(2,1)}, bf16[2,2,4,256,128]{4,3,2,1,0:T(8,128)(2,1)}, bf16[2,2,4,256,128]{4,3,2,1,0:T(8,128)(2,1)}, bf16[2,2,4,256,128]{4,3,2,1,0:T(8,128)(2,1)}) custom-call(s32[4]{0:T(128)} %pad_add_fusion.refs_0_, bf16[10,128,256]{2,1,0:T(8,128)(2,1)} %get-tuple-element.137.refs_9_.refs_1_, ...), custom_call_target="tpu_custom_call" | custom-call | flops 5750000128 | bytes 5000000 | tf_op jit(solution)/shard_map/pack/pallas_call | solution.py:181
  247.8 27.5 %stem_back.1 = (f32[2,256,256]{2,1,0:T(8,128)}, f32[18,8,256]{2,1,0:T(8,128)}, f32[16,256]{1,0:T(8,128)}) custom-call(bf16[128,512]{1,0:T(8,128)(2,1)} %get-tuple-element.134.refs_0_.refs_2_, bf16[5,576,128]{2,1,0:T(8,128)(2,1)} %copy.162.refs_0_.refs_1_, bf16[16,23040]{1,0:T(8,128)(2,1)} %reshape.1394.refs_2_, ...), custom_call_target="tpu_custom_call" | custom-call | flops 31050000384 | bytes 27000000 | tf_op jit(solution)/shard_map/stem_back/pallas_call | solution.py:181
  281.2 11.3 %collective-permute-done.21 = bf16[2,4,64,512]{3,2,1,0:T(8,128)(2,1)S(1)} collective-permute-done((bf16[2,4,64,512]{3,2,1,0:T(8,128)(2,1)}, bf16[2,4,64,512]{3,2,1,0:T(8,128)(2,1)S(1)}, u32[]{:S(2)}, u32[]{:S(2)}) %collective-permute-start.21) | collective-permute-done | bytes 524320 | tf_op jit(solution)/shard_map/ppermute | solution.py:61
  293.4 6.1 %collective-permute-done.32 = bf16[4,64,512]{2,1,0:T(8,128)(2,1)S(1)} collective-permute-done((bf16[4,64,512]{2,1,0:T(8,128)(2,1)S(1)}, bf16[4,64,512]{2,1,0:T(8,128)(2,1)S(1)}, u32[]{:S(2)}, u32[]{:S(2)}) %collective-permute-start.32) | collective-permute-done | bytes 262176 | tf_op jit(solution)/shard_map/ppermute | solution.py:61
  299.5 1.7 collective-permute-start.22
  305.2 2.1 collective-permute-start.35
  308.7 2.6 collective-permute-start.36
  316.9 2.6 collective-permute-start.24
  319.5 5.1 %collective-permute-start.25 = (bf16[2,64,512]{2,1,0:T(8,128)(2,1)}, bf16[2,64,512]{2,1,0:T(8,128)(2,1)}, u32[]{:S(2)}, u32[]{:S(2)}) collective-permute-start(bf16[2,64,512]{2,1,0:T(8,128)(2,1)} %pad_maximum_fusion.15), channel_id=1, source_target_pairs={{0,24},{4,28},{8,0},{12,4},{16,8},{20,12},{24,16},{28,20},{1,25},{... | collective-permute-start | bytes 393224 | tf_op jit(solution)/shard_map/ppermute | solution.py:61
  324.5 2.5 multiply_reduce_fusion.6
  330.5 1.9 fusion.10
  332.4 2.0 collective-permute-start.40
  334.4 2.1 stem_rows.1
  336.5 2.6 all-to-all-start.2
  344.7 2.5 collective-permute-start.42
  349.3 1.9 fusion.49
  353.8 6.2 %all-to-all-done.2 = bf16[32,48,128]{2,1,0:T(8,128)(2,1)S(1)} async-done(((bf16[32,48,128]{2,1,0:T(8,128)(2,1)}), bf16[32,48,128]{2,1,0:T(8,128)(2,1)S(1)}, u32[]{:S(2)}, u32[]{:S(2)}) %all-to-all-start.2) | async-done | bytes 393248 | tf_op jit(solution)/shard_map/all_to_all | solution.py:158
  362.9 5.9 %reduce-scatter.2.cloned.1.call-done = bf16[1,128,512]{2,1,0:T(8,128)(2,1)} async-done(((bf16[32,128,512]{2,1,0:T(8,128)(2,1)}), bf16[1,128,512]{2,1,0:T(8,128)(2,1)}) %reduce-scatter.2.cloned.1.call-update) | async-done | bytes 131088 | tf_op jit(solution)/shard_map/reduce_scatter | solution.py:1474
  373.2 2.6 all-to-all-start.3
  377.9 13.5 %all-to-all-done.3 = bf16[32,64,128]{2,1,0:T(8,128)(2,1)S(1)} async-done(((bf16[32,64,128]{2,1,0:T(8,128)(2,1)}), bf16[32,64,128]{2,1,0:T(8,128)(2,1)S(1)}, u32[]{:S(2)}, u32[]{:S(2)}) %all-to-all-start.3) | async-done | bytes 524320 | tf_op jit(solution)/shard_map/all_to_all | solution.py:158
  396.8 2.0 bitcast_subtract_fusion.2
  (322 shorter events, 96.8 us)
Async XLA Ops:
  7.2 96.5 %all-gather.5.cloned.1.call-start = ((), (), s32[]{:S(2)}) async-start(), calls=%async_computation.6 | async-start | bytes 8650752 | tf_op jit(solution)/shard_map/all_gather | solution.py:1334
  12.0 156.4 %all-gather.7.cloned.1.call-start = ((), (), s32[]{:S(2)}) async-start(), calls=%async_computation.7 | async-start | bytes 4325376 | tf_op jit(solution)/shard_map/all_gather | solution.py:1334
  16.9 20.2 %collective-permute-start.1 = (bf16[512,128]{1,0:T(8,128)(2,1)S(1)}, bf16[512,128]{1,0:T(8,128)(2,1)S(1)}, u32[]{:S(2)}, u32[]{:S(2)}) collective-permute-start(bf16[512,128]{1,0:T(8,128)(2,1)S(1)} %bitcast.664), channel_id=1, source_target_pairs={{0,24},{4,28},{8,0},{12,4},{16,8},{20,12},{24,16},{28,20},{1,25},{... | collective-permute-start | bytes 393224 | tf_op jit(solution)/shard_map/ppermute | solution.py:61
  22.0 15.9 %collective-permute-start.2 = (bf16[512,128]{1,0:T(8,128)(2,1)S(1)}, bf16[512,128]{1,0:T(8,128)(2,1)S(1)}, u32[]{:S(2)}, u32[]{:S(2)}) collective-permute-start(bf16[512,128]{1,0:T(8,128)(2,1)S(1)} %bitcast.665), channel_id=1, source_target_pairs={{0,16},{4,20},{8,24},{12,28},{16,0},{20,4},{24,8},{28,12},{1,17},{... | collective-permute-start | bytes 393224 | tf_op jit(solution)/shard_map/ppermute | solution.py:61
  22.0 15.9 %collective-permute-start.3 = (bf16[512,128]{1,0:T(8,128)(2,1)S(1)}, bf16[512,128]{1,0:T(8,128)(2,1)S(1)}, u32[]{:S(2)}, u32[]{:S(2)}) collective-permute-start(bf16[512,128]{1,0:T(8,128)(2,1)S(1)} %bitcast.666), channel_id=1, source_target_pairs={{0,8},{4,12},{8,16},{12,20},{16,24},{20,28},{24,0},{28,4},{1,9},{5... | collective-permute-start | bytes 393224 | tf_op jit(solution)/shard_map/ppermute | solution.py:61
  24.1 5.2 %collective-permute-start = (bf16[8,80]{1,0:T(8,128)(2,1)S(1)}, bf16[8,80]{1,0:T(8,128)(2,1)S(1)}, u32[]{:S(2)}, u32[]{:S(2)}) collective-permute-start(bf16[8,80]{1,0:T(8,128)(2,1)S(1)} %slice.1081), channel_id=1, source_target_pairs={{0,1},{1,2},{2,3},{4,5},{5,6},{6,7},{8,9},{9,10},{10,11},{12,13},{... | collective-permute-start | bytes 3848 | tf_op jit(solution)/shard_map/ppermute | solution.py:164
  38.0 8.8 %collective-permute-start.4 = (bf16[4,256,128]{2,1,0:T(8,128)(2,1)S(1)}, bf16[4,256,128]{2,1,0:T(8,128)(2,1)S(1)}, u32[]{:S(2)}, u32[]{:S(2)}) collective-permute-start(bf16[4,256,128]{2,1,0:T(8,128)(2,1)S(1)} %get-tuple-element.86), channel_id=1, source_target_pairs={{0,2},{1,3},{2,0},{3,1},{4,6},{5,7},{6,4},{7,5},{8,10},{9,11},{10,... | collective-permute-start | bytes 786440 | tf_op jit(solution)/shard_map/ppermute | solution.py:61
  39.5 9.0 %collective-permute-start.6 = (bf16[4,256,128]{2,1,0:T(8,128)(2,1)S(1)}, bf16[4,256,128]{2,1,0:T(8,128)(2,1)S(1)}, u32[]{:S(2)}, u32[]{:S(2)}) collective-permute-start(bf16[4,256,128]{2,1,0:T(8,128)(2,1)S(1)} %get-tuple-element.87), channel_id=1, source_target_pairs={{0,4},{4,0},{8,12},{12,8},{16,20},{20,16},{24,28},{28,24},{1,5},{5... | collective-permute-start | bytes 786440 | tf_op jit(solution)/shard_map/ppermute | solution.py:61
  46.8 16.9 %collective-permute-start.5 = (bf16[2,4,256,128]{3,2,1,0:T(8,128)(2,1)S(1)}, bf16[2,4,256,128]{3,2,1,0:T(8,128)(2,1)S(1)}, u32[]{:S(2)}, u32[]{:S(2)}) collective-permute-start(bf16[2,4,256,128]{3,2,1,0:T(8,128)(2,1)S(1)} %get-tuple-element.201), channel_id=1, source_target_pairs={{0,4},{4,0},{8,12},{12,8},{16,20},{20,16},{24,28},{28,24},{1,5},{5... | collective-permute-start | bytes 1572872 | tf_op jit(solution)/shard_map/ppermute | solution.py:61
  48.6 18.8 %collective-permute-start.7 = (bf16[2,4,256,128]{3,2,1,0:T(8,128)(2,1)S(1)}, bf16[2,4,256,128]{3,2,1,0:T(8,128)(2,1)S(1)}, u32[]{:S(2)}, u32[]{:S(2)}) collective-permute-start(bf16[2,4,256,128]{3,2,1,0:T(8,128)(2,1)S(1)} %get-tuple-element.203), channel_id=1, source_target_pairs={{0,2},{1,3},{2,0},{3,1},{4,6},{5,7},{6,4},{7,5},{8,10},{9,11},{10,... | collective-permute-start | bytes 1572872 | tf_op jit(solution)/shard_map/ppermute | solution.py:61
  67.7 4.4 %collective-permute-start.8 = (bf16[2,16,256,128]{3,2,1,0:T(8,128)(2,1)S(1)}, bf16[2,16,256,128]{3,2,1,0:T(8,128)(2,1)}, u32[]{:S(2)}, u32[]{:S(2)}) collective-permute-start(bf16[2,16,256,128]{3,2,1,0:T(8,128)(2,1)S(1)} %pad_maximum_fusion.refs_1_), channel_id=1, source_target_pairs={{0,1},{1,0},{2,3},{3,2},{4,5},{5,4},{6,7},{7,6},{8,9},{9,8},{10,11... | collective-permute-start | bytes 6291464 | tf_op jit(solution)/shard_map/ppermute | solution.py:61
  108.5 7.3 %collective-permute-start.9 = (bf16[128,512]{1,0:T(8,128)(2,1)}, bf16[128,512]{1,0:T(8,128)(2,1)S(1)}, u32[]{:S(2)}, u32[]{:S(2)}) collective-permute-start(bf16[128,512]{1,0:T(8,128)(2,1)} %get-tuple-element.94.refs_2_.refs_7_), channel_id=1, source_target_pairs={{0,2},{1,3},{2,0},{3,1},{4,6},{5,7},{6,4},{7,5},{8,10},{9,11},{10,... | collective-permute-start | bytes 393224 | tf_op jit(solution)/shard_map/ppermute | solution.py:61
  131.3 3.4 collective-permute-start.12
  137.6 30.8 %all-to-all-start = ((f32[32,16,128]{2,1,0:T(8,128)}), f32[32,16,128]{2,1,0:T(8,128)S(1)}, u32[]{:S(2)}, u32[]{:S(2)}) async-start(f32[32,16,128]{2,1,0:T(8,128)} %get-tuple-element.103), calls=%async_computation | async-start | bytes 524288 | tf_op jit(solution)/shard_map/all_to_all | solution.py:158
  180.5 13.7 %all-to-all-start.1 = ((f32[32,16,128]{2,1,0:T(8,128)}), f32[32,16,128]{2,1,0:T(8,128)S(1)}, u32[]{:S(2)}, u32[]{:S(2)}) async-start(f32[32,16,128]{2,1,0:T(8,128)} %get-tuple-element.110), calls=%async_computation.1 | async-start | bytes 524288 | tf_op jit(solution)/shard_map/all_to_all | solution.py:158
  183.6 185.1 %reduce-scatter.2.cloned.1.call-start = ((), (), s32[]{:S(2)}) async-start(), calls=%async_computation.5 | async-start | bytes 4325376 | tf_op jit(solution)/shard_map/reduce_scatter | solution.py:1474
  183.7 4.3 %collective-permute-start.13 = (f32[16,512]{1,0:T(8,128)}, f32[16,512]{1,0:T(8,128)S(1)}, u32[]{:S(2)}, u32[]{:S(2)}) collective-permute-start(f32[16,512]{1,0:T(8,128)} %get-tuple-element.108), channel_id=1, source_target_pairs={{0,1},{1,2},{2,3},{4,5},{5,6},{6,7},{8,9},{9,10},{10,11},{12,13},{... | collective-permute-start | bytes 98312 | tf_op jit(solution)/shard_map/ppermute | solution.py:164
  185.8 4.4 %collective-permute-start.14 = (f32[16,512]{1,0:T(8,128)}, f32[16,512]{1,0:T(8,128)S(1)}, u32[]{:S(2)}, u32[]{:S(2)}) collective-permute-start(f32[16,512]{1,0:T(8,128)} %get-tuple-element.109), channel_id=1, source_target_pairs={{1,0},{2,1},{3,2},{5,4},{6,5},{7,6},{9,8},{10,9},{11,10},{13,12},{... | collective-permute-start | bytes 98312 | tf_op jit(solution)/shard_map/ppermute | solution.py:164
  216.2 7.4 %collective-permute-start.16 = (bf16[1,128,512]{2,1,0:T(8,128)(2,1)S(1)}, bf16[1,128,512]{2,1,0:T(8,128)(2,1)S(1)}, u32[]{:S(2)}, u32[]{:S(2)}) collective-permute-start(bf16[1,128,512]{2,1,0:T(8,128)(2,1)S(1)} %get-tuple-element.214), channel_id=1, source_target_pairs={{0,2},{1,3},{2,0},{3,1},{4,6},{5,7},{6,4},{7,5},{8,10},{9,11},{10,... | collective-permute-start | bytes 393224 | tf_op jit(solution)/shard_map/ppermute | solution.py:61
  223.0 10.6 %collective-permute-start.26 = (bf16[2,2,4,64,512]{4,3,2,1,0:T(8,128)(2,1)}, bf16[2,2,4,64,512]{4,3,2,1,0:T(8,128)(2,1)S(1)}, u32[]{:S(2)}, u32[]{:S(2)}) collective-permute-start(bf16[2,2,4,64,512]{4,3,2,1,0:T(8,128)(2,1)} %get-tuple-element.145), channel_id=1, source_target_pairs={{0,1},{1,0},{2,3},{3,2},{4,5},{5,4},{6,7},{7,6},{8,9},{9,8},{10,11... | collective-permute-start | bytes 3145736 | tf_op jit(solution)/shard_map/ppermute | solution.py:61
  223.1 12.9 %collective-permute-start.28 = (bf16[2,2,4,64,512]{4,3,2,1,0:T(8,128)(2,1)}, bf16[2,2,4,64,512]{4,3,2,1,0:T(8,128)(2,1)S(1)}, u32[]{:S(2)}, u32[]{:S(2)}) collective-permute-start(bf16[2,2,4,64,512]{4,3,2,1,0:T(8,128)(2,1)} %get-tuple-element.147), channel_id=1, source_target_pairs={{0,1},{1,0},{2,3},{3,2},{4,5},{5,4},{6,7},{7,6},{8,9},{9,8},{10,11... | collective-permute-start | bytes 3145736 | tf_op jit(solution)/shard_map/ppermute | solution.py:61
  233.0 11.5 %collective-permute-start.17 = (bf16[2,2,4,64,512]{4,3,2,1,0:T(8,128)(2,1)}, bf16[2,2,4,64,512]{4,3,2,1,0:T(8,128)(2,1)S(1)}, u32[]{:S(2)}, u32[]{:S(2)}) collective-permute-start(bf16[2,2,4,64,512]{4,3,2,1,0:T(8,128)(2,1)} %get-tuple-element.130), channel_id=1, source_target_pairs={{0,1},{1,0},{2,3},{3,2},{4,5},{5,4},{6,7},{7,6},{8,9},{9,8},{10,11... | collective-permute-start | bytes 3145736 | tf_op jit(solution)/shard_map/ppermute | solution.py:61
  233.2 12.8 %collective-permute-start.20 = (bf16[2,2,4,64,512]{4,3,2,1,0:T(8,128)(2,1)}, bf16[2,2,4,64,512]{4,3,2,1,0:T(8,128)(2,1)S(1)}, u32[]{:S(2)}, u32[]{:S(2)}) collective-permute-start(bf16[2,2,4,64,512]{4,3,2,1,0:T(8,128)(2,1)} %get-tuple-element.132), channel_id=1, source_target_pairs={{0,1},{1,0},{2,3},{3,2},{4,5},{5,4},{6,7},{7,6},{8,9},{9,8},{10,11... | collective-permute-start | bytes 3145736 | tf_op jit(solution)/shard_map/ppermute | solution.py:61
  234.6 40.7 %collective-permute-start.27 = (bf16[2,4,64,512]{3,2,1,0:T(8,128)(2,1)}, bf16[2,4,64,512]{3,2,1,0:T(8,128)(2,1)}, u32[]{:S(2)}, u32[]{:S(2)}) collective-permute-start(bf16[2,4,64,512]{3,2,1,0:T(8,128)(2,1)} %fusion.6.refs_4_), channel_id=1, source_target_pairs={{0,2},{1,3},{2,0},{3,1},{4,6},{5,7},{6,4},{7,5},{8,10},{9,11},{10,... | collective-permute-start | bytes 1572872 | tf_op jit(solution)/shard_map/ppermute | solution.py:61
  237.1 40.3 %collective-permute-start.29 = (bf16[2,4,64,512]{3,2,1,0:T(8,128)(2,1)}, bf16[2,4,64,512]{3,2,1,0:T(8,128)(2,1)}, u32[]{:S(2)}, u32[]{:S(2)}) collective-permute-start(bf16[2,4,64,512]{3,2,1,0:T(8,128)(2,1)} %fusion.7.refs_5_), channel_id=1, source_target_pairs={{0,4},{4,0},{8,12},{12,8},{16,20},{20,16},{24,28},{28,24},{1,5},{5... | collective-permute-start | bytes 1572872 | tf_op jit(solution)/shard_map/ppermute | solution.py:61
  244.5 68.2 %collective-permute-start.30 = (bf16[2,2,4,256,128]{4,3,2,1,0:T(8,128)(2,1)}, bf16[2,2,4,256,128]{4,3,2,1,0:T(8,128)(2,1)S(1)}, u32[]{:S(2)}, u32[]{:S(2)}) collective-permute-start(bf16[2,2,4,256,128]{4,3,2,1,0:T(8,128)(2,1)} %get-tuple-element.150), channel_id=1, source_target_pairs={{0,1},{1,0},{2,3},{3,2},{4,5},{5,4},{6,7},{7,6},{8,9},{9,8},{10,11... | collective-permute-start | bytes 3145736 | tf_op jit(solution)/shard_map/ppermute | solution.py:61
  244.5 68.7 %collective-permute-start.31 = (bf16[2,2,4,256,128]{4,3,2,1,0:T(8,128)(2,1)}, bf16[2,2,4,256,128]{4,3,2,1,0:T(8,128)(2,1)}, u32[]{:S(2)}, u32[]{:S(2)}) collective-permute-start(bf16[2,2,4,256,128]{4,3,2,1,0:T(8,128)(2,1)} %get-tuple-element.152), channel_id=1, source_target_pairs={{0,1},{1,0},{2,3},{3,2},{4,5},{5,4},{6,7},{7,6},{8,9},{9,8},{10,11... | collective-permute-start | bytes 3145736 | tf_op jit(solution)/shard_map/ppermute | solution.py:61
  246.0 33.8 %collective-permute-start.18 = (bf16[2,4,64,512]{3,2,1,0:T(8,128)(2,1)}, bf16[2,4,64,512]{3,2,1,0:T(8,128)(2,1)S(1)}, u32[]{:S(2)}, u32[]{:S(2)}) collective-permute-start(bf16[2,4,64,512]{3,2,1,0:T(8,128)(2,1)} %fusion.4.refs_10_), channel_id=1, source_target_pairs={{0,2},{1,3},{2,0},{3,1},{4,6},{5,7},{6,4},{7,5},{8,10},{9,11},{10,... | collective-permute-start | bytes 1572872 | tf_op jit(solution)/shard_map/ppermute | solution.py:61
  275.3 17.2 %collective-permute-start.21 = (bf16[2,4,64,512]{3,2,1,0:T(8,128)(2,1)}, bf16[2,4,64,512]{3,2,1,0:T(8,128)(2,1)S(1)}, u32[]{:S(2)}, u32[]{:S(2)}) collective-permute-start(bf16[2,4,64,512]{3,2,1,0:T(8,128)(2,1)} %fusion.5.refs_11_), channel_id=1, source_target_pairs={{0,4},{4,0},{8,12},{12,8},{16,20},{20,16},{24,28},{28,24},{1,5},{5... | collective-permute-start | bytes 1572872 | tf_op jit(solution)/shard_map/ppermute | solution.py:61
  277.4 22.1 %collective-permute-start.32 = (bf16[4,64,512]{2,1,0:T(8,128)(2,1)S(1)}, bf16[4,64,512]{2,1,0:T(8,128)(2,1)S(1)}, u32[]{:S(2)}, u32[]{:S(2)}) collective-permute-start(bf16[4,64,512]{2,1,0:T(8,128)(2,1)S(1)} %fusion.13.refs_7_), channel_id=1, source_target_pairs={{0,4},{4,0},{8,12},{12,8},{16,20},{20,16},{24,28},{28,24},{1,5},{5... | collective-permute-start | bytes 786440 | tf_op jit(solution)/shard_map/ppermute | solution.py:61
  279.8 22.5 %collective-permute-start.33 = (bf16[4,64,512]{2,1,0:T(8,128)(2,1)S(1)}, bf16[4,64,512]{2,1,0:T(8,128)(2,1)S(1)}, u32[]{:S(2)}, u32[]{:S(2)}) collective-permute-start(bf16[4,64,512]{2,1,0:T(8,128)(2,1)S(1)} %fusion.12.refs_8_), channel_id=1, source_target_pairs={{0,2},{1,3},{2,0},{3,1},{4,6},{5,7},{6,4},{7,5},{8,10},{9,11},{10,... | collective-permute-start | bytes 786440 | tf_op jit(solution)/shard_map/ppermute | solution.py:61
  292.5 12.7 %collective-permute-start.19 = (bf16[4,64,512]{2,1,0:T(8,128)(2,1)S(1)}, bf16[4,64,512]{2,1,0:T(8,128)(2,1)S(1)}, u32[]{:S(2)}, u32[]{:S(2)}) collective-permute-start(bf16[4,64,512]{2,1,0:T(8,128)(2,1)S(1)} %fusion.15.refs_9_), channel_id=1, source_target_pairs={{0,4},{4,0},{8,12},{12,8},{16,20},{20,16},{24,28},{28,24},{1,5},{5... | collective-permute-start | bytes 786440 | tf_op jit(solution)/shard_map/ppermute | solution.py:61
  299.5 9.2 %collective-permute-start.22 = (bf16[4,64,512]{2,1,0:T(8,128)(2,1)S(1)}, bf16[4,64,512]{2,1,0:T(8,128)(2,1)S(1)}, u32[]{:S(2)}, u32[]{:S(2)}) collective-permute-start(bf16[4,64,512]{2,1,0:T(8,128)(2,1)S(1)} %fusion.14.refs_10_), channel_id=1, source_target_pairs={{0,2},{1,3},{2,0},{3,1},{4,6},{5,7},{6,4},{7,5},{8,10},{9,11},{10,... | collective-permute-start | bytes 786440 | tf_op jit(solution)/shard_map/ppermute | solution.py:61
  303.5 12.1 %collective-permute-start.34 = (bf16[2,64,512]{2,1,0:T(8,128)(2,1)S(1)}, bf16[2,64,512]{2,1,0:T(8,128)(2,1)S(1)}, u32[]{:S(2)}, u32[]{:S(2)}) collective-permute-start(bf16[2,64,512]{2,1,0:T(8,128)(2,1)S(1)} %pad_maximum_fusion.16), channel_id=1, source_target_pairs={{0,8},{4,12},{8,16},{12,20},{16,24},{20,28},{24,0},{28,4},{1,9},{5... | collective-permute-start | bytes 393224 | tf_op jit(solution)/shard_map/ppermute | solution.py:61
  305.2 11.7 %collective-permute-start.35 = (bf16[2,64,512]{2,1,0:T(8,128)(2,1)S(1)}, bf16[2,64,512]{2,1,0:T(8,128)(2,1)S(1)}, u32[]{:S(2)}, u32[]{:S(2)}) collective-permute-start(bf16[2,64,512]{2,1,0:T(8,128)(2,1)S(1)} %pad_maximum_fusion.17), channel_id=1, source_target_pairs={{0,16},{4,20},{8,24},{12,28},{16,0},{20,4},{24,8},{28,12},{1,17},{... | collective-permute-start | bytes 393224 | tf_op jit(solution)/shard_map/ppermute | solution.py:61
  308.7 10.8 %collective-permute-start.36 = (bf16[2,64,512]{2,1,0:T(8,128)(2,1)S(1)}, bf16[2,64,512]{2,1,0:T(8,128)(2,1)S(1)}, u32[]{:S(2)}, u32[]{:S(2)}) collective-permute-start(bf16[2,64,512]{2,1,0:T(8,128)(2,1)S(1)} %pad_maximum_fusion.18), channel_id=1, source_target_pairs={{0,24},{4,28},{8,0},{12,4},{16,8},{20,12},{24,16},{28,20},{1,25},{... | collective-permute-start | bytes 393224 | tf_op jit(solution)/shard_map/ppermute | solution.py:61
  312.9 15.7 %collective-permute-start.37 = (bf16[2,4,256,128]{3,2,1,0:T(8,128)(2,1)S(1)}, bf16[2,4,256,128]{3,2,1,0:T(8,128)(2,1)S(1)}, u32[]{:S(2)}, u32[]{:S(2)}) collective-permute-start(bf16[2,4,256,128]{3,2,1,0:T(8,128)(2,1)S(1)} %fusion.8.refs_11_), channel_id=1, source_target_pairs={{0,2},{1,3},{2,0},{3,1},{4,6},{5,7},{6,4},{7,5},{8,10},{9,11},{10,... | collective-permute-start | bytes 1572872 | tf_op jit(solution)/shard_map/ppermute | solution.py:61
  314.4 16.1 %collective-permute-start.39 = (bf16[2,4,256,128]{3,2,1,0:T(8,128)(2,1)S(1)}, bf16[2,4,256,128]{3,2,1,0:T(8,128)(2,1)S(1)}, u32[]{:S(2)}, u32[]{:S(2)}) collective-permute-start(bf16[2,4,256,128]{3,2,1,0:T(8,128)(2,1)S(1)} %fusion.9.refs_12_), channel_id=1, source_target_pairs={{0,4},{4,0},{8,12},{12,8},{16,20},{20,16},{24,28},{28,24},{1,5},{5... | collective-permute-start | bytes 1572872 | tf_op jit(solution)/shard_map/ppermute | solution.py:61
  315.6 32.2 %collective-permute-start.23 = (bf16[2,64,512]{2,1,0:T(8,128)(2,1)}, bf16[2,64,512]{2,1,0:T(8,128)(2,1)}, u32[]{:S(2)}, u32[]{:S(2)}) collective-permute-start(bf16[2,64,512]{2,1,0:T(8,128)(2,1)} %pad_maximum_fusion.13), channel_id=1, source_target_pairs={{0,8},{4,12},{8,16},{12,20},{16,24},{20,28},{24,0},{28,4},{1,9},{5... | collective-permute-start | bytes 393224 | tf_op jit(solution)/shard_map/ppermute | solution.py:61
  316.9 32.4 %collective-permute-start.24 = (bf16[2,64,512]{2,1,0:T(8,128)(2,1)}, bf16[2,64,512]{2,1,0:T(8,128)(2,1)}, u32[]{:S(2)}, u32[]{:S(2)}) collective-permute-start(bf16[2,64,512]{2,1,0:T(8,128)(2,1)} %pad_maximum_fusion.14), channel_id=1, source_target_pairs={{0,16},{4,20},{8,24},{12,28},{16,0},{20,4},{24,8},{28,12},{1,17},{... | collective-permute-start | bytes 393224 | tf_op jit(solution)/shard_map/ppermute | solution.py:61
  319.5 29.8 %collective-permute-start.25 = (bf16[2,64,512]{2,1,0:T(8,128)(2,1)}, bf16[2,64,512]{2,1,0:T(8,128)(2,1)}, u32[]{:S(2)}, u32[]{:S(2)}) collective-permute-start(bf16[2,64,512]{2,1,0:T(8,128)(2,1)} %pad_maximum_fusion.15), channel_id=1, source_target_pairs={{0,24},{4,28},{8,0},{12,4},{16,8},{20,12},{24,16},{28,20},{1,25},{... | collective-permute-start | bytes 393224 | tf_op jit(solution)/shard_map/ppermute | solution.py:61
  329.5 9.6 %collective-permute-start.38 = (bf16[4,256,128]{2,1,0:T(8,128)(2,1)}, bf16[4,256,128]{2,1,0:T(8,128)(2,1)}, u32[]{:S(2)}, u32[]{:S(2)}) collective-permute-start(bf16[4,256,128]{2,1,0:T(8,128)(2,1)} %fusion.11), channel_id=1, source_target_pairs={{0,4},{4,0},{8,12},{12,8},{16,20},{20,16},{24,28},{28,24},{1,5},{5... | collective-permute-start | bytes 786440 | tf_op jit(solution)/shard_map/ppermute | solution.py:61
  332.4 9.1 %collective-permute-start.40 = (bf16[4,256,128]{2,1,0:T(8,128)(2,1)}, bf16[4,256,128]{2,1,0:T(8,128)(2,1)}, u32[]{:S(2)}, u32[]{:S(2)}) collective-permute-start(bf16[4,256,128]{2,1,0:T(8,128)(2,1)} %fusion.10), channel_id=1, source_target_pairs={{0,2},{1,3},{2,0},{3,1},{4,6},{5,7},{6,4},{7,5},{8,10},{9,11},{10,... | collective-permute-start | bytes 786440 | tf_op jit(solution)/shard_map/ppermute | solution.py:61
  336.5 23.5 %all-to-all-start.2 = ((bf16[32,48,128]{2,1,0:T(8,128)(2,1)}), bf16[32,48,128]{2,1,0:T(8,128)(2,1)S(1)}, u32[]{:S(2)}, u32[]{:S(2)}) async-start(bf16[32,48,128]{2,1,0:T(8,128)(2,1)} %bitcast.669), calls=%async_computation.3 | async-start | bytes 786432 | tf_op jit(solution)/shard_map/all_to_all | solution.py:158
  343.5 16.6 %collective-permute-start.41 = (bf16[2,256,128]{2,1,0:T(8,128)(2,1)}, bf16[2,256,128]{2,1,0:T(8,128)(2,1)}, u32[]{:S(2)}, u32[]{:S(2)}) collective-permute-start(bf16[2,256,128]{2,1,0:T(8,128)(2,1)} %pad_maximum_fusion.19), channel_id=1, source_target_pairs={{0,8},{4,12},{8,16},{12,20},{16,24},{20,28},{24,0},{28,4},{1,9},{5... | collective-permute-start | bytes 393224 | tf_op jit(solution)/shard_map/ppermute | solution.py:61
  344.7 16.1 %collective-permute-start.42 = (bf16[2,256,128]{2,1,0:T(8,128)(2,1)}, bf16[2,256,128]{2,1,0:T(8,128)(2,1)}, u32[]{:S(2)}, u32[]{:S(2)}) collective-permute-start(bf16[2,256,128]{2,1,0:T(8,128)(2,1)} %pad_maximum_fusion.20), channel_id=1, source_target_pairs={{0,16},{4,20},{8,24},{12,28},{16,0},{20,4},{24,8},{28,12},{1,17},{... | collective-permute-start | bytes 393224 | tf_op jit(solution)/shard_map/ppermute | solution.py:61
  347.8 12.9 %collective-permute-start.43 = (bf16[2,256,128]{2,1,0:T(8,128)(2,1)}, bf16[2,256,128]{2,1,0:T(8,128)(2,1)}, u32[]{:S(2)}, u32[]{:S(2)}) collective-permute-start(bf16[2,256,128]{2,1,0:T(8,128)(2,1)} %pad_maximum_fusion.21), channel_id=1, source_target_pairs={{0,24},{4,28},{8,0},{12,4},{16,8},{20,12},{24,16},{28,20},{1,25},{... | collective-permute-start | bytes 393224 | tf_op jit(solution)/shard_map/ppermute | solution.py:61
  373.2 18.2 %all-to-all-start.3 = ((bf16[32,64,128]{2,1,0:T(8,128)(2,1)}), bf16[32,64,128]{2,1,0:T(8,128)(2,1)S(1)}, u32[]{:S(2)}, u32[]{:S(2)}) async-start(bf16[32,64,128]{2,1,0:T(8,128)(2,1)} %broadcast_in_dim.85), calls=%async_computation.4 | async-start | bytes 1048576 | tf_op jit(solution)/shard_map/all_to_all | solution.py:158
  (52 other events, 497.3 us)
Sparse Core Ops, SparseCore 0:
  12.1 91.4 all-gather.4
  107.1 61.2 all-gather.6
  223.3 145.4 reduce-scatter.1

commit v2 on v1

--- a/solution.py
+++ b/solution.py
@@ -61,6 +61,10 @@
     return lax.ppermute(x, axis, pairs)
 
 
+def held(values, others):
+    return lax.optimization_barrier((values, others))[0] if others else values
+
+
 def total(*parts):
     return functools.reduce(lambda a, b: a + b, [part.astype(f32) for part in parts])
 
@@ -113,6 +117,37 @@
         ]
 
 
+class ReducedOneWay:
+    def __init__(self, keep, send, axes):
+        self.keep, self.out, self.axes = keep, send, axes
+
+    def side(self, array, *index):
+        index = dict(zip(self.axes, index))
+        return array[tuple(index.get(axis, slice(None)) for axis in "xy")]
+
+    def cores(self):
+        self.got = sent(self.out, "c")
+        self.out = low_total(self.side(self.keep, 1), self.side(self.got, 1))
+        return [self.out]
+
+    def first(self):
+        self.more = sent(self.out, self.axes[0])
+        self.out = low_total(self.side(self.keep, 0, 1), self.side(self.got, 0, 1), self.more[1])
+        return [self.out]
+
+    def second(self):
+        last = sent(self.out, self.axes[1])
+        self.parts = self.side(self.keep, 0, 0), self.side(self.got, 0, 0), self.more[0], last
+        self.out = [low_total(*[x[k] for x in self.parts]) for k in range(1, last.shape[0])]
+        return self.out
+
+    def lines(self):
+        got = [sent(x, "z", k + 1) for k, x in enumerate(self.out)]
+        own = total(*[x[0] for x in self.parts], *got)
+        rows = own.shape[0] // 2
+        return [own[:rows], own[rows:]]
+
+
 class Gathered:
     def __init__(self, low):
         self.low = low
@@ -152,6 +187,22 @@
         both = lax.psum_scatter(both, "dp", scatter_dimension=1, tiled=True)
         own.append(both.reshape(own_rows, keep.shape[-1]).astype(f32))
     return own
+
+
+def reduced_cores(keep, send, plan):
+    if plan:
+        both = low_total(keep, sent(send, "c"))
+        ndev = lax.axis_size("dp") * lax.axis_size("mp")
+        groups = [list(range(core, ndev, CORES)) for core in range(CORES)]
+        both = both.reshape(ndev // CORES, 2, *both.shape[3:])
+        own = lax.psum_scatter(
+            both, ("dp", "mp"), scatter_dimension=0, axis_index_groups=groups, tiled=True
+        )
+        return [both], own
+    both = jnp.stack([keep, send], 2)[0].reshape(lax.axis_size("mp"), 2, lax.axis_size("dp"), -1, D)
+    both = lax.psum_scatter(both, "mp", scatter_dimension=0, tiled=True)
+    both = lax.psum_scatter(both, "dp", scatter_dimension=2, tiled=True)
+    return (), both
 
 
 def spread(x):
@@ -223,27 +274,31 @@
 def pieces(spot):
     for c in range(CORES):
         for x in range(COLS):
-            if spot is None:
-                yield c, x, x * CORES + c
-                continue
             yield c, x, ((spot[1] + x) % COLS) * CORES + (spot[0] + c) % CORES
 
 
-def write_whole(to, half, m, grad):
+def core_pieces(spot):
+    for c in range(CORES):
+        for x in range(COLS):
+            yield c, x, x * CORES + (spot[0] + c) % CORES
+
+
+def write_core_piece(to, x, half, grad):
     rows = to.shape[3]
+    grad = grad.astype(bf16)
     for k in range(to.shape[0]):
-        to[k, m, half] = grad[rows * k : rows * k + rows].astype(bf16)
-
-
-def write_piece(spot, parts, half, c, x, grad):
-    to = parts[half + 2 * c]
-    _, deep, lines, _, _ = to.shape
-    rows = D // (lines * deep)
+        to[k, x, half] = grad[rows * k : rows * k + rows]
+
+
+def write_piece(spot, to, half, x, grad):
+    _, deep, lines, rows, _ = to.shape
+    rows = rows // 2
     grad = grad.astype(bf16)
     for z in range(lines):
         for y in range(deep):
             at = (z * deep + y) * rows
-            to[x, (y + deep - spot[2]) % deep, (z + lines - spot[3]) % lines] = grad[at : at + rows]
+            index = x, (y + deep - spot[2]) % deep, (z + lines - spot[3]) % lines
+            to[(*index, slice(rows * half, rows * half + rows))] = grad[at : at + rows]
 
 
 def nn(left, right):
@@ -371,7 +426,7 @@
 
 
 def pack_kernel(shard, n_dp, spot, last_ref, dx_ref, dhead_ref, *refs):
-    parts, flat = refs[:4], refs[4]
+    outs, flat, parts, sem = refs[:4], refs[4], refs[5], refs[6]
     dx = dx_ref[...]
     flat[0 : ROW_AT[2], :] = jnp.zeros((ROW_AT[2], LANES), f32)
     flat[ROW_AT[4] :, :] = jnp.zeros((flat.shape[0] - ROW_AT[4], LANES), f32)
@@ -384,14 +439,15 @@
     for q in range(D // LANES):
         at = ROW_AT[3] + 1025 * q
         turned = pltpu.roll(
-            dhead_ref[LANES * q : LANES * q + LANES, :], 0, 1, stride=1, stride_axis=0
+            dhead_ref[LANES * q : LANES * q + LANES, :].astype(f32), 0, 1, stride=1, stride_axis=0
         )
         flat[pl.ds(at + 8, LANES, stride=8), :] = turned[:, 8 * LANES :]
         flat[at : at + 1, :] = turned[0:1, 0:LANES]
         flat[pl.ds(at + 8, LANES - 1, stride=8), :] += turned[1:, 0:LANES]
         for c in range(1, 8):
             flat[pl.ds(at + c, LANES, stride=8), :] = turned[:, LANES * c : LANES * c + LANES]
-    _, deep, lines, rows, _ = parts[0].shape
+    _, _, deep, lines, rows, _ = parts.shape
+    copies = []
     each = n_dp // (deep * lines)
     rows = rows // each
     for c in range(CORES):
@@ -404,10 +460,16 @@
             row = first_row(shard, dp * (COLS * CORES) + mp)
             for half in range(2):
                 part = flat[rows_at(row + rows * half, rows), :]
-                parts[half + 2 * c][x, y, z, rows_at(rows * k, rows), :] = part.astype(bf16)
+                parts[half + 2 * c, x, y, z, rows_at(rows * k, rows), :] = part.astype(bf16)
             return carry
 
         lax.fori_loop(0, COLS * deep * lines * each, step, 0)
+        for half in range(2):
+            part = half + 2 * c
+            copies.append(pltpu.make_async_copy(parts.at[part], outs[part], sem.at[part]))
+            copies[-1].start()
+    for copy in copies:
+        copy.wait()
 
 
 def stem_chunks(rows):
@@ -766,22 +828,15 @@
     return x + 0.5 * total
 
 
-def ffn_backward(spot, grad, x, vec_ref, which, in_buf, out_buf, pre_ref, normed_ref, parts):
+def ffn_backward(grad, x, vec_ref, which, in_buf, out_buf, pre_ref, normed_ref, order, write):
     low = (0.5 * grad).astype(bf16)
     back = jnp.zeros_like(x)
-    for c, col, m in pieces(spot):
-
-        def write(half, piece):
-            if spot is None:
-                write_whole(parts, half, m, piece)
-            else:
-                write_piece(spot, parts, half, c, col, piece)
-
+    for c, col, m in order:
         pre = pre_ref[m]
         sig = sigmoid(pre)
-        write(1, tn(low, (pre * sig).astype(bf16)))
+        write(c, col, 1, tn(low, (pre * sig).astype(bf16)))
         g_pre = (nn(low, block(out_buf, m)) * (sig * (1.0 + pre * (1.0 - sig)))).astype(bf16)
-        write(0, tn(normed_ref[...], g_pre))
+        write(c, col, 0, tn(normed_ref[...], g_pre))
         back += nt(g_pre, block(in_buf, m))
     dx, gain, shift = layer_norm_back(x, vec_ref[which : which + 1, :], back)
     return grad + dx, gain, shift
@@ -921,6 +976,7 @@
 
 
 def middle_kernel(
+    spot,
     weights,
     more,
     hidden_ref,
@@ -931,7 +987,8 @@
     label_ref,
     weight_ref,
     valid_ref,
-    grad_ref,
+    keep_ref,
+    send_ref,
     g_head_ref,
     dx3_ref,
     act_ref,
@@ -980,12 +1037,21 @@
     loss = jnp.sum(weight * (total - picked), 0, keepdims=True)
     g_logits = (jnp.exp(logits - total) - hit.astype(f32)) * (weight / count)
     g_logits = g_logits.astype(bf16)
-    g_head_ref[...] = tn(normed, g_logits)
+    g_head_ref[...] = tn(normed, g_logits).astype(bf16)
     dx4, gain, shift = layer_norm_back(x4, vec_ref[4:5, :], nt(g_logits, head_ref[...]))
     vgrad_ref[0:1, :] = gain
     vgrad_ref[1:2, :] = shift
     dx3, gain, shift = ffn_backward(
-        None, dx4, x3, vec_ref, 3, in_buf, out_buf, pre_ref, n4_ref, grad_ref
+        dx4,
+        x3,
+        vec_ref,
+        3,
+        in_buf,
+        out_buf,
+        pre_ref,
+        n4_ref,
+        core_pieces(spot),
+        lambda c, *place: write_core_piece((keep_ref, send_ref)[c], *place),
     )
     vgrad_ref[2:3, :] = gain
     vgrad_ref[3:4, :] = shift
@@ -1177,13 +1243,13 @@
             tn(all_ref[...], dkv_ref[m]),
             tn(table_ref[...], dpe_ref[:, lanes]),
         ]
-        write_piece(spot, parts, 0, c, x, jnp.concatenate(grads, 1))
+        write_piece(spot, parts[c], 0, x, jnp.concatenate(grads, 1))
         grads = [
             tn(n3_ref[...], dgate_ref[m]),
             tn(low, att_ref[:, lanes]),
             tn(low_three, act_ref[:, lanes]),
         ]
-        write_piece(spot, parts, 1, c, x, jnp.concatenate(grads, 1))
+        write_piece(spot, parts[c], 1, x, jnp.concatenate(grads, 1))
 
 
 def last_kernel(
@@ -1197,10 +1263,8 @@
     pre_ref,
     n1_ref,
     vec_ref,
-    a_ref,
-    b_ref,
-    a_send_ref,
-    b_send_ref,
+    keep_ref,
+    send_ref,
     dx0_ref,
     vgrad_ref,
     in_buf,
@@ -1217,7 +1281,6 @@
     for copy in copies:
         copy.wait()
     dx0, gain, shift = ffn_backward(
-        spot,
         dx2_ref[...] + dx,
         x0_ref[...],
         vec_ref,
@@ -1226,7 +1289,8 @@
         out_buf,
         pre_ref,
         n1_ref,
-        (a_ref, b_ref, a_send_ref, b_send_ref),
+        pieces(spot),
+        lambda c, x, half, grad: write_piece(spot, (keep_ref, send_ref)[c], half, x, grad),
     )
     vgrad_ref[2:3, :] = gain
     vgrad_ref[3:4, :] = shift
@@ -1444,11 +1508,11 @@
         name="conv",
     )
     stat = spread(stat)
-    two, g_head, dx3, act, dy, yhat, b_low, b_high, part, vg_mid = call(
+    two_keep, two_send, g_head, dx3, act, dy, yhat, b_low, b_high, part, vg_mid = call(
         middle_kernel,
         [
-            ((n_dp if plan else 1, n_mp, 2, own_rows if plan else D, D), bf16),
-            ((D, CPAD), f32),
+            *[((n_dp if plan else 1, COLS, 2, own_rows if plan else D, D), bf16)] * 2,
+            ((D, CPAD), bf16),
             ((tokens, D), f32),
             ((tokens, D), bf16),
             ((tokens, D), f32),
@@ -1458,7 +1522,7 @@
             stat_shape,
             ((6, D), f32),
         ],
-        [weights, more, hidden, stat, x2, head, vec, alignment[0][:, None], weight, valid],
+        [spot, weights, more, hidden, stat, x2, head, vec, alignment[0][:, None], weight, valid],
         [
             pltpu.VMEM((n_mp, tokens, D), f32),
             pltpu.VMEM((tokens, D), bf16),
@@ -1469,12 +1533,7 @@
     )
     b_prev, b_next = passed_along(b_high, 1), passed_along(b_low, -1)
     part = spread(part)
-    if not plan:
-        two = two.reshape(n_mp, 2, n_dp, own_rows, D).transpose(2, 0, 1, 3, 4)
-    two = lax.psum_scatter(
-        two.reshape(ndev, 2 * own_rows, D), ("dp", "mp"), scatter_dimension=0, tiled=True
-    )
-    own_in_two, own_out_two = two.reshape(2, own_rows, D).astype(f32)
+    two_both, own_two = reduced_cores(two_keep, two_send, plan)
     dgate, dx2, vg_conv, loss = call(
         conv_back_kernel,
         [
@@ -1518,6 +1577,7 @@
         [weights, dx2, prob, kv, qu, qv, pe],
         [pltpu.VMEM((2 * tokens, D), f32), *buffers(big_all, LANES, 3 * LANES)],
         us=10,
+        after=two_both,
         name="back",
     )
     if plan:
@@ -1533,30 +1593,36 @@
     else:
         d_mine = lax.psum_scatter(d_all, "mp", scatter_dimension=0, tiled=True)[None]
         wait = ()
+    one_way = [((COLS, deep, lines, 2 * piece_rows, D), bf16)] * 2
     mix = call(
         mix_grad_kernel,
-        split(piece_rows),
+        one_way,
         [spot, dx2, dx3, dgate, n3, act, att, n2, n_all, table, dquery, dkv, dpe],
         us=7,
         after=wait,
         name="mix_grad",
     )
-    mix_sum = Reduced(*mix)
+    mix_sum = ReducedOneWay(*mix, "xy")
     *one, dx0, vg_last = call(
         last_kernel,
-        [*split(piece_rows), ((tokens, D), bf16), ((4, D), f32)],
+        [*one_way, ((tokens, D), bf16), ((4, D), f32)],
         [spot, weights, dx2, d_mine, d_own, x1, x0, pre_one, n1, vec],
         buffers(big_all, D, D),
         us=8,
         after=mix[:1],
         name="last",
     )
-    one_sum = Reduced(*one)
+    one_sum = ReducedOneWay(*one, "yx")
     few_parts = call(
         functools.partial(pack_kernel, shard, n_dp),
         [((COLS, deep, lines, small_rows, LANES), bf16)] * 4,
         [spot, last, dx0, g_head],
-        [pltpu.VMEM((flat_rows, LANES), f32)],
+        [
+            pltpu.VMEM((flat_rows, LANES), f32),
+            pltpu.VMEM((4, COLS, deep, lines, small_rows, LANES), bf16),
+            pltpu.SemaphoreType.DMA((4,)),
+        ],
+        out_any=(0, 1, 2, 3),
         us=5,
         after=mix_sum.cores() if plan else (),
         name="pack",
@@ -1608,11 +1674,16 @@
         few_sum.second()
         own_few = few_sum.lines()
     else:
-        own_mix, own_abo = reduced_whole(mix, own_rows)
-        own_in_one, own_out_one = reduced_whole(one, own_rows)
+
+        def halves(keep, send):
+            return [x[..., D * k : D * k + D, :] for x in (keep, send) for k in range(2)]
+
+        own_mix, own_abo = reduced_whole(halves(*mix), own_rows)
+        own_in_one, own_out_one = reduced_whole(halves(*one), own_rows)
         own_few = reduced_whole(few_parts, half)
     own_chunk = jnp.concatenate(own_few, 0)
 
+    own_in_two, own_out_two = held(own_two, [few]).reshape(2, own_rows, D).astype(f32)
     start = shard * device
     positions = start + jnp.arange(shard, dtype=jnp.int32)
     own = [own_in_one, own_out_one, own_mix, own_abo, own_in_two, own_out_two]
@@ -1632,13 +1703,15 @@
     grad_norm = jnp.sqrt(total_sq)
     factor = clip_norm / jnp.maximum(grad_norm, clip_norm)
 
-    gap = jnp.zeros((chunk, LANES), f32)
-    def window(part, at):
-        padded = jnp.concatenate([gap, part, gap], 0)
-        where = jnp.clip(row - at + chunk, 0, chunk + part.shape[0])
-        return lax.dynamic_slice_in_dim(padded, where, chunk, 0)
-
-    own_chunk = own_chunk + window(few[: ROW_AT[2]], 0) + window(few[ROW_AT[2] : used], ROW_AT[4])
+    rows_of = row + jnp.arange(chunk, dtype=jnp.int32)[:, None]
+    few = jnp.concatenate([few, jnp.zeros((chunk, LANES), f32)], 0)
+
+    def window(begin, end, at):
+        start_at = jnp.clip(row - begin + at, 0, few.shape[0] - chunk)
+        part = lax.dynamic_slice_in_dim(few, start_at, chunk, 0)
+        return jnp.where((rows_of >= begin) & (rows_of < end), part, 0.0)
+
+    own_chunk = own_chunk + window(0, ROW_AT[2], 0) + window(ROW_AT[4], NROWS, ROW_AT[2])
     own_small = lax.dynamic_slice_in_dim(own_chunk.reshape(-1), offset, shard, 0)
 
     grad_in = jnp.stack([own_in_one, own_in_two])

time: 417 us -> 408 us (0.978)
    ppermute x39 -> x34, starting transfers between devices: 48.5 us -> 39 us  [sent(): return lax.ppermute(x, axis, pairs)]
    ppermute x39 -> x34, waiting for transfers between devices: 49.2 us -> 56.9 us  [sent(): return lax.ppermute(x, axis, pairs)]
    reduce_scatter x1, waiting for transfers between devices: 5.87 us -> 0.02 us  [reduced_cores(): lax.psum_scatter(both, ('dp', 'mp'), scatter_dimension=0, axis_index_grou...]
    all_to_all x4, starting transfers between devices: 14.3 us -> 19.7 us  [spread(): return lax.all_to_all(x, ('dp', 'mp'), 0, 0, tiled=True)]
    convert_element_type x19 -> x14, other arithmetic: 16.8 us -> 21.6 us  [low_total(): return total(*parts).astype(bf16)]
    all_to_all x4, waiting for transfers between devices: 23.6 us -> 19.4 us  [spread(): return lax.all_to_all(x, ('dp', 'mp'), 0, 0, tiled=True)]
  transfers between devices with their start and end apart: 51 -> 46, of which waited for: 21 -> 19; matrix products, arithmetic and copies ran while one was open for 13% -> 12% of each run, Pallas kernels for 24% -> 25%
where the time goes in v2:
time: 408 us; the launch traced here: 403 us
  Pallas kernels  126 us (31%)
  waiting for transfers between devices  113 us (28%)
  starting transfers between devices  67.3 us (16%)
  other arithmetic  49.6 us (12%)
  local copies, waits for them, and re-layouts  24.6 us (6%)
  between operations  23.1 us (6%)
    pallas_call x14, Pallas kernels, call(): pl.pallas_call(run, out_shape=[jax.ShapeDtypeStruct(shape, dtype) for sha...  126 us
    ppermute x34, waiting for transfers between devices, sent(): return lax.ppermute(x, axis, pairs)  56.9 us
    ppermute x34, starting transfers between devices, sent(): return lax.ppermute(x, axis, pairs)  39 us
    all_gather x2, waiting for transfers between devices, gathered(): whole = lax.all_gather(jnp.stack(low), ('dp', 'mp'), axis=0)  31.7 us
    convert_element_type x14, other arithmetic, low_total(): return total(*parts).astype(bf16)  21.6 us
    all_to_all x4, starting transfers between devices, spread(): return lax.all_to_all(x, ('dp', 'mp'), 0, 0, tiled=True)  19.7 us
    all_to_all x4, waiting for transfers between devices, spread(): return lax.all_to_all(x, ('dp', 'mp'), 0, 0, tiled=True)  19.4 us
    ppermute x5, starting transfers between devices, passed_along(): return lax.ppermute(x, 'mp', pairs)  8.43 us
  transfers between devices with their start and end apart: 46, of which 19 were waited for; matrix products, arithmetic and copies ran while one was open for 12% of the time, Pallas kernels for 25%

profile of v2, /device:TPU:0, one launch (start us, length us, event | category | flops | bytes accessed | tf_op | source)
XLA Modules:
  0.0 403.3 jit_solution(2814739656116449676)
XLA Ops:
  12.1 2.8 multiply_reduce_fusion.3
  16.9 5.1 %collective-permute-start.1 = (bf16[512,128]{1,0:T(8,128)(2,1)S(1)}, bf16[512,128]{1,0:T(8,128)(2,1)S(1)}, u32[]{:S(2)}, u32[]{:S(2)}) collective-permute-start(bf16[512,128]{1,0:T(8,128)(2,1)S(1)} %bitcast.515), channel_id=1, source_target_pairs={{0,24},{4,28},{8,0},{12,4},{16,8},{20,12},{24,16},{28,20},{1,25},{... | collective-permute-start | bytes 393224 | tf_op jit(solution)/shard_map/ppermute | solution.py:61
  25.6 2.7 fusion.5
  33.0 3.1 reshape.744.refs_2_
  41.1 5.6 %collective-permute-done.4 = bf16[4,256,128]{2,1,0:T(8,128)(2,1)S(1)} collective-permute-done((bf16[4,256,128]{2,1,0:T(8,128)(2,1)S(1)}, bf16[4,256,128]{2,1,0:T(8,128)(2,1)S(1)}, u32[]{:S(2)}, u32[]{:S(2)}) %collective-permute-start.4) | collective-permute-done | bytes 262176 | tf_op jit(solution)/shard_map/ppermute | solution.py:61
  49.9 13.8 %collective-permute-done.5 = bf16[2,4,256,128]{3,2,1,0:T(8,128)(2,1)S(1)} collective-permute-done((bf16[2,4,256,128]{3,2,1,0:T(8,128)(2,1)S(1)}, bf16[2,4,256,128]{3,2,1,0:T(8,128)(2,1)S(1)}, u32[]{:S(2)}, u32[]{:S(2)}) %collective-permute-start.5) | collective-permute-done | bytes 524320 | tf_op jit(solution)/shard_map/ppermute | solution.py:61
  63.8 3.6 collective-permute-done.7
  72.1 9.7 %unpack.1 = (f32[32,256]{1,0:T(8,128)}, bf16[8,128,256]{2,1,0:T(8,128)(2,1)}, bf16[2,256,256]{2,1,0:T(8,128)(2,1)}, bf16[10,256,512]{2,1,0:T(8,128)(2,1)}, bf16[512,1152]{1,0:T(8,128)(2,1)}, /*index=5*/f32[24,512]{1,0:T(8,128)}) custom-call(s32[4]{0:T(128)} %pad_add_fusion.refs_0_, bf16[2,16,256,128]{3,2,1,0:T(8,128)(2,1)} %copy-done.4, ...), custom_call_target="tpu_custom_call" | custom-call | flops 8049999872 | bytes 7000000 | tf_op jit(solution)/shard_map/unpack/pallas_call | solution.py:232
  81.8 13.3 %stem.1 = (f32[128,512]{1,0:T(8,128)}, bf16[20,288,256]{2,1,0:T(8,128)(2,1)}, bf16[10,128,256]{2,1,0:T(8,128)(2,1)}, bf16[10,128,256]{2,1,0:T(8,128)(2,1)}) custom-call(bf16[5,576,128]{2,1,0:T(8,128)(2,1)} %copy.162.refs_0_.refs_1_, bf16[8,128,256]{2,1,0:T(8,128)(2,1)} %get-tuple-element.86.refs_1_.refs_3_, f32[32,256]{1,0:T(8,128)} %get-tuple-element.87.refs_2_.refs_4_, ...), custom_call_target="tpu_custom_call" | custom-call | flops 14949999616 | bytes 13000000 | tf_op jit(solution)/shard_map/stem/pallas_call | solution.py:232
  95.2 8.4 %all-gather.5.cloned.1.call-done = bf16[128,64,512]{2,1,0:T(8,128)(2,1)} async-done(((bf16[4,64,512]{2,1,0:T(8,128)(2,1)}), bf16[128,64,512]{2,1,0:T(8,128)(2,1)}) %all-gather.5.cloned.1.call-update) | async-done | bytes 8388624 | tf_op jit(solution)/shard_map/all_gather | solution.py:1398
  103.6 4.8 %first.1 = (f32[128,512]{1,0:T(8,128)}, f32[4,128,512]{2,1,0:T(8,128)}, bf16[128,512]{1,0:T(8,128)(2,1)}, bf16[128,512]{1,0:T(8,128)(2,1)}) custom-call(bf16[8,4,4,64,512]{4,3,2,1,0:T(8,128)(2,1)} %bitcast.528, f32[128,512]{1,0:T(8,128)} %get-tuple-element.90.refs_1_.refs_6_, f32[24,512]{1,0:T(8,128)} %get-tuple-element.91.refs_2_.refs_3_.refs_6_.refs_7_.refs_15_.refs_9_), custom_call_target="tpu_custom_call" | custom-call | flops 6899999744 | bytes 6000000 | tf_op jit(solution)/shard_map/first/pallas_call | solution.py:232
  110.0 5.9 %position.1 = (bf16[640,512]{1,0:T(8,128)(2,1)}, bf16[128,512]{1,0:T(8,128)(2,1)}, bf16[128,512]{1,0:T(8,128)(2,1)}) custom-call(bf16[8,4,4,64,512]{4,3,2,1,0:T(8,128)(2,1)} %bitcast.529, bf16[640,512]{1,0:T(8,128)(2,1)} %pad_maximum_fusion.3.refs_1_.refs_9_, bf16[128,512]{1,0:T(8,128)(2,1)} %get-tuple-element.92.refs_2_.refs_7_, ...), custom_call_target="tpu_custom_call" | custom-call | flops 5750000128 | bytes 5000000 | tf_op jit(solution)/shard_map/position/pallas_call | solution.py:232
  118.3 10.9 %attention.1 = (f32[128,512]{1,0:T(8,128)}, bf16[4,512,256]{2,1,0:T(8,128)(2,1)}, f32[8,128,512]{2,1,0:T(8,128)}, bf16[128,512]{1,0:T(8,128)(2,1)}, bf16[128,512...) custom-call(bf16[8,4,4,64,512]{4,3,2,1,0:T(8,128)(2,1)} %bitcast.530, ...), custom_call_target="tpu_custom_call" | custom-call | flops 11500000256 | bytes 10000000 | tf_op jit(solution)/shard_map/attention/pallas_call | solution.py:232
  129.2 2.1 collective-permute-start.11
  132.6 2.0 collective-permute-done.12.refs_2_.refs_10_
  135.3 2.3 conv.1
  137.6 6.0 %all-to-all-start = ((f32[32,16,128]{2,1,0:T(8,128)}), f32[32,16,128]{2,1,0:T(8,128)S(1)}, u32[]{:S(2)}, u32[]{:S(2)}) async-start(f32[32,16,128]{2,1,0:T(8,128)} %get-tuple-element.101), calls=%async_computation | async-start | bytes 524288 | tf_op jit(solution)/shard_map/all_to_all | solution.py:209
  145.1 23.3 %all-gather.7.cloned.1.call-done = bf16[64,64,512]{2,1,0:T(8,128)(2,1)} async-done(((bf16[2,64,512]{2,1,0:T(8,128)(2,1)}), bf16[64,64,512]{2,1,0:T(8,128)(2,1)}) %all-gather.7.cloned.1.call-update) | async-done | bytes 4194320 | tf_op jit(solution)/shard_map/all_gather | solution.py:1398
  169.1 12.0 %middle.1 = (bf16[8,2,2,64,512]{4,3,2,1,0:T(8,128)(2,1)}, bf16[8,2,2,64,512]{4,3,2,1,0:T(8,128)(2,1)}, bf16[512,1152]{1,0:T(8,128)(2,1)}, f32[128,512]{1,0:T(8,1...) custom-call(s32[4]{0:T(128)} %pad_add_fusion.refs_0_, ...), custom_call_target="tpu_custom_call" | custom-call | flops 14949999616 | bytes 13000000 | tf_op jit(solution)/shard_map/middle/pallas_call | solution.py:232
  181.5 3.1 all-to-all-start.1
  184.6 2.2 collective-permute-start.13
  188.9 2.3 collective-permute-done.14.refs_4_
  191.2 3.9 all-to-all-done.1.refs_5_
  195.9 4.5 %conv_back.1 = (bf16[4,128,256]{2,1,0:T(8,128)(2,1)}, f32[128,512]{1,0:T(8,128)}, f32[11,512]{1,0:T(8,128)}, f32[1,1]{1,0:T(1,128)}) custom-call(bf16[8,4,4,64,512]{4,3,2,1,0:T(8,128)(2,1)} %bitcast.532, f32[128,512]{1,0:T(8,128)} %get-tuple-element.104.refs_1_, f32[128,512]{1,0:T(8,128)} %get-tuple-element.105.refs_2_, f32[16,512]{1,0:T(8,128)} %copy-done.28, ...), custom_call_target="tpu_custom_call" | custom-call | flops 4600000000 | bytes 4000000 | tf_op jit(solution)/shard_map/conv_back/pallas_call | solution.py:232
  200.3 2.0 add_convert_fusion
  202.4 13.3 %back.1 = (bf16[128,512]{1,0:T(8,128)(2,1)}, bf16[4,512,256]{2,1,0:T(8,128)(2,1)}, bf16[640,512]{1,0:T(8,128)(2,1)}, bf16[512,512]{1,0:T(8,128)(2,1)}, f32[128,512]{1,0:T(8,128)}, /*index=5*/f32[2,512]{1,0:T(2,128)}) custom-call(bf16[8,4,4,64,512]{4,3,2,1,0:T(8,128)(2,1)} %bitcast.533, f32[128,512]{1,0:T(8,128)} %get-tuple-element.112.refs_1_.refs_2_, ...), custom_call_target="tpu_custom_call" | custom-call | flops 11500000256 | bytes 10000000 | tf_op jit(solution)/shard_map/back/pallas_call | solution.py:232
  220.0 6.2 %mix_grad.1 = (bf16[2,2,4,128,512]{4,3,2,1,0:T(8,128)(2,1)}, bf16[2,2,4,128,512]{4,3,2,1,0:T(8,128)(2,1)}) custom-call(s32[4]{0:T(128)} %pad_add_fusion.refs_0_, f32[128,512]{1,0:T(8,128)} %get-tuple-element.112.refs_1_.refs_2_, f32[128,512]{1,0:T(8,128)} %get-tuple-element.111.refs_14_.refs_2_, bf16[4,128,256]{2,1,0:T(8,128)(2,1)} %get-tuple-element.121.refs_3_, ...), custom_call_target="tpu_custom_call" | custom-call | flops 8049999872 | bytes 7000000 | tf_op jit(solution)/shard_map/mix_grad/pallas_call | solution.py:232
  227.3 8.1 %last.1 = (bf16[2,2,4,128,512]{4,3,2,1,0:T(8,128)(2,1)}, bf16[2,2,4,128,512]{4,3,2,1,0:T(8,128)(2,1)}, bf16[128,512]{1,0:T(8,128)(2,1)}, f32[4,512]{1,0:T(4,128)}) custom-call(s32[4]{0:T(128)} %pad_add_fusion.refs_0_, bf16[8,4,4,64,512]{4,3,2,1,0:T(8,128)(2,1)} %bitcast.534, f32[128,512]{1,0:T(8,128)} %get-tuple-element.112.refs_1_.refs_2_, ...), custom_call_target="tpu_custom_call" | custom-call | flops 9200000000 | bytes 8000000 | tf_op jit(solution)/shard_map/last/pallas_call | solution.py:232
  239.9 5.6 %pack.1 = (bf16[2,2,4,256,128]{4,3,2,1,0:T(8,128)(2,1)}, bf16[2,2,4,256,128]{4,3,2,1,0:T(8,128)(2,1)}, bf16[2,2,4,256,128]{4,3,2,1,0:T(8,128)(2,1)}, bf16[2,2,4,256,128]{4,3,2,1,0:T(8,128)(2,1)}) custom-call(s32[4]{0:T(128)} %pad_add_fusion.refs_0_, bf16[10,128,256]{2,1,0:T(8,128)(2,1)} %get-tuple-element.134.refs_9_.refs_1_, ...), custom_call_target="tpu_custom_call" | custom-call | flops 5750000128 | bytes 5000000 | tf_op jit(solution)/shard_map/pack/pallas_call | solution.py:232
  248.6 27.6 %stem_back.1 = (f32[2,256,256]{2,1,0:T(8,128)}, f32[18,8,256]{2,1,0:T(8,128)}, f32[16,256]{1,0:T(8,128)}) custom-call(bf16[128,512]{1,0:T(8,128)(2,1)} %get-tuple-element.131.refs_0_.refs_2_, bf16[5,576,128]{2,1,0:T(8,128)(2,1)} %copy.162.refs_0_.refs_1_, bf16[16,23040]{1,0:T(8,128)(2,1)} %reshape.744.refs_2_, ...), custom_call_target="tpu_custom_call" | custom-call | flops 31050000384 | bytes 27000000 | tf_op jit(solution)/shard_map/stem_back/pallas_call | solution.py:232
  278.1 2.0 fusion.9.refs_10_
  281.2 5.1 %collective-permute-done.25 = bf16[2,4,128,512]{3,2,1,0:T(8,128)(2,1)} collective-permute-done((bf16[2,4,128,512]{3,2,1,0:T(8,128)(2,1)S(1)}, bf16[2,4,128,512]{3,2,1,0:T(8,128)(2,1)}, u32[]{:S(2)}, u32[]{:S(2)}) %collective-permute-start.25) | collective-permute-done | bytes 1048608 | tf_op jit(solution)/shard_map/ppermute | solution.py:61
  286.2 2.4 fusion.3.refs_7_
  288.6 2.2 collective-permute-start.28
  290.8 2.2 fusion.4.refs_8_
  294.0 2.1 stem_rows.1
  296.0 3.7 all-to-all-start.2
  299.7 12.2 %collective-permute-done.32 = bf16[2,4,256,128]{3,2,1,0:T(8,128)(2,1)} collective-permute-done((bf16[2,4,256,128]{3,2,1,0:T(8,128)(2,1)}, bf16[2,4,256,128]{3,2,1,0:T(8,128)(2,1)}, u32[]{:S(2)}, u32[]{:S(2)}) %collective-permute-start.32) | collective-permute-done | bytes 524320 | tf_op jit(solution)/shard_map/ppermute | solution.py:61
  313.2 1.9 collective-permute-start.33
  315.1 1.8 collective-permute-done.28
  319.7 1.7 collective-permute-start.30
  324.3 3.6 collective-permute-done.29
  327.9 4.6 %collective-permute-done.30 = bf16[128,512]{1,0:T(8,128)(2,1)S(1)} collective-permute-done((bf16[128,512]{1,0:T(8,128)(2,1)S(1)}, bf16[128,512]{1,0:T(8,128)(2,1)S(1)}, u32[]{:S(2)}, u32[]{:S(2)}) %collective-permute-start.30) | collective-permute-done | bytes 131104 | tf_op jit(solution)/shard_map/ppermute | solution.py:61
  336.6 2.9 collective-permute-start.21
  346.5 1.8 collective-permute-start.37
  357.6 2.7 collective-permute-done.37
  363.9 7.0 %all-to-all-start.3 = ((bf16[32,64,128]{2,1,0:T(8,128)(2,1)}), bf16[32,64,128]{2,1,0:T(8,128)(2,1)S(1)}, u32[]{:S(2)}, u32[]{:S(2)}) async-start(bf16[32,64,128]{2,1,0:T(8,128)(2,1)} %broadcast_in_dim.102), calls=%async_computation.4 | async-start | bytes 1048576 | tf_op jit(solution)/shard_map/all_to_all | solution.py:209
  371.0 15.5 %all-to-all-done.3 = bf16[32,64,128]{2,1,0:T(8,128)(2,1)S(1)} async-done(((bf16[32,64,128]{2,1,0:T(8,128)(2,1)}), bf16[32,64,128]{2,1,0:T(8,128)(2,1)S(1)}, u32[]{:S(2)}, u32[]{:S(2)}) %all-to-all-start.3) | async-done | bytes 524320 | tf_op jit(solution)/shard_map/all_to_all | solution.py:209
  (267 shorter events, 88.5 us)
Async XLA Ops:
  7.2 96.4 %all-gather.5.cloned.1.call-start = ((), (), s32[]{:S(2)}) async-start(), calls=%async_computation.6 | async-start | bytes 8650752 | tf_op jit(solution)/shard_map/all_gather | solution.py:1398
  12.0 11.7 %copy-start.24 = (bf16[1,1024,80]{1,2,0:T(8,128)(2,1)S(1)}, bf16[1,1024,80]{1,2,0:T(8,128)(2,1)}, u32[]{:S(2)}) copy-start(bf16[1,1024,80]{1,2,0:T(8,128)(2,1)} %param.10) | copy-start | bytes 491524
  12.0 156.4 %all-gather.7.cloned.1.call-start = ((), (), s32[]{:S(2)}) async-start(), calls=%async_computation.7 | async-start | bytes 4325376 | tf_op jit(solution)/shard_map/all_gather | solution.py:1398
  16.9 20.2 %collective-permute-start.1 = (bf16[512,128]{1,0:T(8,128)(2,1)S(1)}, bf16[512,128]{1,0:T(8,128)(2,1)S(1)}, u32[]{:S(2)}, u32[]{:S(2)}) collective-permute-start(bf16[512,128]{1,0:T(8,128)(2,1)S(1)} %bitcast.515), channel_id=1, source_target_pairs={{0,24},{4,28},{8,0},{12,4},{16,8},{20,12},{24,16},{28,20},{1,25},{... | collective-permute-start | bytes 393224 | tf_op jit(solution)/shard_map/ppermute | solution.py:61
  22.0 15.9 %collective-permute-start.2 = (bf16[512,128]{1,0:T(8,128)(2,1)S(1)}, bf16[512,128]{1,0:T(8,128)(2,1)S(1)}, u32[]{:S(2)}, u32[]{:S(2)}) collective-permute-start(bf16[512,128]{1,0:T(8,128)(2,1)S(1)} %bitcast.516), channel_id=1, source_target_pairs={{0,16},{4,20},{8,24},{12,28},{16,0},{20,4},{24,8},{28,12},{1,17},{... | collective-permute-start | bytes 393224 | tf_op jit(solution)/shard_map/ppermute | solution.py:61
  22.0 15.9 %collective-permute-start.3 = (bf16[512,128]{1,0:T(8,128)(2,1)S(1)}, bf16[512,128]{1,0:T(8,128)(2,1)S(1)}, u32[]{:S(2)}, u32[]{:S(2)}) collective-permute-start(bf16[512,128]{1,0:T(8,128)(2,1)S(1)} %bitcast.517), channel_id=1, source_target_pairs={{0,8},{4,12},{8,16},{12,20},{16,24},{20,28},{24,0},{28,4},{1,9},{5... | collective-permute-start | bytes 393224 | tf_op jit(solution)/shard_map/ppermute | solution.py:61
  24.1 5.2 %collective-permute-start = (bf16[8,80]{1,0:T(8,128)(2,1)S(1)}, bf16[8,80]{1,0:T(8,128)(2,1)S(1)}, u32[]{:S(2)}, u32[]{:S(2)}) collective-permute-start(bf16[8,80]{1,0:T(8,128)(2,1)S(1)} %slice.784), channel_id=1, source_target_pairs={{0,1},{1,2},{2,3},{4,5},{5,6},{6,7},{8,9},{9,10},{10,11},{12,13},{... | collective-permute-start | bytes 3848 | tf_op jit(solution)/shard_map/ppermute | solution.py:215
  38.0 8.8 %collective-permute-start.4 = (bf16[4,256,128]{2,1,0:T(8,128)(2,1)S(1)}, bf16[4,256,128]{2,1,0:T(8,128)(2,1)S(1)}, u32[]{:S(2)}, u32[]{:S(2)}) collective-permute-start(bf16[4,256,128]{2,1,0:T(8,128)(2,1)S(1)} %get-tuple-element.84), channel_id=1, source_target_pairs={{0,2},{1,3},{2,0},{3,1},{4,6},{5,7},{6,4},{7,5},{8,10},{9,11},{10,... | collective-permute-start | bytes 786440 | tf_op jit(solution)/shard_map/ppermute | solution.py:61
  39.6 8.9 %collective-permute-start.6 = (bf16[4,256,128]{2,1,0:T(8,128)(2,1)S(1)}, bf16[4,256,128]{2,1,0:T(8,128)(2,1)S(1)}, u32[]{:S(2)}, u32[]{:S(2)}) collective-permute-start(bf16[4,256,128]{2,1,0:T(8,128)(2,1)S(1)} %get-tuple-element.85), channel_id=1, source_target_pairs={{0,4},{4,0},{8,12},{12,8},{16,20},{20,16},{24,28},{28,24},{1,5},{5... | collective-permute-start | bytes 786440 | tf_op jit(solution)/shard_map/ppermute | solution.py:61
  46.8 16.9 %collective-permute-start.5 = (bf16[2,4,256,128]{3,2,1,0:T(8,128)(2,1)S(1)}, bf16[2,4,256,128]{3,2,1,0:T(8,128)(2,1)S(1)}, u32[]{:S(2)}, u32[]{:S(2)}) collective-permute-start(bf16[2,4,256,128]{3,2,1,0:T(8,128)(2,1)S(1)} %get-tuple-element.187), channel_id=1, source_target_pairs={{0,4},{4,0},{8,12},{12,8},{16,20},{20,16},{24,28},{28,24},{1,5},{5... | collective-permute-start | bytes 1572872 | tf_op jit(solution)/shard_map/ppermute | solution.py:61
  48.6 18.8 %collective-permute-start.7 = (bf16[2,4,256,128]{3,2,1,0:T(8,128)(2,1)S(1)}, bf16[2,4,256,128]{3,2,1,0:T(8,128)(2,1)S(1)}, u32[]{:S(2)}, u32[]{:S(2)}) collective-permute-start(bf16[2,4,256,128]{3,2,1,0:T(8,128)(2,1)S(1)} %get-tuple-element.189), channel_id=1, source_target_pairs={{0,2},{1,3},{2,0},{3,1},{4,6},{5,7},{6,4},{7,5},{8,10},{9,11},{10,... | collective-permute-start | bytes 1572872 | tf_op jit(solution)/shard_map/ppermute | solution.py:61
  67.7 4.4 %collective-permute-start.8 = (bf16[2,16,256,128]{3,2,1,0:T(8,128)(2,1)S(1)}, bf16[2,16,256,128]{3,2,1,0:T(8,128)(2,1)}, u32[]{:S(2)}, u32[]{:S(2)}) collective-permute-start(bf16[2,16,256,128]{3,2,1,0:T(8,128)(2,1)S(1)} %pad_maximum_fusion.refs_1_), channel_id=1, source_target_pairs={{0,1},{1,0},{2,3},{3,2},{4,5},{5,4},{6,7},{7,6},{8,9},{9,8},{10,11... | collective-permute-start | bytes 6291464 | tf_op jit(solution)/shard_map/ppermute | solution.py:61
  108.5 7.4 %collective-permute-start.9 = (bf16[128,512]{1,0:T(8,128)(2,1)}, bf16[128,512]{1,0:T(8,128)(2,1)S(1)}, u32[]{:S(2)}, u32[]{:S(2)}) collective-permute-start(bf16[128,512]{1,0:T(8,128)(2,1)} %get-tuple-element.92.refs_2_.refs_7_), channel_id=1, source_target_pairs={{0,2},{1,3},{2,0},{3,1},{4,6},{5,7},{6,4},{7,5},{8,10},{9,11},{10,... | collective-permute-start | bytes 393224 | tf_op jit(solution)/shard_map/ppermute | solution.py:61
  115.9 1.6 collective-permute-start.10
  129.2 3.4 collective-permute-start.11
  131.3 3.4 collective-permute-start.12
  137.6 30.9 %all-to-all-start = ((f32[32,16,128]{2,1,0:T(8,128)}), f32[32,16,128]{2,1,0:T(8,128)S(1)}, u32[]{:S(2)}, u32[]{:S(2)}) async-start(f32[32,16,128]{2,1,0:T(8,128)} %get-tuple-element.101), calls=%async_computation | async-start | bytes 524288 | tf_op jit(solution)/shard_map/all_to_all | solution.py:209
  181.1 19.2 %collective-permute-start.15 = (bf16[8,2,2,64,512]{4,3,2,1,0:T(8,128)(2,1)}, bf16[8,2,2,64,512]{4,3,2,1,0:T(8,128)(2,1)S(1)}, u32[]{:S(2)}, u32[]{:S(2)}) collective-permute-start(bf16[8,2,2,64,512]{4,3,2,1,0:T(8,128)(2,1)} %get-tuple-element.116), channel_id=1, source_target_pairs={{0,1},{1,0},{2,3},{3,2},{4,5},{5,4},{6,7},{7,6},{8,9},{9,8},{10,11... | collective-permute-start | bytes 6291464 | tf_op jit(solution)/shard_map/ppermute | solution.py:61
  181.5 13.7 %all-to-all-start.1 = ((f32[32,16,128]{2,1,0:T(8,128)}), f32[32,16,128]{2,1,0:T(8,128)S(1)}, u32[]{:S(2)}, u32[]{:S(2)}) async-start(f32[32,16,128]{2,1,0:T(8,128)} %get-tuple-element.108), calls=%async_computation.1 | async-start | bytes 524288 | tf_op jit(solution)/shard_map/all_to_all | solution.py:209
  184.6 170.2 %reduce-scatter.2.cloned.1.call-start = ((), (), s32[]{:S(2)}) async-start(), calls=%async_computation.5 | async-start | bytes 2228224 | tf_op jit(solution)/shard_map/reduce_scatter | solution.py:198
  184.6 4.3 %collective-permute-start.13 = (f32[16,512]{1,0:T(8,128)}, f32[16,512]{1,0:T(8,128)S(1)}, u32[]{:S(2)}, u32[]{:S(2)}) collective-permute-start(f32[16,512]{1,0:T(8,128)} %get-tuple-element.106), channel_id=1, source_target_pairs={{0,1},{1,2},{2,3},{4,5},{5,6},{6,7},{8,9},{9,10},{10,11},{12,13},{... | collective-permute-start | bytes 98312 | tf_op jit(solution)/shard_map/ppermute | solution.py:215
  186.8 4.4 %collective-permute-start.14 = (f32[16,512]{1,0:T(8,128)}, f32[16,512]{1,0:T(8,128)S(1)}, u32[]{:S(2)}, u32[]{:S(2)}) collective-permute-start(f32[16,512]{1,0:T(8,128)} %get-tuple-element.107), channel_id=1, source_target_pairs={{1,0},{2,1},{3,2},{5,4},{6,5},{7,6},{9,8},{10,9},{11,10},{13,12},{... | collective-permute-start | bytes 98312 | tf_op jit(solution)/shard_map/ppermute | solution.py:215
  216.7 1.6 collective-permute-start.16
  219.3 7.2 %collective-permute-start.17 = (bf16[1,128,512]{2,1,0:T(8,128)(2,1)S(1)}, bf16[1,128,512]{2,1,0:T(8,128)(2,1)S(1)}, u32[]{:S(2)}, u32[]{:S(2)}) collective-permute-start(bf16[1,128,512]{2,1,0:T(8,128)(2,1)S(1)} %get-tuple-element.203), channel_id=1, source_target_pairs={{0,2},{1,3},{2,0},{3,1},{4,6},{5,7},{6,4},{7,5},{8,10},{9,11},{10,... | collective-permute-start | bytes 393224 | tf_op jit(solution)/shard_map/ppermute | solution.py:61
  226.2 9.7 %collective-permute-start.24 = (bf16[2,2,4,128,512]{4,3,2,1,0:T(8,128)(2,1)}, bf16[2,2,4,128,512]{4,3,2,1,0:T(8,128)(2,1)}, u32[]{:S(2)}, u32[]{:S(2)}) collective-permute-start(bf16[2,2,4,128,512]{4,3,2,1,0:T(8,128)(2,1)} %get-tuple-element.142), channel_id=1, source_target_pairs={{0,1},{1,0},{2,3},{3,2},{4,5},{5,4},{6,7},{7,6},{8,9},{9,8},{10,11... | collective-permute-start | bytes 6291464 | tf_op jit(solution)/shard_map/ppermute | solution.py:61
  235.4 10.7 %collective-permute-start.18 = (bf16[2,2,4,128,512]{4,3,2,1,0:T(8,128)(2,1)}, bf16[2,2,4,128,512]{4,3,2,1,0:T(8,128)(2,1)}, u32[]{:S(2)}, u32[]{:S(2)}) collective-permute-start(bf16[2,2,4,128,512]{4,3,2,1,0:T(8,128)(2,1)} %get-tuple-element.130), channel_id=1, source_target_pairs={{0,1},{1,0},{2,3},{3,2},{4,5},{5,4},{6,7},{7,6},{8,9},{9,8},{10,11... | collective-permute-start | bytes 6291464 | tf_op jit(solution)/shard_map/ppermute | solution.py:61
  238.5 47.7 %collective-permute-start.25 = (bf16[2,4,128,512]{3,2,1,0:T(8,128)(2,1)S(1)}, bf16[2,4,128,512]{3,2,1,0:T(8,128)(2,1)}, u32[]{:S(2)}, u32[]{:S(2)}) collective-permute-start(bf16[2,4,128,512]{3,2,1,0:T(8,128)(2,1)S(1)} %fusion.2.refs_4_), channel_id=1, source_target_pairs={{0,2},{1,3},{2,0},{3,1},{4,6},{5,7},{6,4},{7,5},{8,10},{9,11},{10,... | collective-permute-start | bytes 3145736 | tf_op jit(solution)/shard_map/ppermute | solution.py:61
  245.5 30.8 %collective-permute-start.26 = (bf16[2,2,4,256,128]{4,3,2,1,0:T(8,128)(2,1)}, bf16[2,2,4,256,128]{4,3,2,1,0:T(8,128)(2,1)S(1)}, u32[]{:S(2)}, u32[]{:S(2)}) collective-permute-start(bf16[2,2,4,256,128]{4,3,2,1,0:T(8,128)(2,1)} %get-tuple-element.145), channel_id=1, source_target_pairs={{0,1},{1,0},{2,3},{3,2},{4,5},{5,4},{6,7},{7,6},{8,9},{9,8},{10,11... | collective-permute-start | bytes 3145736 | tf_op jit(solution)/shard_map/ppermute | solution.py:61
  245.8 32.3 %collective-permute-start.27 = (bf16[2,2,4,256,128]{4,3,2,1,0:T(8,128)(2,1)}, bf16[2,2,4,256,128]{4,3,2,1,0:T(8,128)(2,1)}, u32[]{:S(2)}, u32[]{:S(2)}) collective-permute-start(bf16[2,2,4,256,128]{4,3,2,1,0:T(8,128)(2,1)} %get-tuple-element.147), channel_id=1, source_target_pairs={{0,1},{1,0},{2,3},{3,2},{4,5},{5,4},{6,7},{7,6},{8,9},{9,8},{10,11... | collective-permute-start | bytes 3145736 | tf_op jit(solution)/shard_map/ppermute | solution.py:61
  247.6 43.2 %collective-permute-start.19 = (bf16[2,4,128,512]{3,2,1,0:T(8,128)(2,1)S(1)}, bf16[2,4,128,512]{3,2,1,0:T(8,128)(2,1)}, u32[]{:S(2)}, u32[]{:S(2)}) collective-permute-start(bf16[2,4,128,512]{3,2,1,0:T(8,128)(2,1)S(1)} %fusion.1.refs_10_), channel_id=1, source_target_pairs={{0,4},{4,0},{8,12},{12,8},{16,20},{20,16},{24,28},{28,24},{1,5},{5... | collective-permute-start | bytes 3145736 | tf_op jit(solution)/shard_map/ppermute | solution.py:61
  248.6 27.6 %copy-start.10 = (bf16[2,2,4,256,128]{4,3,2,1,0:T(8,128)(2,1)S(1)}, bf16[2,2,4,256,128]{4,3,2,1,0:T(8,128)(2,1)}, u32[]{:S(2)}) copy-start(bf16[2,2,4,256,128]{4,3,2,1,0:T(8,128)(2,1)} %get-tuple-element.144) | copy-start | bytes 3145732
  277.2 34.8 %collective-permute-start.32 = (bf16[2,4,256,128]{3,2,1,0:T(8,128)(2,1)}, bf16[2,4,256,128]{3,2,1,0:T(8,128)(2,1)}, u32[]{:S(2)}, u32[]{:S(2)}) collective-permute-start(bf16[2,4,256,128]{3,2,1,0:T(8,128)(2,1)} %fusion.8.refs_9_), channel_id=1, source_target_pairs={{0,2},{1,3},{2,0},{3,1},{4,6},{5,7},{6,4},{7,5},{8,10},{9,11},{10,... | collective-permute-start | bytes 1572872 | tf_op jit(solution)/shard_map/ppermute | solution.py:61
  280.1 41.4 %collective-permute-start.34 = (bf16[2,4,256,128]{3,2,1,0:T(8,128)(2,1)}, bf16[2,4,256,128]{3,2,1,0:T(8,128)(2,1)}, u32[]{:S(2)}, u32[]{:S(2)}) collective-permute-start(bf16[2,4,256,128]{3,2,1,0:T(8,128)(2,1)} %fusion.9.refs_10_), channel_id=1, source_target_pairs={{0,4},{4,0},{8,12},{12,8},{16,20},{20,16},{24,28},{28,24},{1,5},{5... | collective-permute-start | bytes 1572872 | tf_op jit(solution)/shard_map/ppermute | solution.py:61
  288.6 28.3 %collective-permute-start.28 = (bf16[4,128,512]{2,1,0:T(8,128)(2,1)}, bf16[4,128,512]{2,1,0:T(8,128)(2,1)}, u32[]{:S(2)}, u32[]{:S(2)}) collective-permute-start(bf16[4,128,512]{2,1,0:T(8,128)(2,1)} %fusion.3.refs_7_), channel_id=1, source_target_pairs={{0,4},{4,0},{8,12},{12,8},{16,20},{20,16},{24,28},{28,24},{1,5},{5... | collective-permute-start | bytes 1572872 | tf_op jit(solution)/shard_map/ppermute | solution.py:61
  293.0 40.7 %collective-permute-start.20 = (bf16[4,128,512]{2,1,0:T(8,128)(2,1)}, bf16[4,128,512]{2,1,0:T(8,128)(2,1)S(1)}, u32[]{:S(2)}, u32[]{:S(2)}) collective-permute-start(bf16[4,128,512]{2,1,0:T(8,128)(2,1)} %fusion.4.refs_8_), channel_id=1, source_target_pairs={{0,2},{1,3},{2,0},{3,1},{4,6},{5,7},{6,4},{7,5},{8,10},{9,11},{10,... | collective-permute-start | bytes 1572872 | tf_op jit(solution)/shard_map/ppermute | solution.py:61
  296.0 58.6 %all-to-all-start.2 = ((bf16[32,48,128]{2,1,0:T(8,128)(2,1)}), bf16[32,48,128]{2,1,0:T(8,128)(2,1)S(1)}, u32[]{:S(2)}, u32[]{:S(2)}) async-start(bf16[32,48,128]{2,1,0:T(8,128)(2,1)} %bitcast.520), calls=%async_computation.3 | async-start | bytes 786432 | tf_op jit(solution)/shard_map/all_to_all | solution.py:209
  313.2 28.7 %collective-permute-start.33 = (bf16[4,256,128]{2,1,0:T(8,128)(2,1)S(1)}, bf16[4,256,128]{2,1,0:T(8,128)(2,1)S(1)}, u32[]{:S(2)}, u32[]{:S(2)}) collective-permute-start(bf16[4,256,128]{2,1,0:T(8,128)(2,1)S(1)} %fusion.11), channel_id=1, source_target_pairs={{0,4},{4,0},{8,12},{12,8},{16,20},{20,16},{24,28},{28,24},{1,5},{5... | collective-permute-start | bytes 786440 | tf_op jit(solution)/shard_map/ppermute | solution.py:61
  318.6 9.3 %collective-permute-start.29 = (bf16[128,512]{1,0:T(8,128)(2,1)S(1)}, bf16[128,512]{1,0:T(8,128)(2,1)S(1)}, u32[]{:S(2)}, u32[]{:S(2)}) collective-permute-start(bf16[128,512]{1,0:T(8,128)(2,1)S(1)} %get-tuple-element.174), channel_id=1, source_target_pairs={{0,8},{4,12},{8,16},{12,20},{16,24},{20,28},{24,0},{28,4},{1,9},{5... | collective-permute-start | bytes 393224 | tf_op jit(solution)/shard_map/ppermute | solution.py:61
  319.7 12.8 %collective-permute-start.30 = (bf16[128,512]{1,0:T(8,128)(2,1)S(1)}, bf16[128,512]{1,0:T(8,128)(2,1)S(1)}, u32[]{:S(2)}, u32[]{:S(2)}) collective-permute-start(bf16[128,512]{1,0:T(8,128)(2,1)S(1)} %get-tuple-element.176), channel_id=1, source_target_pairs={{0,16},{4,20},{8,24},{12,28},{16,0},{20,4},{24,8},{28,12},{1,17},{... | collective-permute-start | bytes 393224 | tf_op jit(solution)/shard_map/ppermute | solution.py:61
  321.5 11.0 %collective-permute-start.31 = (bf16[128,512]{1,0:T(8,128)(2,1)S(1)}, bf16[128,512]{1,0:T(8,128)(2,1)S(1)}, u32[]{:S(2)}, u32[]{:S(2)}) collective-permute-start(bf16[128,512]{1,0:T(8,128)(2,1)S(1)} %get-tuple-element.175), channel_id=1, source_target_pairs={{0,24},{4,28},{8,0},{12,4},{16,8},{20,12},{24,16},{28,20},{1,25},{... | collective-permute-start | bytes 393224 | tf_op jit(solution)/shard_map/ppermute | solution.py:61
  327.9 15.2 %collective-permute-start.35 = (bf16[4,256,128]{2,1,0:T(8,128)(2,1)S(1)}, bf16[4,256,128]{2,1,0:T(8,128)(2,1)S(1)}, u32[]{:S(2)}, u32[]{:S(2)}) collective-permute-start(bf16[4,256,128]{2,1,0:T(8,128)(2,1)S(1)} %fusion.10), channel_id=1, source_target_pairs={{0,2},{1,3},{2,0},{3,1},{4,6},{5,7},{6,4},{7,5},{8,10},{9,11},{10,... | collective-permute-start | bytes 786440 | tf_op jit(solution)/shard_map/ppermute | solution.py:61
  336.6 12.4 %collective-permute-start.21 = (bf16[128,512]{1,0:T(8,128)(2,1)S(1)}, bf16[128,512]{1,0:T(8,128)(2,1)S(1)}, u32[]{:S(2)}, u32[]{:S(2)}) collective-permute-start(bf16[128,512]{1,0:T(8,128)(2,1)S(1)} %get-tuple-element.177), channel_id=1, source_target_pairs={{0,8},{4,12},{8,16},{12,20},{16,24},{20,28},{24,0},{28,4},{1,9},{5... | collective-permute-start | bytes 393224 | tf_op jit(solution)/shard_map/ppermute | solution.py:61
  339.5 10.7 %collective-permute-start.22 = (bf16[128,512]{1,0:T(8,128)(2,1)S(1)}, bf16[128,512]{1,0:T(8,128)(2,1)S(1)}, u32[]{:S(2)}, u32[]{:S(2)}) collective-permute-start(bf16[128,512]{1,0:T(8,128)(2,1)S(1)} %get-tuple-element.179), channel_id=1, source_target_pairs={{0,16},{4,20},{8,24},{12,28},{16,0},{20,4},{24,8},{28,12},{1,17},{... | collective-permute-start | bytes 393224 | tf_op jit(solution)/shard_map/ppermute | solution.py:61
  340.6 9.6 %collective-permute-start.23 = (bf16[128,512]{1,0:T(8,128)(2,1)S(1)}, bf16[128,512]{1,0:T(8,128)(2,1)S(1)}, u32[]{:S(2)}, u32[]{:S(2)}) collective-permute-start(bf16[128,512]{1,0:T(8,128)(2,1)S(1)} %get-tuple-element.178), channel_id=1, source_target_pairs={{0,24},{4,28},{8,0},{12,4},{16,8},{20,12},{24,16},{28,20},{1,25},{... | collective-permute-start | bytes 393224 | tf_op jit(solution)/shard_map/ppermute | solution.py:61
  345.1 12.6 %collective-permute-start.36 = (bf16[2,256,128]{2,1,0:T(8,128)(2,1)}, bf16[2,256,128]{2,1,0:T(8,128)(2,1)}, u32[]{:S(2)}, u32[]{:S(2)}) collective-permute-start(bf16[2,256,128]{2,1,0:T(8,128)(2,1)} %pad_maximum_fusion.13), channel_id=1, source_target_pairs={{0,8},{4,12},{8,16},{12,20},{16,24},{20,28},{24,0},{28,4},{1,9},{5... | collective-permute-start | bytes 393224 | tf_op jit(solution)/shard_map/ppermute | solution.py:61
  346.5 13.8 %collective-permute-start.37 = (bf16[2,256,128]{2,1,0:T(8,128)(2,1)}, bf16[2,256,128]{2,1,0:T(8,128)(2,1)S(1)}, u32[]{:S(2)}, u32[]{:S(2)}) collective-permute-start(bf16[2,256,128]{2,1,0:T(8,128)(2,1)} %pad_maximum_fusion.14), channel_id=1, source_target_pairs={{0,16},{4,20},{8,24},{12,28},{16,0},{20,4},{24,8},{28,12},{1,17},{... | collective-permute-start | bytes 393224 | tf_op jit(solution)/shard_map/ppermute | solution.py:61
  349.0 11.3 %collective-permute-start.38 = (bf16[2,256,128]{2,1,0:T(8,128)(2,1)}, bf16[2,256,128]{2,1,0:T(8,128)(2,1)S(1)}, u32[]{:S(2)}, u32[]{:S(2)}) collective-permute-start(bf16[2,256,128]{2,1,0:T(8,128)(2,1)} %pad_maximum_fusion.15), channel_id=1, source_target_pairs={{0,24},{4,28},{8,0},{12,4},{16,8},{20,12},{24,16},{28,20},{1,25},{... | collective-permute-start | bytes 393224 | tf_op jit(solution)/shard_map/ppermute | solution.py:61
  363.9 22.5 %all-to-all-start.3 = ((bf16[32,64,128]{2,1,0:T(8,128)(2,1)}), bf16[32,64,128]{2,1,0:T(8,128)(2,1)S(1)}, u32[]{:S(2)}, u32[]{:S(2)}) async-start(bf16[32,64,128]{2,1,0:T(8,128)(2,1)} %broadcast_in_dim.102), calls=%async_computation.4 | async-start | bytes 1048576 | tf_op jit(solution)/shard_map/all_to_all | solution.py:209
  (31 other events, 93.9 us)
Sparse Core Ops, SparseCore 0:
  12.1 91.4 all-gather.4
  107.1 61.2 all-gather.6
  236.0 95.5 reduce-scatter.1

commit v3 on v2

--- a/solution.py
+++ b/solution.py
@@ -944,9 +944,10 @@
     high_ref[...] = gated_ref[rows - HALO :, :]
 
 
-def write_stats(stat_ref, first, second, number):
+def write_stats(stat_ref, first, second, number=None):
     rows = [x[:, LANES * k : LANES * k + LANES] for x in (first, second) for k in range(4)]
-    rows.append(jnp.broadcast_to(number, (8, LANES)))
+    if number is not None:
+        rows.append(jnp.broadcast_to(number, (8, LANES)))
     stat_ref[...] = jnp.broadcast_to(jnp.concatenate(rows, 0)[None], stat_ref.shape)
 
 
@@ -954,7 +955,7 @@
     whole = jnp.sum(stat_ref[...], 0)
     first = jnp.concatenate([whole[k : k + 1] for k in range(4)], 1)
     second = jnp.concatenate([whole[k : k + 1] for k in range(4, 8)], 1)
-    return first, second, whole[8:9, 0:1]
+    return first, second, whole[8:9, 0:1] if whole.shape[0] > 8 else None
 
 
 def conv_kernel(prev_ref, gated_ref, next_ref, vec_ref, valid_ref, hidden_ref, stat_ref, wide):
@@ -998,6 +999,7 @@
     high_ref,
     part_ref,
     vgrad_ref,
+    loss_ref,
     pre_ref,
     n4_ref,
     c_buf,
@@ -1081,8 +1083,8 @@
         part_ref,
         jnp.concatenate([a for a, _ in parts], 1),
         jnp.concatenate([b for _, b in parts], 1),
-        loss,
-    )
+    )
+    loss_ref[...] = loss
 
 
 def conv_back_kernel(
@@ -1105,7 +1107,7 @@
     dgate_ref,
     dx2_ref,
     vgrad_ref,
-    loss_ref,
+    count_ref,
     wide,
     wide_y,
     dh,
@@ -1117,8 +1119,8 @@
     first, second, count = read_stats(stat_ref)
     mean = first / count
     inverse = lax.rsqrt(second / count - mean * mean + norm_eps)
-    first, second, loss = read_stats(part_ref)
-    loss_ref[...] = loss / count
+    first, second, _ = read_stats(part_ref)
+    count_ref[...] = count
     wide[0:HALO, :] = prev_ref[0:HALO, :]
     wide[HALO : HALO + rows, :] = dy_ref[...]
     wide[HALO + rows :, :] = next_ref[0:HALO, :]
@@ -1508,7 +1510,7 @@
         name="conv",
     )
     stat = spread(stat)
-    two_keep, two_send, g_head, dx3, act, dy, yhat, b_low, b_high, part, vg_mid = call(
+    two_keep, two_send, g_head, dx3, act, dy, yhat, b_low, b_high, part, vg_mid, loss = call(
         middle_kernel,
         [
             *[((n_dp if plan else 1, COLS, 2, own_rows if plan else D, D), bf16)] * 2,
@@ -1519,8 +1521,9 @@
             ((tokens, D), f32),
             ((2 * HALO, D), f32),
             ((2 * HALO, D), f32),
-            stat_shape,
+            ((ndev, 8, LANES), f32),
             ((6, D), f32),
+            ((1, 1), f32),
         ],
         [spot, weights, more, hidden, stat, x2, head, vec, alignment[0][:, None], weight, valid],
         [
@@ -1534,7 +1537,7 @@
     b_prev, b_next = passed_along(b_high, 1), passed_along(b_low, -1)
     part = spread(part)
     two_both, own_two = reduced_cores(two_keep, two_send, plan)
-    dgate, dx2, vg_conv, loss = call(
+    dgate, dx2, vg_conv, count = call(
         conv_back_kernel,
         [
             ((n_mp, tokens, 2 * LANES), bf16),
@@ -1689,13 +1692,13 @@
     own = [own_in_one, own_out_one, own_mix, own_abo, own_in_two, own_out_two]
     packed = lax.dynamic_slice_in_dim(own_chunk.reshape(-1), offset, shard, 0)
     local_sq = sum(jnp.sum(grad * grad) for grad in own) + jnp.sum(packed * packed)
-    high = local_sq.astype(bf16)
-    rest = local_sq - high.astype(f32)
-    middle = rest.astype(bf16)
-    lowest = (rest - middle.astype(f32)).astype(bf16)
-    lane = jnp.arange(LANES)[None, :]
-    number = jnp.where(lane == 0, high, jnp.where(lane == 1, middle, jnp.where(lane == 2, lowest, 0)))
-    number = jnp.broadcast_to(number, (16, LANES)).astype(bf16)
+    numbers = []
+    for value in (local_sq, loss[0, 0]):
+        for _ in range(3):
+            numbers.append(value.astype(bf16))
+            value = value - numbers[-1].astype(f32)
+    number = jnp.pad(jnp.stack(numbers), (0, LANES - len(numbers)))
+    number = jnp.broadcast_to(number, (16, LANES))
     known = jnp.concatenate([few.astype(bf16), number], 0)
     known = spread(jnp.broadcast_to(known[None], (ndev, share + 16, LANES))).astype(f32)
     few = known[:, :share].reshape(ndev * share, LANES)
@@ -1726,7 +1729,7 @@
         outs.extend(adam(state, grad * factor, rate))
     outs.extend(adam(small, own_small * factor, small_rate(positions)))
     vec_grad = few[ROW_AT[2] : used].reshape(23, D) * factor
-    return (*outs, vec_grad, loss[0, 0], grad_norm)
+    return (*outs, vec_grad, jnp.sum(known[:, share, 3:6]) / count[0, 0], grad_norm)
 
 
 def solution(mesh):

time: 408 us -> 409 us (level)
  waiting for transfers between devices: 113 us -> 105 us
  starting transfers between devices: 67.3 us -> 73.4 us
    ppermute x34, waiting for transfers between devices: 56.9 us -> 51.9 us  [sent(): return lax.ppermute(x, axis, pairs)]
    ppermute x34, starting transfers between devices: 39 us -> 43.2 us  [sent(): return lax.ppermute(x, axis, pairs)]
where the time goes in v3:
time: 409 us; the launch traced here: 404 us
  Pallas kernels  126 us (31%)
  waiting for transfers between devices  105 us (26%)
  starting transfers between devices  73.4 us (18%)
  other arithmetic  49.8 us (12%)
  between operations  26.9 us (7%)
  local copies, waits for them, and re-layouts  22.7 us (6%)
    pallas_call x14, Pallas kernels, call(): pl.pallas_call(run, out_shape=[jax.ShapeDtypeStruct(shape, dtype) for sha...  126 us
    ppermute x34, waiting for transfers between devices, sent(): return lax.ppermute(x, axis, pairs)  51.9 us
    ppermute x34, starting transfers between devices, sent(): return lax.ppermute(x, axis, pairs)  43.2 us
    all_gather x2, waiting for transfers between devices, gathered(): whole = lax.all_gather(jnp.stack(low), ('dp', 'mp'), axis=0)  31.7 us
    convert_element_type x14, other arithmetic, low_total(): return total(*parts).astype(bf16)  21.7 us
    all_to_all x4, starting transfers between devices, spread(): return lax.all_to_all(x, ('dp', 'mp'), 0, 0, tiled=True)  21.6 us
    all_to_all x4, waiting for transfers between devices, spread(): return lax.all_to_all(x, ('dp', 'mp'), 0, 0, tiled=True)  17.1 us
    ppermute x5, starting transfers between devices, passed_along(): return lax.ppermute(x, 'mp', pairs)  8.43 us
  transfers between devices with their start and end apart: 46, of which 19 were waited for; matrix products, arithmetic and copies ran while one was open for 12% of the time, Pallas kernels for 25%

profile of v3, /device:TPU:0, one launch (start us, length us, event | category | flops | bytes accessed | tf_op | source)
XLA Modules:
  0.0 404.1 jit_solution(16253918109899128351)
XLA Ops:
  12.1 2.8 multiply_reduce_fusion.3
  16.9 5.1 %collective-permute-start.1 = (bf16[512,128]{1,0:T(8,128)(2,1)S(1)}, bf16[512,128]{1,0:T(8,128)(2,1)S(1)}, u32[]{:S(2)}, u32[]{:S(2)}) collective-permute-start(bf16[512,128]{1,0:T(8,128)(2,1)S(1)} %bitcast.522), channel_id=1, source_target_pairs={{0,24},{4,28},{8,0},{12,4},{16,8},{20,12},{24,16},{28,20},{1,25},{... | collective-permute-start | bytes 393224 | tf_op jit(solution)/shard_map/ppermute | solution.py:61
  25.6 2.7 fusion.5
  33.0 3.1 reshape.725.refs_2_
  41.1 5.6 %collective-permute-done.4 = bf16[4,256,128]{2,1,0:T(8,128)(2,1)S(1)} collective-permute-done((bf16[4,256,128]{2,1,0:T(8,128)(2,1)S(1)}, bf16[4,256,128]{2,1,0:T(8,128)(2,1)S(1)}, u32[]{:S(2)}, u32[]{:S(2)}) %collective-permute-start.4) | collective-permute-done | bytes 262176 | tf_op jit(solution)/shard_map/ppermute | solution.py:61
  46.8 1.7 collective-permute-start.5
  49.9 13.8 %collective-permute-done.5 = bf16[2,4,256,128]{3,2,1,0:T(8,128)(2,1)S(1)} collective-permute-done((bf16[2,4,256,128]{3,2,1,0:T(8,128)(2,1)S(1)}, bf16[2,4,256,128]{3,2,1,0:T(8,128)(2,1)S(1)}, u32[]{:S(2)}, u32[]{:S(2)}) %collective-permute-start.5) | collective-permute-done | bytes 524320 | tf_op jit(solution)/shard_map/ppermute | solution.py:61
  63.8 3.6 collective-permute-done.7
  72.1 9.7 %unpack.1 = (f32[32,256]{1,0:T(8,128)}, bf16[8,128,256]{2,1,0:T(8,128)(2,1)}, bf16[2,256,256]{2,1,0:T(8,128)(2,1)}, bf16[10,256,512]{2,1,0:T(8,128)(2,1)}, bf16[512,1152]{1,0:T(8,128)(2,1)}, /*index=5*/f32[24,512]{1,0:T(8,128)}) custom-call(s32[4]{0:T(128)} %pad_add_fusion.refs_0_, bf16[2,16,256,128]{3,2,1,0:T(8,128)(2,1)} %copy-done.4, ...), custom_call_target="tpu_custom_call" | custom-call | flops 8049999872 | bytes 7000000 | tf_op jit(solution)/shard_map/unpack/pallas_call | solution.py:232
  81.8 13.3 %stem.1 = (f32[128,512]{1,0:T(8,128)}, bf16[20,288,256]{2,1,0:T(8,128)(2,1)}, bf16[10,128,256]{2,1,0:T(8,128)(2,1)}, bf16[10,128,256]{2,1,0:T(8,128)(2,1)}) custom-call(bf16[5,576,128]{2,1,0:T(8,128)(2,1)} %copy.162.refs_0_.refs_1_, bf16[8,128,256]{2,1,0:T(8,128)(2,1)} %get-tuple-element.87.refs_1_.refs_3_, f32[32,256]{1,0:T(8,128)} %get-tuple-element.88.refs_2_.refs_4_, ...), custom_call_target="tpu_custom_call" | custom-call | flops 14949999616 | bytes 13000000 | tf_op jit(solution)/shard_map/stem/pallas_call | solution.py:232
  95.2 8.4 %all-gather.5.cloned.1.call-done = bf16[128,64,512]{2,1,0:T(8,128)(2,1)} async-done(((bf16[4,64,512]{2,1,0:T(8,128)(2,1)}), bf16[128,64,512]{2,1,0:T(8,128)(2,1)}) %all-gather.5.cloned.1.call-update) | async-done | bytes 8388624 | tf_op jit(solution)/shard_map/all_gather | solution.py:1400
  103.6 4.8 %first.1 = (f32[128,512]{1,0:T(8,128)}, f32[4,128,512]{2,1,0:T(8,128)}, bf16[128,512]{1,0:T(8,128)(2,1)}, bf16[128,512]{1,0:T(8,128)(2,1)}) custom-call(bf16[8,4,4,64,512]{4,3,2,1,0:T(8,128)(2,1)} %bitcast.535, f32[128,512]{1,0:T(8,128)} %get-tuple-element.91.refs_1_.refs_6_, f32[24,512]{1,0:T(8,128)} %get-tuple-element.92.refs_2_.refs_3_.refs_6_.refs_7_.refs_15_.refs_9_), custom_call_target="tpu_custom_call" | custom-call | flops 6899999744 | bytes 6000000 | tf_op jit(solution)/shard_map/first/pallas_call | solution.py:232
  110.0 5.8 %position.1 = (bf16[640,512]{1,0:T(8,128)(2,1)}, bf16[128,512]{1,0:T(8,128)(2,1)}, bf16[128,512]{1,0:T(8,128)(2,1)}) custom-call(bf16[8,4,4,64,512]{4,3,2,1,0:T(8,128)(2,1)} %bitcast.536, bf16[640,512]{1,0:T(8,128)(2,1)} %pad_maximum_fusion.3.refs_1_.refs_9_, bf16[128,512]{1,0:T(8,128)(2,1)} %get-tuple-element.93.refs_2_.refs_7_, ...), custom_call_target="tpu_custom_call" | custom-call | flops 5750000128 | bytes 5000000 | tf_op jit(solution)/shard_map/position/pallas_call | solution.py:232
  118.3 10.9 %attention.1 = (f32[128,512]{1,0:T(8,128)}, bf16[4,512,256]{2,1,0:T(8,128)(2,1)}, f32[8,128,512]{2,1,0:T(8,128)}, bf16[128,512]{1,0:T(8,128)(2,1)}, bf16[128,512...) custom-call(bf16[8,4,4,64,512]{4,3,2,1,0:T(8,128)(2,1)} %bitcast.537, ...), custom_call_target="tpu_custom_call" | custom-call | flops 11500000256 | bytes 10000000 | tf_op jit(solution)/shard_map/attention/pallas_call | solution.py:232
  129.2 2.1 collective-permute-start.11
  132.6 2.1 collective-permute-done.12.refs_2_.refs_10_
  135.3 2.3 conv.1
  137.6 6.0 %all-to-all-start = ((f32[32,16,128]{2,1,0:T(8,128)}), f32[32,16,128]{2,1,0:T(8,128)S(1)}, u32[]{:S(2)}, u32[]{:S(2)}) async-start(f32[32,16,128]{2,1,0:T(8,128)} %get-tuple-element.102), calls=%async_computation | async-start | bytes 524288 | tf_op jit(solution)/shard_map/all_to_all | solution.py:209
  145.1 23.3 %all-gather.7.cloned.1.call-done = bf16[64,64,512]{2,1,0:T(8,128)(2,1)} async-done(((bf16[2,64,512]{2,1,0:T(8,128)(2,1)}), bf16[64,64,512]{2,1,0:T(8,128)(2,1)}) %all-gather.7.cloned.1.call-update) | async-done | bytes 4194320 | tf_op jit(solution)/shard_map/all_gather | solution.py:1400
  169.1 12.0 %middle.1 = (bf16[8,2,2,64,512]{4,3,2,1,0:T(8,128)(2,1)}, bf16[8,2,2,64,512]{4,3,2,1,0:T(8,128)(2,1)}, bf16[512,1152]{1,0:T(8,128)(2,1)}, f32[128,512]{1,0:T(8,1...) custom-call(s32[4]{0:T(128)} %pad_add_fusion.refs_0_, ...), custom_call_target="tpu_custom_call" | custom-call | flops 14949999616 | bytes 13000000 | tf_op jit(solution)/shard_map/middle/pallas_call | solution.py:232
  181.5 3.1 all-to-all-start.1
  184.6 2.2 collective-permute-start.13
  188.9 2.3 collective-permute-done.14.refs_4_
  193.4 4.4 %conv_back.1 = (bf16[4,128,256]{2,1,0:T(8,128)(2,1)}, f32[128,512]{1,0:T(8,128)}, f32[11,512]{1,0:T(8,128)}, f32[1,1]{1,0:T(1,128)}) custom-call(bf16[8,4,4,64,512]{4,3,2,1,0:T(8,128)(2,1)} %bitcast.539, f32[128,512]{1,0:T(8,128)} %get-tuple-element.105.refs_1_, f32[128,512]{1,0:T(8,128)} %get-tuple-element.106.refs_2_, f32[16,512]{1,0:T(8,128)} %copy-done.28, ...), custom_call_target="tpu_custom_call" | custom-call | flops 4600000000 | bytes 4000000 | tf_op jit(solution)/shard_map/conv_back/pallas_call | solution.py:232
  197.9 2.0 add_convert_fusion
  199.9 13.3 %back.1 = (bf16[128,512]{1,0:T(8,128)(2,1)}, bf16[4,512,256]{2,1,0:T(8,128)(2,1)}, bf16[640,512]{1,0:T(8,128)(2,1)}, bf16[512,512]{1,0:T(8,128)(2,1)}, f32[128,512]{1,0:T(8,128)}, /*index=5*/f32[2,512]{1,0:T(2,128)}) custom-call(bf16[8,4,4,64,512]{4,3,2,1,0:T(8,128)(2,1)} %bitcast.540, f32[128,512]{1,0:T(8,128)} %get-tuple-element.113.refs_1_.refs_2_, ...), custom_call_target="tpu_custom_call" | custom-call | flops 11500000256 | bytes 10000000 | tf_op jit(solution)/shard_map/back/pallas_call | solution.py:232
  218.2 6.2 %mix_grad.1 = (bf16[2,2,4,128,512]{4,3,2,1,0:T(8,128)(2,1)}, bf16[2,2,4,128,512]{4,3,2,1,0:T(8,128)(2,1)}) custom-call(s32[4]{0:T(128)} %pad_add_fusion.refs_0_, f32[128,512]{1,0:T(8,128)} %get-tuple-element.113.refs_1_.refs_2_, f32[128,512]{1,0:T(8,128)} %get-tuple-element.112.refs_14_.refs_2_, bf16[4,128,256]{2,1,0:T(8,128)(2,1)} %get-tuple-element.122.refs_3_, ...), custom_call_target="tpu_custom_call" | custom-call | flops 8049999872 | bytes 7000000 | tf_op jit(solution)/shard_map/mix_grad/pallas_call | solution.py:232
  225.7 8.1 %last.1 = (bf16[2,2,4,128,512]{4,3,2,1,0:T(8,128)(2,1)}, bf16[2,2,4,128,512]{4,3,2,1,0:T(8,128)(2,1)}, bf16[128,512]{1,0:T(8,128)(2,1)}, f32[4,512]{1,0:T(4,128)}) custom-call(s32[4]{0:T(128)} %pad_add_fusion.refs_0_, bf16[8,4,4,64,512]{4,3,2,1,0:T(8,128)(2,1)} %bitcast.541, f32[128,512]{1,0:T(8,128)} %get-tuple-element.113.refs_1_.refs_2_, ...), custom_call_target="tpu_custom_call" | custom-call | flops 9200000000 | bytes 8000000 | tf_op jit(solution)/shard_map/last/pallas_call | solution.py:232
  238.6 5.5 %pack.1 = (bf16[2,2,4,256,128]{4,3,2,1,0:T(8,128)(2,1)}, bf16[2,2,4,256,128]{4,3,2,1,0:T(8,128)(2,1)}, bf16[2,2,4,256,128]{4,3,2,1,0:T(8,128)(2,1)}, bf16[2,2,4,256,128]{4,3,2,1,0:T(8,128)(2,1)}) custom-call(s32[4]{0:T(128)} %pad_add_fusion.refs_0_, bf16[10,128,256]{2,1,0:T(8,128)(2,1)} %get-tuple-element.135.refs_9_.refs_1_, ...), custom_call_target="tpu_custom_call" | custom-call | flops 5750000128 | bytes 5000000 | tf_op jit(solution)/shard_map/pack/pallas_call | solution.py:232
  247.7 27.6 %stem_back.1 = (f32[2,256,256]{2,1,0:T(8,128)}, f32[18,8,256]{2,1,0:T(8,128)}, f32[16,256]{1,0:T(8,128)}) custom-call(bf16[128,512]{1,0:T(8,128)(2,1)} %get-tuple-element.132.refs_0_.refs_2_, bf16[5,576,128]{2,1,0:T(8,128)(2,1)} %copy.162.refs_0_.refs_1_, bf16[16,23040]{1,0:T(8,128)(2,1)} %reshape.725.refs_2_, ...), custom_call_target="tpu_custom_call" | custom-call | flops 31050000384 | bytes 27000000 | tf_op jit(solution)/shard_map/stem_back/pallas_call | solution.py:232
  277.2 2.0 fusion.9.refs_10_
  280.2 2.1 collective-permute-done.25
  282.3 2.4 fusion.3.refs_7_
  284.7 2.7 collective-permute-start.28
  287.4 2.2 fusion.4.refs_8_
  290.1 2.0 stem_rows.1
  292.2 6.0 %all-to-all-start.2 = ((bf16[32,48,128]{2,1,0:T(8,128)(2,1)}), bf16[32,48,128]{2,1,0:T(8,128)(2,1)S(1)}, u32[]{:S(2)}, u32[]{:S(2)}) async-start(bf16[32,48,128]{2,1,0:T(8,128)(2,1)} %bitcast.527), calls=%async_computation.3 | async-start | bytes 786432 | tf_op jit(solution)/shard_map/all_to_all | solution.py:209
  298.2 9.0 %collective-permute-done.32 = bf16[2,4,256,128]{3,2,1,0:T(8,128)(2,1)} collective-permute-done((bf16[2,4,256,128]{3,2,1,0:T(8,128)(2,1)}, bf16[2,4,256,128]{3,2,1,0:T(8,128)(2,1)}, u32[]{:S(2)}, u32[]{:S(2)}) %collective-permute-start.32) | collective-permute-done | bytes 524320 | tf_op jit(solution)/shard_map/ppermute | solution.py:61
  308.4 3.3 collective-permute-start.33
  311.8 4.7 %collective-permute-done.28 = bf16[4,128,512]{2,1,0:T(8,128)(2,1)} collective-permute-done((bf16[4,128,512]{2,1,0:T(8,128)(2,1)}, bf16[4,128,512]{2,1,0:T(8,128)(2,1)}, u32[]{:S(2)}, u32[]{:S(2)}) %collective-permute-start.28) | collective-permute-done | bytes 524320 | tf_op jit(solution)/shard_map/ppermute | solution.py:61
  316.5 1.6 fusion.23
  319.5 2.6 collective-permute-start.30
  324.8 2.6 collective-permute-done.29
  327.4 4.2 %collective-permute-done.30 = bf16[128,512]{1,0:T(8,128)(2,1)S(1)} collective-permute-done((bf16[128,512]{1,0:T(8,128)(2,1)S(1)}, bf16[128,512]{1,0:T(8,128)(2,1)S(1)}, u32[]{:S(2)}, u32[]{:S(2)}) %collective-permute-start.30) | collective-permute-done | bytes 131104 | tf_op jit(solution)/shard_map/ppermute | solution.py:61
  334.9 3.0 collective-permute-start.21
  356.0 2.8 collective-permute-done.37
  362.6 6.6 %all-to-all-start.3 = ((bf16[32,64,128]{2,1,0:T(8,128)(2,1)}), bf16[32,64,128]{2,1,0:T(8,128)(2,1)S(1)}, u32[]{:S(2)}, u32[]{:S(2)}) async-start(bf16[32,64,128]{2,1,0:T(8,128)(2,1)} %broadcast_in_dim.80), calls=%async_computation.4 | async-start | bytes 1048576 | tf_op jit(solution)/shard_map/all_to_all | solution.py:209
  369.2 15.5 %all-to-all-done.3 = bf16[32,64,128]{2,1,0:T(8,128)(2,1)S(1)} async-done(((bf16[32,64,128]{2,1,0:T(8,128)(2,1)}), bf16[32,64,128]{2,1,0:T(8,128)(2,1)S(1)}, u32[]{:S(2)}, u32[]{:S(2)}) %all-to-all-start.3) | async-done | bytes 524320 | tf_op jit(solution)/shard_map/all_to_all | solution.py:209
  (268 shorter events, 87.7 us)
Async XLA Ops:
  7.2 96.4 %all-gather.5.cloned.1.call-start = ((), (), s32[]{:S(2)}) async-start(), calls=%async_computation.6 | async-start | bytes 8650752 | tf_op jit(solution)/shard_map/all_gather | solution.py:1400
  12.0 11.7 %copy-start.23 = (bf16[1,1024,80]{1,2,0:T(8,128)(2,1)S(1)}, bf16[1,1024,80]{1,2,0:T(8,128)(2,1)}, u32[]{:S(2)}) copy-start(bf16[1,1024,80]{1,2,0:T(8,128)(2,1)} %param.10) | copy-start | bytes 491524
  12.0 156.4 %all-gather.7.cloned.1.call-start = ((), (), s32[]{:S(2)}) async-start(), calls=%async_computation.7 | async-start | bytes 4325376 | tf_op jit(solution)/shard_map/all_gather | solution.py:1400
  16.9 20.2 %collective-permute-start.1 = (bf16[512,128]{1,0:T(8,128)(2,1)S(1)}, bf16[512,128]{1,0:T(8,128)(2,1)S(1)}, u32[]{:S(2)}, u32[]{:S(2)}) collective-permute-start(bf16[512,128]{1,0:T(8,128)(2,1)S(1)} %bitcast.522), channel_id=1, source_target_pairs={{0,24},{4,28},{8,0},{12,4},{16,8},{20,12},{24,16},{28,20},{1,25},{... | collective-permute-start | bytes 393224 | tf_op jit(solution)/shard_map/ppermute | solution.py:61
  22.0 15.9 %collective-permute-start.2 = (bf16[512,128]{1,0:T(8,128)(2,1)S(1)}, bf16[512,128]{1,0:T(8,128)(2,1)S(1)}, u32[]{:S(2)}, u32[]{:S(2)}) collective-permute-start(bf16[512,128]{1,0:T(8,128)(2,1)S(1)} %bitcast.523), channel_id=1, source_target_pairs={{0,16},{4,20},{8,24},{12,28},{16,0},{20,4},{24,8},{28,12},{1,17},{... | collective-permute-start | bytes 393224 | tf_op jit(solution)/shard_map/ppermute | solution.py:61
  22.0 15.9 %collective-permute-start.3 = (bf16[512,128]{1,0:T(8,128)(2,1)S(1)}, bf16[512,128]{1,0:T(8,128)(2,1)S(1)}, u32[]{:S(2)}, u32[]{:S(2)}) collective-permute-start(bf16[512,128]{1,0:T(8,128)(2,1)S(1)} %bitcast.524), channel_id=1, source_target_pairs={{0,8},{4,12},{8,16},{12,20},{16,24},{20,28},{24,0},{28,4},{1,9},{5... | collective-permute-start | bytes 393224 | tf_op jit(solution)/shard_map/ppermute | solution.py:61
  24.1 5.2 %collective-permute-start = (bf16[8,80]{1,0:T(8,128)(2,1)S(1)}, bf16[8,80]{1,0:T(8,128)(2,1)S(1)}, u32[]{:S(2)}, u32[]{:S(2)}) collective-permute-start(bf16[8,80]{1,0:T(8,128)(2,1)S(1)} %slice.788), channel_id=1, source_target_pairs={{0,1},{1,2},{2,3},{4,5},{5,6},{6,7},{8,9},{9,10},{10,11},{12,13},{... | collective-permute-start | bytes 3848 | tf_op jit(solution)/shard_map/ppermute | solution.py:215
  38.0 8.7 %collective-permute-start.4 = (bf16[4,256,128]{2,1,0:T(8,128)(2,1)S(1)}, bf16[4,256,128]{2,1,0:T(8,128)(2,1)S(1)}, u32[]{:S(2)}, u32[]{:S(2)}) collective-permute-start(bf16[4,256,128]{2,1,0:T(8,128)(2,1)S(1)} %get-tuple-element.85), channel_id=1, source_target_pairs={{0,2},{1,3},{2,0},{3,1},{4,6},{5,7},{6,4},{7,5},{8,10},{9,11},{10,... | collective-permute-start | bytes 786440 | tf_op jit(solution)/shard_map/ppermute | solution.py:61
  39.6 8.9 %collective-permute-start.6 = (bf16[4,256,128]{2,1,0:T(8,128)(2,1)S(1)}, bf16[4,256,128]{2,1,0:T(8,128)(2,1)S(1)}, u32[]{:S(2)}, u32[]{:S(2)}) collective-permute-start(bf16[4,256,128]{2,1,0:T(8,128)(2,1)S(1)} %get-tuple-element.86), channel_id=1, source_target_pairs={{0,4},{4,0},{8,12},{12,8},{16,20},{20,16},{24,28},{28,24},{1,5},{5... | collective-permute-start | bytes 786440 | tf_op jit(solution)/shard_map/ppermute | solution.py:61
  46.8 16.9 %collective-permute-start.5 = (bf16[2,4,256,128]{3,2,1,0:T(8,128)(2,1)S(1)}, bf16[2,4,256,128]{3,2,1,0:T(8,128)(2,1)S(1)}, u32[]{:S(2)}, u32[]{:S(2)}) collective-permute-start(bf16[2,4,256,128]{3,2,1,0:T(8,128)(2,1)S(1)} %get-tuple-element.191), channel_id=1, source_target_pairs={{0,4},{4,0},{8,12},{12,8},{16,20},{20,16},{24,28},{28,24},{1,5},{5... | collective-permute-start | bytes 1572872 | tf_op jit(solution)/shard_map/ppermute | solution.py:61
  48.6 18.9 %collective-permute-start.7 = (bf16[2,4,256,128]{3,2,1,0:T(8,128)(2,1)S(1)}, bf16[2,4,256,128]{3,2,1,0:T(8,128)(2,1)S(1)}, u32[]{:S(2)}, u32[]{:S(2)}) collective-permute-start(bf16[2,4,256,128]{3,2,1,0:T(8,128)(2,1)S(1)} %get-tuple-element.193), channel_id=1, source_target_pairs={{0,2},{1,3},{2,0},{3,1},{4,6},{5,7},{6,4},{7,5},{8,10},{9,11},{10,... | collective-permute-start | bytes 1572872 | tf_op jit(solution)/shard_map/ppermute | solution.py:61
  67.7 4.4 %collective-permute-start.8 = (bf16[2,16,256,128]{3,2,1,0:T(8,128)(2,1)S(1)}, bf16[2,16,256,128]{3,2,1,0:T(8,128)(2,1)}, u32[]{:S(2)}, u32[]{:S(2)}) collective-permute-start(bf16[2,16,256,128]{3,2,1,0:T(8,128)(2,1)S(1)} %pad_maximum_fusion.refs_1_), channel_id=1, source_target_pairs={{0,1},{1,0},{2,3},{3,2},{4,5},{5,4},{6,7},{7,6},{8,9},{9,8},{10,11... | collective-permute-start | bytes 6291464 | tf_op jit(solution)/shard_map/ppermute | solution.py:61
  108.5 7.3 %collective-permute-start.9 = (bf16[128,512]{1,0:T(8,128)(2,1)}, bf16[128,512]{1,0:T(8,128)(2,1)S(1)}, u32[]{:S(2)}, u32[]{:S(2)}) collective-permute-start(bf16[128,512]{1,0:T(8,128)(2,1)} %get-tuple-element.93.refs_2_.refs_7_), channel_id=1, source_target_pairs={{0,2},{1,3},{2,0},{3,1},{4,6},{5,7},{6,4},{7,5},{8,10},{9,11},{10,... | collective-permute-start | bytes 393224 | tf_op jit(solution)/shard_map/ppermute | solution.py:61
  115.9 1.6 collective-permute-start.10
  129.2 3.4 collective-permute-start.11
  131.3 3.4 collective-permute-start.12
  137.6 30.8 %all-to-all-start = ((f32[32,16,128]{2,1,0:T(8,128)}), f32[32,16,128]{2,1,0:T(8,128)S(1)}, u32[]{:S(2)}, u32[]{:S(2)}) async-start(f32[32,16,128]{2,1,0:T(8,128)} %get-tuple-element.102), calls=%async_computation | async-start | bytes 524288 | tf_op jit(solution)/shard_map/all_to_all | solution.py:209
  181.1 16.7 %collective-permute-start.15 = (bf16[8,2,2,64,512]{4,3,2,1,0:T(8,128)(2,1)}, bf16[8,2,2,64,512]{4,3,2,1,0:T(8,128)(2,1)S(1)}, u32[]{:S(2)}, u32[]{:S(2)}) collective-permute-start(bf16[8,2,2,64,512]{4,3,2,1,0:T(8,128)(2,1)} %get-tuple-element.117), channel_id=1, source_target_pairs={{0,1},{1,0},{2,3},{3,2},{4,5},{5,4},{6,7},{7,6},{8,9},{9,8},{10,11... | collective-permute-start | bytes 6291464 | tf_op jit(solution)/shard_map/ppermute | solution.py:61
  181.5 11.3 %all-to-all-start.1 = ((f32[32,8,128]{2,1,0:T(8,128)}), f32[32,8,128]{2,1,0:T(8,128)S(1)}, u32[]{:S(2)}, u32[]{:S(2)}) async-start(f32[32,8,128]{2,1,0:T(8,128)} %get-tuple-element.109), calls=%async_computation.1 | async-start | bytes 262144 | tf_op jit(solution)/shard_map/all_to_all | solution.py:209
  184.5 168.5 %reduce-scatter.2.cloned.1.call-start = ((), (), s32[]{:S(2)}) async-start(), calls=%async_computation.5 | async-start | bytes 2228224 | tf_op jit(solution)/shard_map/reduce_scatter | solution.py:198
  184.6 4.3 %collective-permute-start.13 = (f32[16,512]{1,0:T(8,128)}, f32[16,512]{1,0:T(8,128)S(1)}, u32[]{:S(2)}, u32[]{:S(2)}) collective-permute-start(f32[16,512]{1,0:T(8,128)} %get-tuple-element.107), channel_id=1, source_target_pairs={{0,1},{1,2},{2,3},{4,5},{5,6},{6,7},{8,9},{9,10},{10,11},{12,13},{... | collective-permute-start | bytes 98312 | tf_op jit(solution)/shard_map/ppermute | solution.py:215
  186.8 4.4 %collective-permute-start.14 = (f32[16,512]{1,0:T(8,128)}, f32[16,512]{1,0:T(8,128)S(1)}, u32[]{:S(2)}, u32[]{:S(2)}) collective-permute-start(f32[16,512]{1,0:T(8,128)} %get-tuple-element.108), channel_id=1, source_target_pairs={{1,0},{2,1},{3,2},{5,4},{6,5},{7,6},{9,8},{10,9},{11,10},{13,12},{... | collective-permute-start | bytes 98312 | tf_op jit(solution)/shard_map/ppermute | solution.py:215
  214.2 2.3 collective-permute-start.16
  217.5 7.5 %collective-permute-start.17 = (bf16[1,128,512]{2,1,0:T(8,128)(2,1)S(1)}, bf16[1,128,512]{2,1,0:T(8,128)(2,1)S(1)}, u32[]{:S(2)}, u32[]{:S(2)}) collective-permute-start(bf16[1,128,512]{2,1,0:T(8,128)(2,1)S(1)} %get-tuple-element.207), channel_id=1, source_target_pairs={{0,2},{1,3},{2,0},{3,1},{4,6},{5,7},{6,4},{7,5},{8,10},{9,11},{10,... | collective-permute-start | bytes 393224 | tf_op jit(solution)/shard_map/ppermute | solution.py:61
  224.4 11.1 %collective-permute-start.24 = (bf16[2,2,4,128,512]{4,3,2,1,0:T(8,128)(2,1)}, bf16[2,2,4,128,512]{4,3,2,1,0:T(8,128)(2,1)}, u32[]{:S(2)}, u32[]{:S(2)}) collective-permute-start(bf16[2,2,4,128,512]{4,3,2,1,0:T(8,128)(2,1)} %get-tuple-element.143), channel_id=1, source_target_pairs={{0,1},{1,0},{2,3},{3,2},{4,5},{5,4},{6,7},{7,6},{8,9},{9,8},{10,11... | collective-permute-start | bytes 6291464 | tf_op jit(solution)/shard_map/ppermute | solution.py:61
  233.8 10.8 %collective-permute-start.18 = (bf16[2,2,4,128,512]{4,3,2,1,0:T(8,128)(2,1)}, bf16[2,2,4,128,512]{4,3,2,1,0:T(8,128)(2,1)}, u32[]{:S(2)}, u32[]{:S(2)}) collective-permute-start(bf16[2,2,4,128,512]{4,3,2,1,0:T(8,128)(2,1)} %get-tuple-element.131), channel_id=1, source_target_pairs={{0,1},{1,0},{2,3},{3,2},{4,5},{5,4},{6,7},{7,6},{8,9},{9,8},{10,11... | collective-permute-start | bytes 6291464 | tf_op jit(solution)/shard_map/ppermute | solution.py:61
  237.0 45.3 %collective-permute-start.25 = (bf16[2,4,128,512]{3,2,1,0:T(8,128)(2,1)S(1)}, bf16[2,4,128,512]{3,2,1,0:T(8,128)(2,1)}, u32[]{:S(2)}, u32[]{:S(2)}) collective-permute-start(bf16[2,4,128,512]{3,2,1,0:T(8,128)(2,1)S(1)} %fusion.2.refs_4_), channel_id=1, source_target_pairs={{0,2},{1,3},{2,0},{3,1},{4,6},{5,7},{6,4},{7,5},{8,10},{9,11},{10,... | collective-permute-start | bytes 3145736 | tf_op jit(solution)/shard_map/ppermute | solution.py:61
  244.1 31.3 %collective-permute-start.26 = (bf16[2,2,4,256,128]{4,3,2,1,0:T(8,128)(2,1)}, bf16[2,2,4,256,128]{4,3,2,1,0:T(8,128)(2,1)S(1)}, u32[]{:S(2)}, u32[]{:S(2)}) collective-permute-start(bf16[2,2,4,256,128]{4,3,2,1,0:T(8,128)(2,1)} %get-tuple-element.146), channel_id=1, source_target_pairs={{0,1},{1,0},{2,3},{3,2},{4,5},{5,4},{6,7},{7,6},{8,9},{9,8},{10,11... | collective-permute-start | bytes 3145736 | tf_op jit(solution)/shard_map/ppermute | solution.py:61
  244.2 33.1 %collective-permute-start.27 = (bf16[2,2,4,256,128]{4,3,2,1,0:T(8,128)(2,1)}, bf16[2,2,4,256,128]{4,3,2,1,0:T(8,128)(2,1)}, u32[]{:S(2)}, u32[]{:S(2)}) collective-permute-start(bf16[2,2,4,256,128]{4,3,2,1,0:T(8,128)(2,1)} %get-tuple-element.148), channel_id=1, source_target_pairs={{0,1},{1,0},{2,3},{3,2},{4,5},{5,4},{6,7},{7,6},{8,9},{9,8},{10,11... | collective-permute-start | bytes 3145736 | tf_op jit(solution)/shard_map/ppermute | solution.py:61
  246.2 41.2 %collective-permute-start.19 = (bf16[2,4,128,512]{3,2,1,0:T(8,128)(2,1)S(1)}, bf16[2,4,128,512]{3,2,1,0:T(8,128)(2,1)}, u32[]{:S(2)}, u32[]{:S(2)}) collective-permute-start(bf16[2,4,128,512]{3,2,1,0:T(8,128)(2,1)S(1)} %fusion.1.refs_10_), channel_id=1, source_target_pairs={{0,4},{4,0},{8,12},{12,8},{16,20},{20,16},{24,28},{28,24},{1,5},{5... | collective-permute-start | bytes 3145736 | tf_op jit(solution)/shard_map/ppermute | solution.py:61
  247.7 27.6 %copy-start.10 = (bf16[2,2,4,256,128]{4,3,2,1,0:T(8,128)(2,1)S(1)}, bf16[2,2,4,256,128]{4,3,2,1,0:T(8,128)(2,1)}, u32[]{:S(2)}) copy-start(bf16[2,2,4,256,128]{4,3,2,1,0:T(8,128)(2,1)} %get-tuple-element.145) | copy-start | bytes 3145732
  276.3 30.9 %collective-permute-start.32 = (bf16[2,4,256,128]{3,2,1,0:T(8,128)(2,1)}, bf16[2,4,256,128]{3,2,1,0:T(8,128)(2,1)}, u32[]{:S(2)}, u32[]{:S(2)}) collective-permute-start(bf16[2,4,256,128]{3,2,1,0:T(8,128)(2,1)} %fusion.8.refs_9_), channel_id=1, source_target_pairs={{0,2},{1,3},{2,0},{3,1},{4,6},{5,7},{6,4},{7,5},{8,10},{9,11},{10,... | collective-permute-start | bytes 1572872 | tf_op jit(solution)/shard_map/ppermute | solution.py:61
  279.2 42.9 %collective-permute-start.34 = (bf16[2,4,256,128]{3,2,1,0:T(8,128)(2,1)}, bf16[2,4,256,128]{3,2,1,0:T(8,128)(2,1)}, u32[]{:S(2)}, u32[]{:S(2)}) collective-permute-start(bf16[2,4,256,128]{3,2,1,0:T(8,128)(2,1)} %fusion.9.refs_10_), channel_id=1, source_target_pairs={{0,4},{4,0},{8,12},{12,8},{16,20},{20,16},{24,28},{28,24},{1,5},{5... | collective-permute-start | bytes 1572872 | tf_op jit(solution)/shard_map/ppermute | solution.py:61
  284.7 31.8 %collective-permute-start.28 = (bf16[4,128,512]{2,1,0:T(8,128)(2,1)}, bf16[4,128,512]{2,1,0:T(8,128)(2,1)}, u32[]{:S(2)}, u32[]{:S(2)}) collective-permute-start(bf16[4,128,512]{2,1,0:T(8,128)(2,1)} %fusion.3.refs_7_), channel_id=1, source_target_pairs={{0,4},{4,0},{8,12},{12,8},{16,20},{20,16},{24,28},{28,24},{1,5},{5... | collective-permute-start | bytes 1572872 | tf_op jit(solution)/shard_map/ppermute | solution.py:61
  289.6 43.2 %collective-permute-start.20 = (bf16[4,128,512]{2,1,0:T(8,128)(2,1)}, bf16[4,128,512]{2,1,0:T(8,128)(2,1)S(1)}, u32[]{:S(2)}, u32[]{:S(2)}) collective-permute-start(bf16[4,128,512]{2,1,0:T(8,128)(2,1)} %fusion.4.refs_8_), channel_id=1, source_target_pairs={{0,2},{1,3},{2,0},{3,1},{4,6},{5,7},{6,4},{7,5},{8,10},{9,11},{10,... | collective-permute-start | bytes 1572872 | tf_op jit(solution)/shard_map/ppermute | solution.py:61
  292.2 60.8 %all-to-all-start.2 = ((bf16[32,48,128]{2,1,0:T(8,128)(2,1)}), bf16[32,48,128]{2,1,0:T(8,128)(2,1)S(1)}, u32[]{:S(2)}, u32[]{:S(2)}) async-start(bf16[32,48,128]{2,1,0:T(8,128)(2,1)} %bitcast.527), calls=%async_computation.3 | async-start | bytes 786432 | tf_op jit(solution)/shard_map/all_to_all | solution.py:209
  308.4 31.8 %collective-permute-start.33 = (bf16[4,256,128]{2,1,0:T(8,128)(2,1)S(1)}, bf16[4,256,128]{2,1,0:T(8,128)(2,1)S(1)}, u32[]{:S(2)}, u32[]{:S(2)}) collective-permute-start(bf16[4,256,128]{2,1,0:T(8,128)(2,1)S(1)} %fusion.11), channel_id=1, source_target_pairs={{0,4},{4,0},{8,12},{12,8},{16,20},{20,16},{24,28},{28,24},{1,5},{5... | collective-permute-start | bytes 786440 | tf_op jit(solution)/shard_map/ppermute | solution.py:61
  318.1 9.3 %collective-permute-start.29 = (bf16[128,512]{1,0:T(8,128)(2,1)S(1)}, bf16[128,512]{1,0:T(8,128)(2,1)S(1)}, u32[]{:S(2)}, u32[]{:S(2)}) collective-permute-start(bf16[128,512]{1,0:T(8,128)(2,1)S(1)} %get-tuple-element.178), channel_id=1, source_target_pairs={{0,8},{4,12},{8,16},{12,20},{16,24},{20,28},{24,0},{28,4},{1,9},{5... | collective-permute-start | bytes 393224 | tf_op jit(solution)/shard_map/ppermute | solution.py:61
  319.5 12.1 %collective-permute-start.30 = (bf16[128,512]{1,0:T(8,128)(2,1)S(1)}, bf16[128,512]{1,0:T(8,128)(2,1)S(1)}, u32[]{:S(2)}, u32[]{:S(2)}) collective-permute-start(bf16[128,512]{1,0:T(8,128)(2,1)S(1)} %get-tuple-element.180), channel_id=1, source_target_pairs={{0,16},{4,20},{8,24},{12,28},{16,0},{20,4},{24,8},{28,12},{1,17},{... | collective-permute-start | bytes 393224 | tf_op jit(solution)/shard_map/ppermute | solution.py:61
  322.1 9.5 %collective-permute-start.31 = (bf16[128,512]{1,0:T(8,128)(2,1)S(1)}, bf16[128,512]{1,0:T(8,128)(2,1)S(1)}, u32[]{:S(2)}, u32[]{:S(2)}) collective-permute-start(bf16[128,512]{1,0:T(8,128)(2,1)S(1)} %get-tuple-element.179), channel_id=1, source_target_pairs={{0,24},{4,28},{8,0},{12,4},{16,8},{20,12},{24,16},{28,20},{1,25},{... | collective-permute-start | bytes 393224 | tf_op jit(solution)/shard_map/ppermute | solution.py:61
  327.4 14.1 %collective-permute-start.35 = (bf16[4,256,128]{2,1,0:T(8,128)(2,1)S(1)}, bf16[4,256,128]{2,1,0:T(8,128)(2,1)S(1)}, u32[]{:S(2)}, u32[]{:S(2)}) collective-permute-start(bf16[4,256,128]{2,1,0:T(8,128)(2,1)S(1)} %fusion.10), channel_id=1, source_target_pairs={{0,2},{1,3},{2,0},{3,1},{4,6},{5,7},{6,4},{7,5},{8,10},{9,11},{10,... | collective-permute-start | bytes 786440 | tf_op jit(solution)/shard_map/ppermute | solution.py:61
  334.9 12.5 %collective-permute-start.21 = (bf16[128,512]{1,0:T(8,128)(2,1)S(1)}, bf16[128,512]{1,0:T(8,128)(2,1)S(1)}, u32[]{:S(2)}, u32[]{:S(2)}) collective-permute-start(bf16[128,512]{1,0:T(8,128)(2,1)S(1)} %get-tuple-element.181), channel_id=1, source_target_pairs={{0,8},{4,12},{8,16},{12,20},{16,24},{20,28},{24,0},{28,4},{1,9},{5... | collective-permute-start | bytes 393224 | tf_op jit(solution)/shard_map/ppermute | solution.py:61
  337.8 10.8 %collective-permute-start.22 = (bf16[128,512]{1,0:T(8,128)(2,1)S(1)}, bf16[128,512]{1,0:T(8,128)(2,1)S(1)}, u32[]{:S(2)}, u32[]{:S(2)}) collective-permute-start(bf16[128,512]{1,0:T(8,128)(2,1)S(1)} %get-tuple-element.183), channel_id=1, source_target_pairs={{0,16},{4,20},{8,24},{12,28},{16,0},{20,4},{24,8},{28,12},{1,17},{... | collective-permute-start | bytes 393224 | tf_op jit(solution)/shard_map/ppermute | solution.py:61
  339.4 9.3 %collective-permute-start.23 = (bf16[128,512]{1,0:T(8,128)(2,1)S(1)}, bf16[128,512]{1,0:T(8,128)(2,1)S(1)}, u32[]{:S(2)}, u32[]{:S(2)}) collective-permute-start(bf16[128,512]{1,0:T(8,128)(2,1)S(1)} %get-tuple-element.182), channel_id=1, source_target_pairs={{0,24},{4,28},{8,0},{12,4},{16,8},{20,12},{24,16},{28,20},{1,25},{... | collective-permute-start | bytes 393224 | tf_op jit(solution)/shard_map/ppermute | solution.py:61
  343.5 12.5 %collective-permute-start.36 = (bf16[2,256,128]{2,1,0:T(8,128)(2,1)}, bf16[2,256,128]{2,1,0:T(8,128)(2,1)S(1)}, u32[]{:S(2)}, u32[]{:S(2)}) collective-permute-start(bf16[2,256,128]{2,1,0:T(8,128)(2,1)} %pad_maximum_fusion.13), channel_id=1, source_target_pairs={{0,8},{4,12},{8,16},{12,20},{16,24},{20,28},{24,0},{28,4},{1,9},{5... | collective-permute-start | bytes 393224 | tf_op jit(solution)/shard_map/ppermute | solution.py:61
  345.4 13.4 %collective-permute-start.37 = (bf16[2,256,128]{2,1,0:T(8,128)(2,1)}, bf16[2,256,128]{2,1,0:T(8,128)(2,1)}, u32[]{:S(2)}, u32[]{:S(2)}) collective-permute-start(bf16[2,256,128]{2,1,0:T(8,128)(2,1)} %pad_maximum_fusion.14), channel_id=1, source_target_pairs={{0,16},{4,20},{8,24},{12,28},{16,0},{20,4},{24,8},{28,12},{1,17},{... | collective-permute-start | bytes 393224 | tf_op jit(solution)/shard_map/ppermute | solution.py:61
  347.4 11.4 %collective-permute-start.38 = (bf16[2,256,128]{2,1,0:T(8,128)(2,1)}, bf16[2,256,128]{2,1,0:T(8,128)(2,1)}, u32[]{:S(2)}, u32[]{:S(2)}) collective-permute-start(bf16[2,256,128]{2,1,0:T(8,128)(2,1)} %pad_maximum_fusion.15), channel_id=1, source_target_pairs={{0,24},{4,28},{8,0},{12,4},{16,8},{20,12},{24,16},{28,20},{1,25},{... | collective-permute-start | bytes 393224 | tf_op jit(solution)/shard_map/ppermute | solution.py:61
  362.6 22.1 %all-to-all-start.3 = ((bf16[32,64,128]{2,1,0:T(8,128)(2,1)}), bf16[32,64,128]{2,1,0:T(8,128)(2,1)S(1)}, u32[]{:S(2)}, u32[]{:S(2)}) async-start(bf16[32,64,128]{2,1,0:T(8,128)(2,1)} %broadcast_in_dim.80), calls=%async_computation.4 | async-start | bytes 1048576 | tf_op jit(solution)/shard_map/all_to_all | solution.py:209
  (31 other events, 100.8 us)
Sparse Core Ops, SparseCore 0:
  12.1 91.4 all-gather.4
  107.1 61.2 all-gather.6
  235.6 97.3 reduce-scatter.1
